TPU v7x, 128 devices: a whole 4x4x4 slice. The times are simulated.
128 devices in a mesh: enc: 16 (over x, y), dec: 4 (over z), ret: 2 (over core).
Axes of the slice: x: 4, y: 4, z: 4, core: 2. Of those that a mesh axis runs over, the one named last changes fastest.
Arguments:
- enc_states: bfloat16 [32, 2, 256, 4096], P('enc', 'ret'), may hold values from -22 to 22
- kv_weight: bfloat16 [4096, 64, 128], P(None, 'dec'), may hold values from -1 to 1
- queries: bfloat16 [8, 128, 64, 64], P('ret', None, ('dec', 'enc')), may hold values from -47 to 47
- out_grad: bfloat16 [8, 128, 64, 64], P('ret', None, ('dec', 'enc')), may hold values from -6 to 6
- passage_order: int32 [2, 32], P('ret'), may hold values from 0 to 31, each once within a row
- passage_blocks: int32 [2, 32], P('ret'), may hold values from 1 to 2
- ret_tokens: bfloat16 [32, 2, 256, 768], P('enc', 'ret'), may hold values from -6 to 6
- ret_weight: bfloat16 [768, 768], replicated, may hold values from -0.21875 to 0.21875
- question_emb: float32 [8, 768], P('ret'), may hold values from -7 to 7
Outputs:
- kv_grad: bfloat16 [32, 2, 256, 64, 128], P('enc', 'ret', None, 'dec')
- kv_weight_grad: bfloat16 [4096, 64, 128], P(('enc', 'ret'), 'dec')
- ret_weight_grad: bfloat16 [768, 768], replicated
Inputs may be any that keep to these rules, and one draw needn't show every extreme that they name: `passage_order`: each row lists every passage of its group once; slots i * 8 to (i + 1) * 8 - 1 belong to question i of the group.
All inputs are finite; a program needn't handle non-finite values.
Results may differ from a plain program's by a relative error of at most 0.025.
Values may be sent and summed in bfloat16 or wider, within the bound.
No kernel may reach another device: no remote copies, remote signals or barrier semaphores. Data moves between devices by JAX's collectives and lax.ppermute only.
A program may use at most 128 MiB of HBM per device.

v0:
```python
import math

import jax
import jax.numpy as jnp
from jax import lax
from jax.sharding import PartitionSpec as P

HEADS = 64
BLK = 128
PASS = 8


def gelu_grad(pre_act, upstream):
    return jax.vjp(jax.nn.gelu, pre_act)[1](upstream)[0]


def on_device(
    enc_states,
    kv_weight,
    queries,
    out_grad,
    passage_order,
    passage_blocks,
    ret_tokens,
    ret_weight,
    question_emb,
):
    pass_dev = enc_states.shape[0]
    slot_len = enc_states.shape[2]
    width = enc_states.shape[3]
    heads_dec = kv_weight.shape[1]
    pair_width = kv_weight.shape[2]
    head_dim = pair_width // 2
    enc_rank = lax.axis_index("enc")
    dec_rank = lax.axis_index("dec")
    order_row = passage_order[0]
    blocks_row = passage_blocks[0]
    group_pass = order_row.shape[0]
    question_count = queries.shape[0]
    query_len = queries.shape[1]
    highest = lax.Precision.HIGHEST
    own_blocks = lax.dynamic_slice_in_dim(blocks_row, enc_rank * pass_dev, pass_dev)
    tok_rows = enc_states.reshape(pass_dev * slot_len, width)
    weight_flat = kv_weight.reshape(width, heads_dec * pair_width)
    key_value = jnp.dot(tok_rows, weight_flat, preferred_element_type=jnp.float32)
    key_value = key_value.reshape(pass_dev * slot_len, heads_dec, pair_width)
    gathered = lax.all_to_all(key_value, "enc", split_axis=1, concat_axis=0, tiled=True)
    heads_here = gathered.shape[1]
    gathered = gathered.reshape(group_pass, slot_len, heads_here, pair_width)
    chosen = order_row.reshape(question_count, PASS)
    key_count = PASS * slot_len
    selected = gathered[chosen].reshape(question_count, key_count, heads_here, pair_width)
    keys = selected[..., :head_dim]
    values = selected[..., head_dim:]
    positions = jnp.arange(slot_len, dtype=jnp.int32)
    live = (positions[None, None, :] < BLK * blocks_row[chosen][:, :, None]).reshape(
        question_count, key_count
    )
    scale = 1.0 / math.sqrt(head_dim)
    query_wide = queries.astype(jnp.float32)
    grad_wide = out_grad.astype(jnp.float32)
    scores = jnp.einsum("qlhc,qkhc->qhlk", query_wide, keys, precision=highest) * scale
    masked = jnp.where(live[:, None, None, :], scores, -1e30)
    top = jnp.max(masked, axis=-1, keepdims=True)
    expo = jnp.where(live[:, None, None, :], jnp.exp(masked - top), 0.0)
    probs = expo / jnp.sum(expo, axis=-1, keepdims=True)
    probs_low = probs.astype(jnp.bfloat16)
    attended = jnp.einsum(
        "qhlk,qkhc->qlhc", probs_low.astype(jnp.float32), values, precision=highest
    )
    value_grad = jnp.einsum(
        "qhlk,qlhc->qkhc", probs_low, out_grad, preferred_element_type=jnp.float32
    )
    prob_grad = jnp.einsum("qlhc,qkhc->qhlk", grad_wide, values, precision=highest)
    row_dot = jnp.einsum("qlhc,qlhc->qhl", grad_wide, attended)
    score_grad = (probs * (prob_grad - row_dot[..., None]) * scale).astype(jnp.bfloat16)
    key_grad = jnp.einsum(
        "qhlk,qlhc->qkhc", score_grad, queries, preferred_element_type=jnp.float32
    )
    pair_grad = jnp.concatenate([key_grad, value_grad], axis=-1).astype(jnp.bfloat16)
    pair_grad = pair_grad.reshape(question_count * PASS, slot_len, heads_here, pair_width)
    placed = (
        jnp.zeros((group_pass, slot_len, heads_here, pair_width), jnp.bfloat16)
        .at[order_row]
        .set(pair_grad)
    )
    returned = lax.all_to_all(
        placed.reshape(group_pass * slot_len, heads_here, pair_width),
        "enc",
        split_axis=0,
        concat_axis=1,
        tiled=True,
    )
    kv_grad = returned.reshape(pass_dev, 1, slot_len, heads_dec, pair_width)
    mass_part = jnp.sum(probs, axis=(1, 2)).reshape(question_count, PASS, slot_len).sum(axis=-1) / (
        HEADS * query_len
    )
    ret_rows = ret_tokens.reshape(pass_dev * slot_len, ret_tokens.shape[3])
    ret_width = ret_rows.shape[1]
    pre_act = jnp.dot(ret_rows, ret_weight, preferred_element_type=jnp.float32).reshape(
        pass_dev, slot_len, ret_width
    )
    hidden = jax.nn.gelu(pre_act)
    own_live = positions[None, :] < BLK * own_blocks[:, None]
    own_length = (BLK * own_blocks).astype(jnp.float32)
    embed_own = jnp.sum(jnp.where(own_live[..., None], hidden, 0.0), axis=1) / own_length[:, None]
    owner_map = (
        order_row[:, None] == enc_rank * pass_dev + jnp.arange(pass_dev, dtype=jnp.int32)[None, :]
    ).astype(jnp.float32)
    slot_embed = jnp.dot(owner_map, embed_own, precision=highest)
    emb_rep = jnp.repeat(question_emb, PASS, axis=0)
    score_part = jnp.sum(emb_rep * slot_embed, axis=-1) * (dec_rank == 0).astype(jnp.float32)
    passage_mass, ret_scores = lax.psum(
        (mass_part, score_part.reshape(question_count, PASS)), ("enc", "dec")
    )
    top_score = jnp.max(ret_scores, axis=-1, keepdims=True)
    expo_score = jnp.exp(ret_scores - top_score)
    score_gap = expo_score / jnp.sum(expo_score, axis=-1, keepdims=True) - passage_mass
    gap_rows = score_gap.reshape(-1, 1) * emb_rep
    embed_grad = jnp.dot(jnp.transpose(owner_map), gap_rows, precision=highest)
    hidden_grad = jnp.where(
        own_live[..., None], (embed_grad / own_length[:, None])[:, None, :], 0.0
    )
    pre_grad = gelu_grad(pre_act, hidden_grad).astype(jnp.bfloat16)
    ret_part_grad = lax.dot_general(
        ret_rows,
        pre_grad.reshape(-1, ret_width),
        (((0,), (0,)), ((), ())),
        preferred_element_type=jnp.float32,
    )
    ret_weight_grad = lax.psum(ret_part_grad.astype(jnp.bfloat16), ("enc", "ret"))
    grad_flat = returned.reshape(pass_dev * slot_len, heads_dec * pair_width)
    term = lax.dot_general(
        tok_rows, grad_flat, (((0,), (0,)), ((), ())), preferred_element_type=jnp.float32
    )
    weight_total = lax.psum_scatter(
        term.reshape(
            width // (lax.axis_size("enc") * lax.axis_size("ret")) * lax.axis_size(("enc", "ret")),
            heads_dec,
            pair_width,
        ).astype(jnp.bfloat16),
        ("enc", "ret"),
        scatter_dimension=0,
        tiled=True,
    )
    return (kv_grad, weight_total, ret_weight_grad)


def solution(mesh):
    return jax.shard_map(
        on_device,
        mesh=mesh,
        in_specs=(
            P("enc", "ret", None, None),
            P(None, "dec", None),
            P("ret", None, ("dec", "enc"), None),
            P("ret", None, ("dec", "enc"), None),
            P("ret", None),
            P("ret", None),
            P("enc", "ret", None, None),
            P(),
            P("ret", None),
        ),
        out_specs=(P("enc", "ret", None, "dec", None), P(("enc", "ret"), "dec", None), P()),
        check_vma=False,
    )
```

profile of v0, /device:TPU:0, one launch (start us, length us, event | category | flops | bytes accessed | tf_op | source)
XLA Modules:
  0.0 607.5 jit_solution(14512993675005288566)
XLA Ops:
  7.2 17.3 %copy.86 = bf16[512,8,16,128]{3,1,2,0:T(8,128)(2,1)} copy(bf16[512,8,16,128]{3,2,1,0:T(8,128)(2,1)} %bitcast.145) | data formatting | bytes 33554432
  24.5 20.7 %copy.56 = bf16[2048,4096]{1,0:T(8,128)(2,1)} copy(bf16[2048,4096]{0,1:T(8,128)(2,1)} %bitcast.138) | data formatting | bytes 33554432 | tf_op jit(solution)/shard_map/dot_general | solution.py:45
  45.3 14.2 %fusion.55 = f32[512,16,128]{2,0,1:T(8,128)} fusion(bf16[512,4096,1]{1,0,2:T(8,128)(2,1)} %bitcast.153, bf16[16,128,4096]{2,1,0:T(8,128)(2,1)} %bitcast.146), kind=kOutput, calls=%fused_computation.92 | convolution fusion | flops 8589934592 | bytes 25165824 | tf_op jit(solution)/shard_map/dot_general | solution.py:45
  59.4 7.3 %all-to-all-start = ((f32[512,16,128]{2,0,1:T(8,128)}), f32[512,16,128]{2,0,1:T(8,128)}, u32[]{:S(2)}, u32[]{:S(2)}) async-start(f32[512,16,128]{2,0,1:T(8,128)} %fusion.55), calls=%async_computation | async-start | bytes 8388608 | tf_op jit(solution)/shard_map/all_to_all | solution.py:47
  67.0 2.2 select_reduce_fusion
  71.9 58.0 %all-to-all-done = f32[512,16,128]{2,0,1:T(8,128)} async-done(((f32[512,16,128]{2,0,1:T(8,128)}), f32[512,16,128]{2,0,1:T(8,128)}, u32[]{:S(2)}, u32[]{:S(2)}) %all-to-all-start) | async-done | bytes 4194336 | tf_op jit(solution)/shard_map/all_to_all | solution.py:47
  129.9 5.0 gather_fusion.1
  134.9 3.8 fusion.1
  138.8 3.6 fusion.54
  142.4 4.9 fusion.29
  148.2 3.3 fusion.3
  153.1 1.5 concatenate.17
  155.5 1.5 concatenate.18
  157.0 1.7 maximum_bitcast_fusion
  158.8 3.0 copy.64
  162.3 4.0 scatter_fusion
  166.8 2.9 reduce.12
  169.7 4.0 reshape.337
  173.6 10.1 %all-to-all-start.1 = ((bf16[16,2,32768]{2,1,0:T(2,128)(2,1)}), bf16[16,2,32768]{2,1,0:T(2,128)(2,1)S(1)}, u32[]{:S(2)}, u32[]{:S(2)}) async-start(bf16[16,2,32768]{2,1,0:T(2,128)(2,1)} %reshape.337), calls=%async_computation.1 | async-start | bytes 4194304 | tf_op jit(solution)/shard_map/all_to_all | solution.py:87
  183.7 3.4 fusion.52
  187.2 189.0 %all-reduce = (f32[4,8]{1,0:T(4,128)S(1)}, f32[4,8]{1,0:T(4,128)S(1)}) all-reduce(f32[4,8]{1,0:T(4,128)S(1)} %broadcast_multiply_fusion, f32[4,8]{1,0:T(4,128)S(1)} %mul.128), channel_id=1, replica_groups=mesh['enc'=16,'dec'=4,'ret'=2] {'enc','dec'}, use_global_device_ids=true, to_apply=%region_11.12 | all-reduce | flops 64 | bytes 512 | tf_op jit(solution)/shard_map/psum | solution.py:113
  377.0 2.6 fusion.20
  379.5 3.0 fusion.24
  382.6 7.0 %reshape.338 = bf16[8192,1,128]{2,1,0:T(2,128)(2,1)} reshape(bf16[16,2,32768]{2,1,0:T(2,128)(2,1)S(1)} %all-to-all-done.1) | data formatting | bytes 4194304
  389.6 2.5 copy.77
  392.1 2.6 copy.66
  394.7 14.8 %convolution_convert_fusion = bf16[2048,4096]{1,0:T(8,128)(2,1)} fusion(bf16[512,2048]{0,1:T(8,128)(2,1)} %bitcast.148, bf16[512,4096]{1,0:T(8,128)(2,1)} %bitcast.154), kind=kOutput, calls=%fused_computation.5 | convolution fusion | flops 8598323200 | bytes 23068672 | tf_op jit(solution)/shard_map/dot_general | solution.py:133
  409.5 22.3 %copy.67 = bf16[4096,16,128]{2,1,0:T(8,128)(2,1)} copy(bf16[4096,16,128]{0,2,1:T(8,128)(2,1)} %bitcast.147) | data formatting | bytes 33554432 | tf_op jit(solution)/shard_map/convert_element_type | solution.py:141
  431.8 49.6 %all-reduce.3.cloned.1.call-done = bf16[768,768]{0,1:T(8,128)(2,1)} async-done(((bf16[768,768]{0,1:T(8,128)(2,1)}), bf16[768,768]{0,1:T(8,128)(2,1)}) %all-reduce.3.cloned.1.call-update) | async-done | bytes 1179664 | tf_op jit(solution)/shard_map/psum | solution.py:131
  481.4 2.4 copy.69
  483.7 2.7 copy.68
  486.4 114.3 %reduce-scatter.2.cloned.1.call-done = bf16[128,16,128]{2,1,0:T(8,128)(2,1)} async-done(((bf16[4096,16,128]{2,1,0:T(8,128)(2,1)}), bf16[128,16,128]{2,1,0:T(8,128)(2,1)}) %reduce-scatter.2.cloned.1.call-update) | async-done | bytes 524304 | tf_op jit(solution)/shard_map/reduce_scatter | solution.py:136
  (59 shorter events, 8.2 us)
Async XLA Ops:
  7.2 59.8 %copy-start = (bf16[768,768]{1,0:T(8,128)(2,1)S(1)}, bf16[768,768]{1,0:T(8,128)(2,1)}, u32[]{:S(2)}) copy-start(bf16[768,768]{1,0:T(8,128)(2,1)} %param.16) | copy-start | bytes 3538948
  59.4 7.3 %copy-start.2 = (s32[1,32]{1,0:T(1,128)S(1)}, s32[1,32]{1,0:T(1,128)}, u32[]{:S(2)}) copy-start(s32[1,32]{1,0:T(1,128)} %param.14) | copy-start | bytes 388
  59.4 7.5 %copy-start.6 = (bf16[2,1,256,768]{3,2,1,0:T(8,128)(2,1)S(1)}, bf16[2,1,256,768]{3,2,1,0:T(8,128)(2,1)}, u32[]{:S(2)}) copy-start(bf16[2,1,256,768]{3,2,1,0:T(8,128)(2,1)} %param.15) | copy-start | bytes 2359300
  59.4 70.5 %all-to-all-start = ((f32[512,16,128]{2,0,1:T(8,128)}), f32[512,16,128]{2,0,1:T(8,128)}, u32[]{:S(2)}, u32[]{:S(2)}) async-start(f32[512,16,128]{2,0,1:T(8,128)} %fusion.55), calls=%async_computation | async-start | bytes 8388608 | tf_op jit(solution)/shard_map/all_to_all | solution.py:47
  66.9 2.2 copy-start.8
  66.9 2.2 copy-start.9
  129.9 5.0 copy-start.5
  138.7 3.6 copy-start.3
  138.8 3.6 copy-start.7
  142.4 5.8 copy-start.4
  173.6 208.9 %all-to-all-start.1 = ((bf16[16,2,32768]{2,1,0:T(2,128)(2,1)}), bf16[16,2,32768]{2,1,0:T(2,128)(2,1)S(1)}, u32[]{:S(2)}, u32[]{:S(2)}) async-start(bf16[16,2,32768]{2,1,0:T(2,128)(2,1)} %reshape.337), calls=%async_computation.1 | async-start | bytes 4194304 | tf_op jit(solution)/shard_map/all_to_all | solution.py:87
  183.7 297.7 %all-reduce.3.cloned.1.call-start = ((), (), s32[]{:S(2)}) async-start(), calls=%async_computation.4 | async-start | bytes 2359296 | tf_op jit(solution)/shard_map/psum | solution.py:131
  382.5 218.2 %reduce-scatter.2.cloned.1.call-start = ((), (), s32[]{:S(2)}) async-start(), calls=%async_computation.3 | async-start | bytes 17301504 | tf_op jit(solution)/shard_map/reduce_scatter | solution.py:136
  483.7 116.9 %copy-start.1 = (bf16[768,768]{1,0:T(8,128)(2,1)S(1)}, bf16[768,768]{1,0:T(8,128)(2,1)}, u32[]{:S(2)}) copy-start(bf16[768,768]{1,0:T(8,128)(2,1)} %param.16) | copy-start | bytes 3538948
Sparse Core Ops, SparseCore 0:
  382.6 98.7 all-reduce.2
  485.8 114.7 reduce-scatter.1
where the time goes:
time: 609 us; the launch traced here: 608 us
  waiting for transfers between devices  222 us (36%)
  blocking collectives  189 us (31%)
  local copies, waits for them, and re-layouts  101 us (17%)
  matrix products  48.5 us (8%)
  starting transfers between devices  17.4 us (3%)
  other arithmetic  15.5 us (3%)
  between operations  14.3 us (2%)
    psum x1, blocking collectives, on_device(): lax.psum((mass_part, score_part.reshape(question_count, PASS)), ('enc', '...  189 us
    reduce_scatter x1, waiting for transfers between devices, on_device(): lax.psum_scatter(term.reshape(width // (lax.axis_size('enc') * lax.axis_s...  114 us
    all_to_all x1, waiting for transfers between devices, on_device(): lax.all_to_all(key_value, 'enc', split_axis=1, concat_axis=0, tiled=True)  58 us
    psum x1, waiting for transfers between devices, on_device(): lax.psum(ret_part_grad.astype(jnp.bfloat16), ('enc', 'ret'))  49.6 us
    unnamed x31, local copies, waits for them, and re-layouts  36.5 us
    convert_element_type x1, local copies, waits for them, and re-layouts, on_device(): weight_total = lax.psum_scatter(term.reshape(width // (lax.axis_size('enc...  22.3 us
    dot_general x1, local copies, waits for them, and re-layouts, on_device(): jnp.dot(tok_rows, weight_flat, preferred_element_type=jnp.float32)  20.7 us
    dot_general x1, matrix products, on_device(): lax.dot_general(tok_rows, grad_flat, (((0,), (0,)), ((), ())), preferred_...  14.8 us
  transfers between devices with their start and end apart: 4, of which 3 were waited for; matrix products, arithmetic and copies ran while one was open for 11% of the time, Pallas kernels for 0%

commit v1 on v0

v1 whole, which is shorter than its diff:
```python
import functools

import jax
import jax.numpy as jnp
from jax import lax
from jax.experimental import pallas as pl
from jax.experimental.pallas import tpu as pltpu
from jax.sharding import PartitionSpec as P

BLK = 128
PASS = 8
N_ENC = 16
SIDE = 4
N_DEC = 4
LQ = 128
HD = 64
SLOT = 256
F32 = jnp.float32
BF16 = jnp.bfloat16
VMEM = 60 << 20


def gelu_grad(pre_act, upstream):
    return jax.vjp(jax.nn.gelu, pre_act)[1](upstream)[0]


def project_kernel(x_ref, w_ref, o_ref):
    @pl.when(pl.program_id(0) == 0)
    def _():
        o_ref[...] = jnp.zeros_like(o_ref)

    rows = x_ref[...]
    by_head = jnp.swapaxes(w_ref[...], 0, 1)
    for pair in range(by_head.shape[0] // 2):
        both = jnp.concatenate([by_head[2 * pair], by_head[2 * pair + 1]], axis=1)
        part = jnp.dot(rows, both, preferred_element_type=F32)
        o_ref[2 * pair] += part[:, :128]
        o_ref[2 * pair + 1] += part[:, 128:]


def project(tok_rows, kv_weight, depth=512):
    tokens, width = tok_rows.shape
    heads, pair_width = kv_weight.shape[1:]
    return pl.pallas_call(
        project_kernel,
        grid=(width // depth,),
        out_shape=jax.ShapeDtypeStruct((heads, tokens, pair_width), F32),
        in_specs=[
            pl.BlockSpec((tokens, depth), lambda i: (0, i)),
            pl.BlockSpec((depth, heads, pair_width), lambda i: (i, 0, 0)),
        ],
        out_specs=pl.BlockSpec((heads, tokens, pair_width), lambda i: (0, 0, 0)),
        compiler_params=pltpu.CompilerParams(vmem_limit_bytes=VMEM),
        cost_estimate=pl.CostEstimate(
            flops=2 * tokens * width * heads * pair_width,
            bytes_accessed=24 << 20,
            transcendentals=0,
        ),
        name="project",
    )(tok_rows, kv_weight)


def turn_kernel(rank_ref, x_ref, mine_ref, send_ref):
    rank = rank_ref[0]
    mine_ref[0] = x_ref[:, pl.ds(pl.multiple_of(rank * 128, 128), 128)].T
    send_ref[0] = x_ref[:, pl.ds(pl.multiple_of((1 - rank) * 128, 128), 128)].T


def turn(ret_rank, tok_rows):
    tokens, width = tok_rows.shape
    half = jax.ShapeDtypeStruct((N_ENC, 128, tokens), BF16)
    return pl.pallas_call(
        turn_kernel,
        grid_spec=pltpu.PrefetchScalarGridSpec(
            num_scalar_prefetch=1,
            grid=(N_ENC,),
            in_specs=[pl.BlockSpec((tokens, 256), lambda i, r: (0, i))],
            out_specs=[pl.BlockSpec((1, 128, tokens), lambda i, r: (i, 0, 0))] * 2,
        ),
        out_shape=[half, half],
        compiler_params=pltpu.CompilerParams(vmem_limit_bytes=VMEM),
        cost_estimate=pl.CostEstimate(flops=0, bytes_accessed=8 << 20, transcendentals=0),
        name="turn",
    )(ret_rank.reshape(1), tok_rows)


def local_scores(kv_ref, qd_ref, head, passage, question, blocks):
    pair = kv_ref[head, passage * SLOT : (passage + 1) * SLOT, :]
    high = pair.astype(BF16)
    low = (pair - high.astype(F32)).astype(BF16)
    rows = qd_ref[head, pl.ds(pl.multiple_of(question * LQ, LQ), LQ), :]
    lane = lax.broadcasted_iota(jnp.int32, rows.shape, 1)
    zero = jnp.zeros_like(rows)
    stacked = jnp.concatenate(
        [jnp.where(lane < HD, rows, zero), jnp.where(lane < HD, zero, rows)], axis=0
    )
    both = lax.dot_general(
        jnp.concatenate([high, low], axis=1),
        jnp.concatenate([stacked, stacked], axis=1),
        (((1,), (1,)), ((), ())),
        preferred_element_type=F32,
    )
    scores = both[:, :LQ]
    place = lax.broadcasted_iota(jnp.int32, scores.shape, 0)
    return jnp.where(place < BLK * blocks, scores, -1e30), both[:, LQ:], stacked


def stats_kernel(heads, question_ref, blocks_ref, kv_ref, qd_ref, score_ref, o_ref):
    step = pl.program_id(0)
    per_step = kv_ref.shape[0]

    @pl.when(step == 0)
    def _():
        o_ref[4 * heads :, :] = score_ref[...]

    for passage in range(2):
        tops, dots = [], []
        for head in range(per_step):
            scores, prob_grad, _ = local_scores(
                kv_ref, qd_ref, head, passage, question_ref[passage], blocks_ref[passage]
            )
            top = jnp.max(scores, axis=0, keepdims=True)
            expo = jnp.exp(scores - top)
            total = jnp.sum(expo, axis=0, keepdims=True)
            tops.append(top + jnp.log(total))
            dots.append(jnp.sum(expo * prob_grad, axis=0, keepdims=True) / total)
        place = passage * heads + step * per_step
        o_ref[pl.ds(pl.multiple_of(place, 8), per_step), :] = jnp.concatenate(tops, axis=0)
        o_ref[pl.ds(pl.multiple_of(2 * heads + place, 8), per_step), :] = jnp.concatenate(
            dots, axis=0
        )


def local_stats(own_question, own_blocks, key_value, gathered, score_rows):
    heads, tokens, pair_width = key_value.shape
    per_step = 8
    rows = 4 * heads + 8
    return pl.pallas_call(
        functools.partial(stats_kernel, heads),
        grid_spec=pltpu.PrefetchScalarGridSpec(
            num_scalar_prefetch=2,
            grid=(heads // per_step,),
            in_specs=[
                pl.BlockSpec((per_step, tokens, pair_width), lambda i, *_: (i, 0, 0)),
                pl.BlockSpec((per_step,) + gathered.shape[1:], lambda i, *_: (i, 0, 0)),
                pl.BlockSpec((8, 128), lambda i, *_: (0, 0)),
            ],
            out_specs=pl.BlockSpec((rows, 128), lambda i, *_: (0, 0)),
        ),
        out_shape=jax.ShapeDtypeStruct((rows, 128), F32),
        compiler_params=pltpu.CompilerParams(vmem_limit_bytes=VMEM),
        cost_estimate=pl.CostEstimate(
            flops=2 << 30, bytes_accessed=6 << 20, transcendentals=1 << 20
        ),
        name="local_stats",
    )(own_question, own_blocks, key_value, gathered, score_rows)


def back_kernel(
    heads,
    question_ref,
    blocks_ref,
    own_ref,
    order_ref,
    kv_ref,
    qd_ref,
    stats_ref,
    grad_ref,
    flat_ref,
    aux_ref,
    norm_ref,
):
    step = pl.program_id(0)
    per_step = kv_ref.shape[0]

    @pl.when(step == 0)
    def _():
        aux = []
        shares = []
        for passage in range(2):
            tops, dots, marks = [], [], []
            for slot in range(PASS):
                place = order_ref[question_ref[passage] * PASS + slot]
                owner = place // 2
                at = place - 2 * owner
                tops.append(
                    stats_ref[owner, pl.ds(pl.multiple_of(at * heads, heads), heads), :]
                )
                dots.append(
                    stats_ref[
                        owner,
                        pl.ds(pl.multiple_of((2 + at) * heads, heads), heads),
                        :,
                    ]
                )
                pair = stats_ref[owner, 4 * heads : 4 * heads + 8, :]
                marks.append(jnp.where(at == 0, pair[0:1], pair[1:2]))
            top = functools.reduce(jnp.maximum, tops)
            total = sum(jnp.exp(t - top) for t in tops)
            norm = top + jnp.log(total)
            norm_ref[passage] = norm
            norm_ref[2 + passage] = sum(jnp.exp(t - norm) * d for t, d in zip(tops, dots))
            own = stats_ref[own_ref[0], passage * heads : (passage + 1) * heads, :]
            mass = jnp.sum(jnp.exp(own - norm), axis=0, keepdims=True)
            aux.append(jnp.broadcast_to(jnp.sum(mass, axis=1, keepdims=True), (1, 128)))
            best = functools.reduce(jnp.maximum, marks)
            mark = stats_ref[own_ref[0], 4 * heads : 4 * heads + 8, :][passage : passage + 1]
            shares.append(jnp.exp(mark - best) / sum(jnp.exp(m - best) for m in marks))
        aux_ref[...] = jnp.concatenate(aux + shares + [jnp.zeros((4, 128), F32)], axis=0)

    for passage in range(2):
        norms = norm_ref[passage, pl.ds(pl.multiple_of(step * per_step, 8), per_step), :]
        dots = norm_ref[2 + passage, pl.ds(pl.multiple_of(step * per_step, 8), per_step), :]
        grads = []
        for head in range(per_step):
            scores, prob_grad, stacked = local_scores(
                kv_ref, qd_ref, head, passage, question_ref[passage], blocks_ref[passage]
            )
            probs = jnp.exp(scores - norms[head : head + 1])
            score_grad = probs * (prob_grad - dots[head : head + 1])
            left = jnp.concatenate([score_grad, probs], axis=1).astype(BF16)
            grad = jnp.dot(left, stacked, preferred_element_type=F32).astype(BF16)
            flat_ref[
                passage * SLOT : (passage + 1) * SLOT, head * 128 : (head + 1) * 128
            ] = grad
            grads.append(grad)
        grad_ref[passage * SLOT : (passage + 1) * SLOT] = jnp.swapaxes(
            jnp.stack(grads, axis=0), 0, 1
        )


def backward(own_question, own_blocks, enc_rank, order_row, key_value, gathered, stats):
    heads, tokens, pair_width = key_value.shape
    per_step = 8
    return pl.pallas_call(
        functools.partial(back_kernel, heads),
        grid_spec=pltpu.PrefetchScalarGridSpec(
            num_scalar_prefetch=4,
            grid=(heads // per_step,),
            in_specs=[
                pl.BlockSpec((per_step, tokens, pair_width), lambda i, *_: (i, 0, 0)),
                pl.BlockSpec((per_step,) + gathered.shape[1:], lambda i, *_: (i, 0, 0)),
                pl.BlockSpec(stats.shape, lambda i, *_: (0, 0, 0)),
            ],
            out_specs=[
                pl.BlockSpec((tokens, per_step, pair_width), lambda i, *_: (0, i, 0)),
                pl.BlockSpec((tokens, per_step * pair_width), lambda i, *_: (0, i)),
                pl.BlockSpec((8, 128), lambda i, *_: (0, 0)),
            ],
            scratch_shapes=[pltpu.VMEM((4, heads, 128), F32)],
        ),
        out_shape=[
            jax.ShapeDtypeStruct((tokens, heads, pair_width), BF16),
            jax.ShapeDtypeStruct((tokens, heads * pair_width), BF16),
            jax.ShapeDtypeStruct((8, 128), F32),
        ],
        compiler_params=pltpu.CompilerParams(vmem_limit_bytes=VMEM),
        cost_estimate=pl.CostEstimate(
            flops=3 << 30, bytes_accessed=10 << 20, transcendentals=1 << 20
        ),
        name="backward",
    )(own_question, own_blocks, enc_rank.reshape(1), order_row, key_value, gathered, stats)


def weight_kernel(which_ref, mine_ref, other_ref, own_ref, far_ref, o_ref):
    rows = SIDE * 128
    depth = mine_ref.shape[-1]
    near = mine_ref[...].reshape(rows, depth)
    far = other_ref[...].reshape(rows, depth)
    columns = own_ref.shape[1] // 2
    for half in range(2):
        at = slice(half * columns, (half + 1) * columns)
        total = jnp.dot(near, own_ref[:, at], preferred_element_type=F32)
        total += jnp.dot(far, far_ref[:, at], preferred_element_type=F32)
        o_ref[0, half] = total.astype(BF16)


def weight_chunks(which, part, mine, other, grad_own, grad_far):
    tokens = mine.shape[-1]
    columns = grad_own.shape[1] // 2
    count = which.shape[0]
    if part == 0:
        turned = pl.BlockSpec((1, SIDE, 128, tokens), lambda i, w: (w[i], 0, 0, 0))
    else:
        turned = pl.BlockSpec((SIDE, 1, 128, tokens), lambda i, w: (0, w[i], 0, 0))
    grads = pl.BlockSpec((tokens, columns), lambda i, w: (0, part))
    return pl.pallas_call(
        weight_kernel,
        grid_spec=pltpu.PrefetchScalarGridSpec(
            num_scalar_prefetch=1,
            grid=(count,),
            in_specs=[turned, turned, grads, grads],
            out_specs=pl.BlockSpec(
                (1, 2, SIDE * 128, columns // 2), lambda i, w: (i, 0, 0, 0)
            ),
        ),
        out_shape=jax.ShapeDtypeStruct((count, 2, SIDE * 128, columns // 2), BF16),
        compiler_params=pltpu.CompilerParams(vmem_limit_bytes=VMEM),
        cost_estimate=pl.CostEstimate(
            flops=count * 4 * SIDE * 128 * tokens * columns,
            bytes_accessed=count << 22,
            transcendentals=0,
        ),
        name="weight_chunks",
    )(which, mine, other, grad_own, grad_far)


def ring_pairs(axis, step):
    pairs = []
    for x in range(SIDE):
        for y in range(SIDE):
            to = ((x + step) % SIDE, y) if axis == 0 else (x, (y + step) % SIDE)
            pairs.append((x * SIDE + y, to[0] * SIDE + to[1]))
    return pairs


def send(value, axis, step):
    return lax.ppermute(value, "enc", ring_pairs(axis, step))


def add(*terms):
    return sum(t.astype(F32) for t in terms).astype(BF16)


def on_device(
    enc_states,
    kv_weight,
    queries,
    out_grad,
    passage_order,
    passage_blocks,
    ret_tokens,
    ret_weight,
    question_emb,
):
    pass_dev, _, slot_len, width = enc_states.shape
    heads, pair_width = kv_weight.shape[1:]
    question_count, query_len = queries.shape[:2]
    enc_rank = lax.axis_index("enc")
    dec_rank = lax.axis_index("dec")
    ret_rank = lax.axis_index("ret")
    order_row = passage_order[0]
    blocks_row = passage_blocks[0]
    tokens = pass_dev * slot_len
    swap = [(0, 1), (1, 0)]

    packed = jnp.concatenate(
        [queries[:, :, 0, :] * jnp.asarray(0.125, BF16), out_grad[:, :, 0, :]], axis=-1
    ).reshape(question_count * query_len, pair_width)
    gathered = lax.all_to_all(
        jnp.broadcast_to(packed[None], (N_ENC,) + packed.shape),
        "enc",
        split_axis=0,
        concat_axis=0,
        tiled=True,
    )

    tok_rows = enc_states.reshape(tokens, width)
    mine, to_send = turn(ret_rank, tok_rows)
    other = lax.ppermute(to_send, "ret", swap)
    key_value = project(tok_rows, kv_weight)

    own_pass = enc_rank * pass_dev + jnp.arange(pass_dev, dtype=jnp.int32)
    slot_of = jnp.sum(
        jnp.where(
            order_row[None, :] == own_pass[:, None],
            jnp.arange(order_row.shape[0], dtype=jnp.int32)[None, :],
            0,
        ),
        axis=1,
    )
    own_question = slot_of // PASS
    own_blocks = lax.dynamic_slice_in_dim(blocks_row, enc_rank * pass_dev, pass_dev)
    own_emb = jnp.sum(
        jnp.where(
            (own_question[:, None] == jnp.arange(question_count)[None, :])[..., None],
            question_emb[None],
            0.0,
        ),
        axis=1,
    )
    ret_rows = ret_tokens.reshape(tokens, ret_tokens.shape[3])
    ret_width = ret_rows.shape[1]
    pre_act = jnp.dot(ret_rows, ret_weight, preferred_element_type=F32).reshape(
        pass_dev, slot_len, ret_width
    )
    own_live = jnp.arange(slot_len, dtype=jnp.int32)[None, :] < BLK * own_blocks[:, None]
    own_length = (BLK * own_blocks).astype(F32)
    embed_own = (
        jnp.sum(jnp.where(own_live[..., None], jax.nn.gelu(pre_act), 0.0), axis=1)
        / own_length[:, None]
    )
    own_score = jnp.sum(own_emb * embed_own, axis=-1)
    score_rows = jnp.broadcast_to(
        jnp.concatenate([own_score, jnp.zeros((8 - pass_dev,), F32)])[:, None], (8, 128)
    )

    stats = local_stats(own_question, own_blocks, key_value, gathered, score_rows)
    stats_all = lax.all_to_all(
        jnp.broadcast_to(stats[None], (N_ENC,) + stats.shape),
        "enc",
        split_axis=0,
        concat_axis=0,
        tiled=True,
    )
    grad_rows, grad_flat, aux = backward(
        own_question, own_blocks, enc_rank, order_row, key_value, gathered, stats_all
    )
    kv_grad = grad_rows.reshape(pass_dev, 1, slot_len, heads, pair_width)
    grad_far = lax.ppermute(grad_flat, "ret", swap)

    mine4 = mine.reshape(SIDE, SIDE, 128, tokens)
    other4 = other.reshape(SIDE, SIDE, 128, tokens)
    at = (enc_rank // SIDE, enc_rank % SIDE)
    opposite, rest = [], []
    for part in range(2):
        which = (at[part] + jnp.array([2], jnp.int32)) % SIDE
        opposite.append(weight_chunks(which, part, mine4, other4, grad_flat, grad_far))
    came = []
    for part in range(2):
        came.append(
            (send(opposite[part][0, 0], part, 1), send(opposite[part][0, 1], part, -1))
        )
    for part in range(2):
        which = (at[part] + jnp.array([1, 3, 0], jnp.int32)) % SIDE
        rest.append(weight_chunks(which, part, mine4, other4, grad_flat, grad_far))
    sent = []
    for part in range(2):
        chunk = rest[part]
        up = jnp.stack([add(chunk[0, 0], came[part][0]), chunk[0, 1]])
        down = jnp.stack([chunk[1, 0], add(chunk[1, 1], came[part][1])])
        sent.append((send(up, part, 1), send(down, part, -1)))
    sums = []
    for part in range(2):
        total = add(rest[part][2], sent[part][0], sent[part][1])
        sums.append(total.reshape(2, SIDE, 128, total.shape[-1]))
    pick = lambda a, k: lax.dynamic_index_in_dim(a, k % SIDE, 1, keepdims=False)
    came = []
    for part in range(2):
        far = pick(sums[part], at[1 - part] + 2)
        came.append((send(far[0], 1 - part, 1), send(far[1], 1 - part, -1)))
    sent = []
    for part in range(2):
        up, down = pick(sums[part], at[1 - part] + 1), pick(sums[part], at[1 - part] + 3)
        up = jnp.stack([add(up[0], came[part][0]), up[1]])
        down = jnp.stack([down[0], add(down[1], came[part][1])])
        sent.append((send(up, 1 - part, 1), send(down, 1 - part, -1)))
    done = []
    for part in range(2):
        total = add(pick(sums[part], at[1 - part]), sent[part][0], sent[part][1])
        done += [total[0], total[1]]
    weight_total = jnp.concatenate(done, axis=1).reshape(128, heads, pair_width)

    masses = aux
    for step in range(1, N_DEC):
        masses = masses + lax.ppermute(
            aux, "dec", [(i, (i + step) % N_DEC) for i in range(N_DEC)]
        )
    own_mass = masses[:pass_dev, 0] / (N_DEC * heads * query_len)
    gap = aux[pass_dev : 2 * pass_dev, 0] - own_mass
    embed_grad = gap[:, None] * own_emb / own_length[:, None]
    hidden_grad = jnp.where(own_live[..., None], embed_grad[:, None, :], 0.0)
    pre_grad = gelu_grad(pre_act, hidden_grad).astype(BF16).reshape(tokens, ret_width)
    share = ret_width // N_DEC
    part_rows = lax.dynamic_slice_in_dim(ret_rows, dec_rank * share, share, axis=1)
    ret_part = lax.dot_general(
        part_rows, pre_grad, (((0,), (0,)), ((), ())), preferred_element_type=F32
    ).reshape(2, share // 2, ret_width)
    keep = lax.dynamic_index_in_dim(ret_part, ret_rank, 0, keepdims=False)
    give = lax.dynamic_index_in_dim(ret_part, 1 - ret_rank, 0, keepdims=False)
    ret_half = add(keep, lax.ppermute(give.astype(BF16), "ret", swap))
    pieces = lax.all_to_all(
        ret_half.reshape(N_ENC, share // 2 // N_ENC * ret_width),
        "enc",
        split_axis=0,
        concat_axis=0,
        tiled=True,
    )
    piece = jnp.sum(pieces.astype(F32), axis=0, keepdims=True).astype(BF16)
    half = lax.all_to_all(
        jnp.broadcast_to(piece, pieces.shape), "enc", split_axis=0, concat_axis=0, tiled=True
    ).reshape(share // 2, ret_width)
    half_far = lax.ppermute(half, "ret", swap)
    quarter = jnp.where(
        ret_rank == 0, jnp.stack([half, half_far]), jnp.stack([half_far, half])
    ).reshape(share, ret_width)
    ret_weight_grad = jnp.zeros((N_DEC, share, ret_width), BF16)
    for step in range(N_DEC):
        piece = quarter
        if step:
            piece = lax.ppermute(
                quarter, "dec", [(i, (i + step) % N_DEC) for i in range(N_DEC)]
            )
        ret_weight_grad = lax.dynamic_update_index_in_dim(
            ret_weight_grad, piece, (dec_rank - step) % N_DEC, 0
        )
    return (kv_grad, weight_total, ret_weight_grad.reshape(ret_width, ret_width))


def solution(mesh):
    return jax.shard_map(
        on_device,
        mesh=mesh,
        in_specs=(
            P("enc", "ret", None, None),
            P(None, "dec", None),
            P("ret", None, ("dec", "enc"), None),
            P("ret", None, ("dec", "enc"), None),
            P("ret", None),
            P("ret", None),
            P("enc", "ret", None, None),
            P(),
            P("ret", None),
        ),
        out_specs=(P("enc", "ret", None, "dec", None), P(("enc", "ret"), "dec", None), P()),
        check_vma=False,
    )
```

time: 609 us -> 226 us (0.37)
  waiting for transfers between devices: 222 us -> 40 us
  blocking collectives: 189 us -> 26.2 us
  local copies, waits for them, and re-layouts: 101 us -> 19.7 us
  Pallas kernels: 0 us -> 63.7 us
  matrix products: 48.5 us -> 2.43 us
  starting transfers between devices: 17.4 us -> 49.9 us
  between operations: 14.3 us -> 1.63 us
    psum x1 -> x0, blocking collectives: 189 us -> none  [on_device(): lax.psum((mass_part, score_part.reshape(question_count, PASS)), ('enc', '...]
    reduce_scatter x1 -> x0, waiting for transfers between devices: 114 us -> none  [on_device(): lax.psum_scatter(term.reshape(width // (lax.axis_size('enc') * lax.axis_s...]
    pallas_call x0 -> x8, Pallas kernels: none -> 63.7 us  [the longest x4 23.5 us: weight_chunks(): pl.pallas_call(weight_kernel, grid_spec=pltpu.PrefetchScalarGridSpec(num_...]
    psum x1 -> x0, waiting for transfers between devices: 49.6 us -> none  [on_device(): lax.psum(ret_part_grad.astype(jnp.bfloat16), ('enc', 'ret'))]
    all_to_all x2, waiting for transfers between devices: 58 us -> 11.4 us  [the longest x1 11.4 us: on_device(): lax.all_to_all(jnp.broadcast_to(packed[None], (N_ENC,) + packed.shape), '...]
    dot_general x11 -> x2, matrix products: 48.5 us -> 2.43 us  [the longest x1 2.11 us: on_device(): jnp.dot(ret_rows, ret_weight, preferred_element_type=F32)]
    ppermute x0 -> x26, starting transfers between devices: none -> 39 us  [the longest x16 27 us: send(): return lax.ppermute(value, 'enc', ring_pairs(axis, step))]
    unnamed x31 -> x49, local copies, waits for them, and re-layouts: 36.5 us -> 7.22 us
  transfers between devices with their start and end apart: 4 -> 28, of which waited for: 3 -> 11; matrix products, arithmetic and copies ran while one was open for 11% -> 14% of each run, Pallas kernels for 0% -> 26%
where the time goes in v1:
time: 226 us; the launch traced here: 224 us
  Pallas kernels  63.7 us (28%)
  starting transfers between devices  49.9 us (22%)
  waiting for transfers between devices  40 us (18%)
  blocking collectives  26.2 us (12%)
  other arithmetic  20.7 us (9%)
  local copies, waits for them, and re-layouts  19.7 us (9%)
  matrix products  2.43 us (1%)
    ppermute x16, starting transfers between devices, send(): return lax.ppermute(value, 'enc', ring_pairs(axis, step))  27 us
    pallas_call x4, Pallas kernels, weight_chunks(): pl.pallas_call(weight_kernel, grid_spec=pltpu.PrefetchScalarGridSpec(num_...  23.5 us
    ppermute x16, waiting for transfers between devices, send(): return lax.ppermute(value, 'enc', ring_pairs(axis, step))  17.6 us
    pallas_call x1, Pallas kernels, project(): pl.pallas_call(project_kernel, grid=(width // depth,), out_shape=jax.Shap...  16.1 us
    all_to_all x1, blocking collectives, on_device(): lax.all_to_all(ret_half.reshape(N_ENC, share // 2 // N_ENC * ret_width),...  14.9 us
    all_to_all x1, waiting for transfers between devices, on_device(): lax.all_to_all(jnp.broadcast_to(packed[None], (N_ENC,) + packed.shape), '...  11.4 us
    all_to_all x1, blocking collectives, on_device(): lax.all_to_all(jnp.broadcast_to(piece, pieces.shape), 'enc', split_axis=0...  11.3 us
    pallas_call x1, Pallas kernels, turn(): pl.pallas_call(turn_kernel, grid_spec=pltpu.PrefetchScalarGridSpec(num_sc...  10.7 us
  transfers between devices with their start and end apart: 28, of which 11 were waited for; matrix products, arithmetic and copies ran while one was open for 14% of the time, Pallas kernels for 26%

profile of v1, /device:TPU:0, one launch (start us, length us, event | category | flops | bytes accessed | tf_op | source)
XLA Modules:
  0.0 224.3 jit_solution(17015114833272535424)
XLA Ops:
  4.5 7.3 %all-to-all-start = ((bf16[16,512,128]{2,1,0:T(8,128)(2,1)}), bf16[16,512,128]{2,1,0:T(8,128)(2,1)}, u32[]{:S(2)}, u32[]{:S(2)}) async-start(bf16[16,512,128]{2,1,0:T(8,128)(2,1)} %broadcast_in_dim.116), calls=%async_computation | async-start | bytes 4194304 | tf_op jit(solution)/shard_map/all_to_all | solution.py:350
  12.4 2.1 select_reduce_fusion
  14.7 16.1 %project.1.kv_ref = f32[16,512,128]{2,1,0:T(8,128)} custom-call(bf16[512,4096]{1,0:T(8,128)(2,1)} %bitcast.159, bf16[4096,16,128]{2,1,0:T(8,128)(2,1)} %w_ref.1), custom_call_target="tpu_custom_call" | custom-call | flops 8589934592 | bytes 25165824 | tf_op jit(solution)/shard_map/project/pallas_call | solution.py:44
  30.8 11.4 %all-to-all-done.qd_ref = bf16[16,512,128]{2,1,0:T(8,128)(2,1)} async-done(((bf16[16,512,128]{2,1,0:T(8,128)(2,1)}), bf16[16,512,128]{2,1,0:T(8,128)(2,1)}, u32[]{:S(2)}, u32[]{:S(2)}) %all-to-all-start) | async-done | bytes 2097184 | tf_op jit(solution)/shard_map/all_to_all | solution.py:350
  42.9 5.7 %local_stats.1 = f32[72,128]{1,0:T(8,128)} custom-call(s32[2]{0:T(128)} %copy-done.12, s32[2]{0:T(128)} %copy-done.11, f32[16,512,128]{2,1,0:T(8,128)} %project.1.kv_ref, bf16[16,512,128]{2,1,0:T(8,128)(2,1)} %all-to-all-done.qd_ref, f32[8,128]{1,0:T(8,128)} %broadcast_in_dim.122.score_ref), custom_call_target="tpu_custom_call" | custom-call | flops 2147483648 | bytes 6291456 | tf_op jit(solution)/shard_map/local_stats/pallas_call | solution.py:138
  50.2 3.6 %all-to-all-start.1 = ((f32[16,72,128]{2,1,0:T(8,128)}), f32[16,72,128]{2,1,0:T(8,128)S(1)}, u32[]{:S(2)}, u32[]{:S(2)}) async-start(f32[16,72,128]{2,1,0:T(8,128)} %broadcast_in_dim.123), calls=%async_computation.1 | async-start | bytes 1179648 | tf_op jit(solution)/shard_map/all_to_all | solution.py:399
  53.9 10.7 %turn.1 = (bf16[16,128,512]{2,1,0:T(8,128)(2,1)}, bf16[16,128,512]{2,1,0:T(8,128)(2,1)}) custom-call(s32[1]{0:T(128)} %bitcast.9.rank_ref, bf16[512,4096]{1,0:T(8,128)(2,1)} %bitcast.160), custom_call_target="tpu_custom_call" | custom-call | bytes 8388608 | tf_op jit(solution)/shard_map/turn/pallas_call | solution.py:72
  65.4 7.7 %backward.1 = (bf16[512,16,128]{2,1,0:T(8,128)(2,1)}, bf16[512,2048]{1,0:T(8,128)(2,1)}, f32[8,128]{1,0:T(8,128)}) custom-call(s32[2]{0:T(128)} %copy-done.12, s32[2]{0:T(128)} %copy-done.11, s32[1]{0:T(128)} %bitcast.2.own_ref, s32[32]{0:T(128)} %bitcast.186, f32[16,512,128]{2,1,0:T(8,128)} %project.1.kv_ref, bf16[16,512,128]{2,1,0:T(8,128)(2,1)} %all-to-all-done.qd_ref, ...), custom_call_target="tpu_custom_call" | custom-call | flops 3221225472 | bytes 10485760 | tf_op jit(solution)/shard_map/backward/pallas_call | solution.py:235
  75.0 3.6 %collective-permute-start.19 = (f32[8,128]{1,0:T(8,128)}, f32[8,128]{1,0:T(8,128)S(1)}, u32[]{:S(2)}, u32[]{:S(2)}) collective-permute-start(f32[8,128]{1,0:T(8,128)} %get-tuple-element.12), channel_id=1, source_target_pairs={{0,4},{2,6},{4,0},{6,2},{1,5},{3,7},{5,1},{7,3},{8,12},{10,14},{12... | collective-permute-start | bytes 12296 | tf_op jit(solution)/shard_map/ppermute | solution.py:456
  84.0 2.6 %fusion.10 = bf16[2,256,768]{2,1,0:T(8,128)(2,1)S(1)} fusion(f32[2,256,768]{2,1,0:T(8,128)} %get-tuple-element.61, f32[2,768]{1,0:T(2,128)S(1)} %multiply_divide_fusion, pred[2,256]{1,0:T(4,128)(4,1)S(1)} %iota_compare_fusion), kind=kLoop, calls=%fused_computation.16 | loop fusion | flops 8257536 | bytes 2365952 | tf_op jit(solution)/shard_map/convert_element_type | solution.py:463
  90.5 14.9 %all_to_all.26 = bf16[16,2,2304]{2,1,0:T(2,128)(2,1)S(1)} all-to-all(bf16[16,2,2304]{2,1,0:T(2,128)(2,1)S(1)} %reshape.298), channel_id=1, replica_groups=mesh['enc'=16,'dec'=4,'ret'=2] {'enc'}, dimensions={0} | all-to-all | bytes 294912 | tf_op jit(solution)/shard_map/all_to_all | solution.py:472
  107.5 11.3 %all_to_all.27 = bf16[16,2,2304]{2,1,0:T(2,128)(2,1)S(1)} all-to-all(bf16[16,2,2304]{2,1,0:T(2,128)(2,1)S(1)} %reshape.300), channel_id=1, replica_groups=mesh['enc'=16,'dec'=4,'ret'=2] {'enc'}, dimensions={0} | all-to-all | bytes 294912 | tf_op jit(solution)/shard_map/all_to_all | solution.py:480
  122.1 3.7 %collective-permute-start.24 = (bf16[192,768]{1,0:T(8,128)(2,1)S(1)}, bf16[192,768]{1,0:T(8,128)(2,1)}, u32[]{:S(2)}, u32[]{:S(2)}) collective-permute-start(bf16[192,768]{1,0:T(8,128)(2,1)S(1)} %bitcast.168), channel_id=1, source_target_pairs={{0,4},{2,6},{4,0},{6,2},{1,5},{3,7},{5,1},{7,3},{8,12},{10,14},{12... | collective-permute-start | bytes 884744 | tf_op jit(solution)/shard_map/ppermute | solution.py:491
  125.9 6.2 %collective-permute-done.23 = bf16[192,768]{1,0:T(8,128)(2,1)S(1)} collective-permute-done((bf16[192,768]{1,0:T(8,128)(2,1)S(1)}, bf16[192,768]{1,0:T(8,128)(2,1)S(1)}, u32[]{:S(2)}, u32[]{:S(2)}) %collective-permute-start.23) | collective-permute-done | bytes 294944 | tf_op jit(solution)/shard_map/ppermute | solution.py:491
  133.5 4.1 %weight_chunks.5 = bf16[1,2,512,512]{3,2,1,0:T(8,128)(2,1)} custom-call(s32[1]{0:T(128)S(6)} %select_n.180.which_ref, bf16[4,4,128,512]{3,2,1,0:T(8,128)(2,1)} %bitcast.151, bf16[4,4,128,512]{3,2,1,0:T(8,128)(2,1)} %bitcast.155, bf16[512,2048]{1,0:T(8,128)(2,1)} %get-tuple-element.11.own_ref, bf16[512,2048]{1,0:T(8,128)(2,1)} %collective-permute-done.1.far_ref), custom_call_target="tpu_custom_call" | custom-call | flops 1073741824 | bytes 4194304 | tf_op jit(solution)/shard_map/weight_chunks/pallas_call | solution.py:287
  137.6 2.1 slice_bitcast_fusion.12
  140.1 2.8 %collective-permute-start.4 = (bf16[512,512]{1,0:T(8,128)(2,1)S(1)}, bf16[512,512]{1,0:T(8,128)(2,1)}, u32[]{:S(2)}, u32[]{:S(2)}) collective-permute-start(bf16[512,512]{1,0:T(8,128)(2,1)S(1)} %get-tuple-element.45), channel_id=1, source_target_pairs={{0,96},{8,104},{16,112},{24,120},{32,0},{40,8},{48,16},{56,24},{64... | collective-permute-start | bytes 1572872 | tf_op jit(solution)/shard_map/ppermute | solution.py:318
  142.9 4.1 %weight_chunks.7 = bf16[1,2,512,512]{3,2,1,0:T(8,128)(2,1)} custom-call(s32[1]{0:T(128)S(6)} %select_n.191.which_ref, bf16[4,4,128,512]{3,2,1,0:T(8,128)(2,1)} %bitcast.152, bf16[4,4,128,512]{3,2,1,0:T(8,128)(2,1)} %bitcast.156, bf16[512,2048]{1,0:T(8,128)(2,1)} %get-tuple-element.11.own_ref, bf16[512,2048]{1,0:T(8,128)(2,1)} %collective-permute-done.1.far_ref), custom_call_target="tpu_custom_call" | custom-call | flops 1073741824 | bytes 4194304 | tf_op jit(solution)/shard_map/weight_chunks/pallas_call | solution.py:287
  146.9 2.3 %slice_bitcast_fusion.6 = (bf16[512,512]{1,0:T(8,128)(2,1)}, bf16[512,512]{1,0:T(8,128)(2,1)}) fusion(bf16[1,2,512,512]{3,2,1,0:T(8,128)(2,1)} %weight_chunks.7), kind=kLoop, calls=%fused_computation.46 | loop fusion | bytes 2097152 | tf_op jit(solution)/shard_map/squeeze | solution.py:422
  149.7 2.8 %collective-permute-start.12 = (bf16[512,512]{1,0:T(8,128)(2,1)}, bf16[512,512]{1,0:T(8,128)(2,1)}, u32[]{:S(2)}, u32[]{:S(2)}) collective-permute-start(bf16[512,512]{1,0:T(8,128)(2,1)} %get-tuple-element.53), channel_id=1, source_target_pairs={{0,24},{8,0},{16,8},{24,16},{32,56},{40,32},{48,40},{56,48},{64,88... | collective-permute-start | bytes 1572872 | tf_op jit(solution)/shard_map/ppermute | solution.py:318
  152.4 7.6 %weight_chunks.4 = bf16[3,2,512,512]{3,2,1,0:T(8,128)(2,1)} custom-call(s32[3]{0:T(128)} %get-tuple-element.58.which_ref, bf16[4,4,128,512]{3,2,1,0:T(8,128)(2,1)} %bitcast.153, bf16[4,4,128,512]{3,2,1,0:T(8,128)(2,1)} %bitcast.157, bf16[512,2048]{1,0:T(8,128)(2,1)} %get-tuple-element.11.own_ref, bf16[512,2048]{1,0:T(8,128)(2,1)} %collective-permute-done.1.far_ref), custom_call_target="tpu_custom_call" | custom-call | flops 3221225472 | bytes 12582912 | tf_op jit(solution)/shard_map/weight_chunks/pallas_call | solution.py:287
  161.4 7.7 %weight_chunks.6 = bf16[3,2,512,512]{3,2,1,0:T(8,128)(2,1)} custom-call(s32[3]{0:T(128)} %get-tuple-element.59.which_ref, bf16[4,4,128,512]{3,2,1,0:T(8,128)(2,1)} %bitcast.154, bf16[4,4,128,512]{3,2,1,0:T(8,128)(2,1)} %bitcast.158, bf16[512,2048]{1,0:T(8,128)(2,1)} %get-tuple-element.11.own_ref, bf16[512,2048]{1,0:T(8,128)(2,1)} %collective-permute-done.1.far_ref), custom_call_target="tpu_custom_call" | custom-call | flops 3221225472 | bytes 12582912 | tf_op jit(solution)/shard_map/weight_chunks/pallas_call | solution.py:287
  171.9 3.3 %collective-permute-start.5 = (bf16[2,512,512]{2,1,0:T(8,128)(2,1)S(1)}, bf16[2,512,512]{2,1,0:T(8,128)(2,1)S(1)}, u32[]{:S(2)}, u32[]{:S(2)}) collective-permute-start(bf16[2,512,512]{2,1,0:T(8,128)(2,1)S(1)} %pad_maximum_fusion.1), channel_id=1, source_target_pairs={{0,96},{8,104},{16,112},{24,120},{32,0},{40,8},{48,16},{56,24},{64... | collective-permute-start | bytes 3145736 | tf_op jit(solution)/shard_map/ppermute | solution.py:318
  180.5 3.2 %collective-permute-start.13 = (bf16[2,512,512]{2,1,0:T(8,128)(2,1)}, bf16[2,512,512]{2,1,0:T(8,128)(2,1)}, u32[]{:S(2)}, u32[]{:S(2)}) collective-permute-start(bf16[2,512,512]{2,1,0:T(8,128)(2,1)} %pad_maximum_fusion.3), channel_id=1, source_target_pairs={{0,24},{8,0},{16,8},{24,16},{32,56},{40,32},{48,40},{56,48},{64,88... | collective-permute-start | bytes 3145736 | tf_op jit(solution)/shard_map/ppermute | solution.py:318
  184.8 11.1 %collective-permute-done.3 = bf16[2,512,512]{2,1,0:T(8,128)(2,1)S(1)} collective-permute-done((bf16[2,512,512]{2,1,0:T(8,128)(2,1)S(1)}, bf16[2,512,512]{2,1,0:T(8,128)(2,1)S(1)}, u32[]{:S(2)}, u32[]{:S(2)}) %collective-permute-start.3) | collective-permute-done | bytes 1048608 | tf_op jit(solution)/shard_map/ppermute | solution.py:318
  198.5 3.3 %collective-permute-start.8 = (bf16[128,512]{0,1:T(8,128)(2,1)S(1)}, bf16[128,512]{0,1:T(8,128)(2,1)S(1)}, u32[]{:S(2)}, u32[]{:S(2)}) collective-permute-start(bf16[128,512]{0,1:T(8,128)(2,1)S(1)} %bitcast.181), channel_id=1, source_target_pairs={{0,24},{8,0},{16,8},{24,16},{32,56},{40,32},{48,40},{56,48},{64,88... | collective-permute-start | bytes 393224 | tf_op jit(solution)/shard_map/ppermute | solution.py:318
  202.0 2.1 collective-permute-done.11
  204.5 2.3 %fusion.1 = bf16[2,512,512]{2,1,0:T(8,128)(2,1)S(1)} fusion(bf16[2,512,512]{2,1,0:T(8,128)(2,1)} %collective-permute-done.13, bf16[2,512,512]{2,1,0:T(8,128)(2,1)} %collective-permute-done.11, bf16[3,2,512,512]{3,2,1,0:T(8,128)(2,1)} %weight_chunks.6), kind=kLoop, calls=%fused_computation.6 | loop fusion | flops 3145728 | bytes 4194304 | tf_op jit(solution)/shard_map/convert_element_type | solution.py:322
  207.6 3.3 %collective-permute-start.16 = (bf16[128,512]{0,1:T(8,128)(2,1)S(1)}, bf16[128,512]{0,1:T(8,128)(2,1)S(1)}, u32[]{:S(2)}, u32[]{:S(2)}) collective-permute-start(bf16[128,512]{0,1:T(8,128)(2,1)S(1)} %bitcast.183), channel_id=1, source_target_pairs={{0,96},{8,104},{16,112},{24,120},{32,0},{40,8},{48,16},{56,24},{64... | collective-permute-start | bytes 393224 | tf_op jit(solution)/shard_map/ppermute | solution.py:318
  211.4 3.8 %collective-permute-start.9 = (bf16[2,128,512]{1,2,0:T(8,128)(2,1)S(1)}, bf16[2,128,512]{1,2,0:T(8,128)(2,1)S(1)}, u32[]{:S(2)}, u32[]{:S(2)}) collective-permute-start(bf16[2,128,512]{1,2,0:T(8,128)(2,1)S(1)} %pad_maximum_fusion.6), channel_id=1, source_target_pairs={{0,24},{8,0},{16,8},{24,16},{32,56},{40,32},{48,40},{56,48},{64,88... | collective-permute-start | bytes 786440 | tf_op jit(solution)/shard_map/ppermute | solution.py:318
  215.4 3.3 %collective-permute-start.17 = (bf16[2,128,512]{1,2,0:T(8,128)(2,1)S(1)}, bf16[2,128,512]{1,2,0:T(8,128)(2,1)S(1)}, u32[]{:S(2)}, u32[]{:S(2)}) collective-permute-start(bf16[2,128,512]{1,2,0:T(8,128)(2,1)S(1)} %pad_maximum_fusion.8), channel_id=1, source_target_pairs={{0,96},{8,104},{16,112},{24,120},{32,0},{40,8},{48,16},{56,24},{64... | collective-permute-start | bytes 786440 | tf_op jit(solution)/shard_map/ppermute | solution.py:318
  219.5 3.4 %collective-permute-done.15 = bf16[2,128,512]{1,2,0:T(8,128)(2,1)S(1)} collective-permute-done((bf16[2,128,512]{1,2,0:T(8,128)(2,1)S(1)}, bf16[2,128,512]{1,2,0:T(8,128)(2,1)S(1)}, u32[]{:S(2)}, u32[]{:S(2)}) %collective-permute-start.15) | collective-permute-done | bytes 262176 | tf_op jit(solution)/shard_map/ppermute | solution.py:318
  (155 shorter events, 43.4 us)
Async XLA Ops:
  0.6 11.8 %copy-start = (bf16[768,768]{1,0:T(8,128)(2,1)S(1)}, bf16[768,768]{1,0:T(8,128)(2,1)}, u32[]{:S(2)}) copy-start(bf16[768,768]{1,0:T(8,128)(2,1)} %param.20) | copy-start | bytes 3538948
  4.5 7.9 %copy-start.7 = (bf16[2,1,256,768]{3,2,1,0:T(8,128)(2,1)S(1)}, bf16[2,1,256,768]{3,2,1,0:T(8,128)(2,1)}, u32[]{:S(2)}) copy-start(bf16[2,1,256,768]{3,2,1,0:T(8,128)(2,1)} %param.19) | copy-start | bytes 2359300
  4.5 37.8 %all-to-all-start = ((bf16[16,512,128]{2,1,0:T(8,128)(2,1)}), bf16[16,512,128]{2,1,0:T(8,128)(2,1)}, u32[]{:S(2)}, u32[]{:S(2)}) async-start(bf16[16,512,128]{2,1,0:T(8,128)(2,1)} %broadcast_in_dim.116), calls=%async_computation | async-start | bytes 4194304 | tf_op jit(solution)/shard_map/all_to_all | solution.py:350
  50.2 14.3 %all-to-all-start.1 = ((f32[16,72,128]{2,1,0:T(8,128)}), f32[16,72,128]{2,1,0:T(8,128)S(1)}, u32[]{:S(2)}, u32[]{:S(2)}) async-start(f32[16,72,128]{2,1,0:T(8,128)} %broadcast_in_dim.123), calls=%async_computation.1 | async-start | bytes 1179648 | tf_op jit(solution)/shard_map/all_to_all | solution.py:399
  64.6 67.6 %collective-permute-start = (bf16[16,128,512]{2,1,0:T(8,128)(2,1)}, bf16[16,128,512]{2,1,0:T(8,128)(2,1)S(1)}, u32[]{:S(2)}, u32[]{:S(2)}) collective-permute-start(bf16[16,128,512]{2,1,0:T(8,128)(2,1)} %get-tuple-element.10), channel_id=1, source_target_pairs={{0,1},{1,0},{2,3},{3,2},{4,5},{5,4},{6,7},{7,6},{8,9},{9,8},{10,11... | collective-permute-start | bytes 6291464 | tf_op jit(solution)/shard_map/ppermute | solution.py:360
  73.1 6.9 %collective-permute-start.18 = (f32[8,128]{1,0:T(8,128)}, f32[8,128]{1,0:T(8,128)S(1)}, u32[]{:S(2)}, u32[]{:S(2)}) collective-permute-start(f32[8,128]{1,0:T(8,128)} %get-tuple-element.12), channel_id=1, source_target_pairs={{0,2},{2,4},{4,6},{6,0},{1,3},{3,5},{5,7},{7,1},{8,10},{10,12},{12... | collective-permute-start | bytes 12296 | tf_op jit(solution)/shard_map/ppermute | solution.py:456
  75.0 5.4 %collective-permute-start.19 = (f32[8,128]{1,0:T(8,128)}, f32[8,128]{1,0:T(8,128)S(1)}, u32[]{:S(2)}, u32[]{:S(2)}) collective-permute-start(f32[8,128]{1,0:T(8,128)} %get-tuple-element.12), channel_id=1, source_target_pairs={{0,4},{2,6},{4,0},{6,2},{1,5},{3,7},{5,1},{7,3},{8,12},{10,14},{12... | collective-permute-start | bytes 12296 | tf_op jit(solution)/shard_map/ppermute | solution.py:456
  78.6 3.8 %collective-permute-start.20 = (f32[8,128]{1,0:T(8,128)}, f32[8,128]{1,0:T(8,128)S(1)}, u32[]{:S(2)}, u32[]{:S(2)}) collective-permute-start(f32[8,128]{1,0:T(8,128)} %get-tuple-element.12), channel_id=1, source_target_pairs={{0,6},{2,0},{4,2},{6,4},{1,7},{3,1},{5,3},{7,5},{8,14},{10,8},{12,... | collective-permute-start | bytes 12296 | tf_op jit(solution)/shard_map/ppermute | solution.py:456
  79.9 52.3 %collective-permute-start.1 = (bf16[512,2048]{1,0:T(8,128)(2,1)}, bf16[512,2048]{1,0:T(8,128)(2,1)}, u32[]{:S(2)}, u32[]{:S(2)}) collective-permute-start(bf16[512,2048]{1,0:T(8,128)(2,1)} %get-tuple-element.11.own_ref), channel_id=1, source_target_pairs={{0,1},{1,0},{2,3},{3,2},{4,5},{5,4},{6,7},{7,6},{8,9},{9,8},{10,11... | collective-permute-start | bytes 6291464 | tf_op jit(solution)/shard_map/ppermute | solution.py:410
  86.9 1.5 collective-permute-start.21
  107.5 14.1 %copy-start.9 = (s32[3]{0:T(128)S(1)}, s32[3]{0:T(128)}, u32[]{:S(2)}) copy-start(s32[3]{0:T(128)} %constant.216.clone) | copy-start | bytes 40
  120.0 1.5 collective-permute-start.22
  121.4 10.7 %collective-permute-start.23 = (bf16[192,768]{1,0:T(8,128)(2,1)S(1)}, bf16[192,768]{1,0:T(8,128)(2,1)S(1)}, u32[]{:S(2)}, u32[]{:S(2)}) collective-permute-start(bf16[192,768]{1,0:T(8,128)(2,1)S(1)} %bitcast.167), channel_id=1, source_target_pairs={{0,2},{2,4},{4,6},{6,0},{1,3},{3,5},{5,7},{7,1},{8,10},{10,12},{12... | collective-permute-start | bytes 884744 | tf_op jit(solution)/shard_map/ppermute | solution.py:491
  122.1 58.4 %collective-permute-start.24 = (bf16[192,768]{1,0:T(8,128)(2,1)S(1)}, bf16[192,768]{1,0:T(8,128)(2,1)}, u32[]{:S(2)}, u32[]{:S(2)}) collective-permute-start(bf16[192,768]{1,0:T(8,128)(2,1)S(1)} %bitcast.168), channel_id=1, source_target_pairs={{0,4},{2,6},{4,0},{6,2},{1,5},{3,7},{5,1},{7,3},{8,12},{10,14},{12... | collective-permute-start | bytes 884744 | tf_op jit(solution)/shard_map/ppermute | solution.py:491
  139.6 29.4 %collective-permute-start.2 = (bf16[512,512]{1,0:T(8,128)(2,1)}, bf16[512,512]{1,0:T(8,128)(2,1)S(1)}, u32[]{:S(2)}, u32[]{:S(2)}) collective-permute-start(bf16[512,512]{1,0:T(8,128)(2,1)} %get-tuple-element.44), channel_id=1, source_target_pairs={{0,32},{8,40},{16,48},{24,56},{32,64},{40,72},{48,80},{56,88},{64,... | collective-permute-start | bytes 1572872 | tf_op jit(solution)/shard_map/ppermute | solution.py:318
  140.1 29.7 %collective-permute-start.4 = (bf16[512,512]{1,0:T(8,128)(2,1)S(1)}, bf16[512,512]{1,0:T(8,128)(2,1)}, u32[]{:S(2)}, u32[]{:S(2)}) collective-permute-start(bf16[512,512]{1,0:T(8,128)(2,1)S(1)} %get-tuple-element.45), channel_id=1, source_target_pairs={{0,96},{8,104},{16,112},{24,120},{32,0},{40,8},{48,16},{56,24},{64... | collective-permute-start | bytes 1572872 | tf_op jit(solution)/shard_map/ppermute | solution.py:318
  149.2 26.1 %collective-permute-start.10 = (bf16[512,512]{1,0:T(8,128)(2,1)}, bf16[512,512]{1,0:T(8,128)(2,1)}, u32[]{:S(2)}, u32[]{:S(2)}) collective-permute-start(bf16[512,512]{1,0:T(8,128)(2,1)} %get-tuple-element.52), channel_id=1, source_target_pairs={{0,8},{8,16},{16,24},{24,0},{32,40},{40,48},{48,56},{56,32},{64,72... | collective-permute-start | bytes 1572872 | tf_op jit(solution)/shard_map/ppermute | solution.py:318
  149.7 27.1 %collective-permute-start.12 = (bf16[512,512]{1,0:T(8,128)(2,1)}, bf16[512,512]{1,0:T(8,128)(2,1)}, u32[]{:S(2)}, u32[]{:S(2)}) collective-permute-start(bf16[512,512]{1,0:T(8,128)(2,1)} %get-tuple-element.53), channel_id=1, source_target_pairs={{0,24},{8,0},{16,8},{24,16},{32,56},{40,32},{48,40},{56,48},{64,88... | collective-permute-start | bytes 1572872 | tf_op jit(solution)/shard_map/ppermute | solution.py:318
  171.7 24.2 %collective-permute-start.3 = (bf16[2,512,512]{2,1,0:T(8,128)(2,1)S(1)}, bf16[2,512,512]{2,1,0:T(8,128)(2,1)S(1)}, u32[]{:S(2)}, u32[]{:S(2)}) collective-permute-start(bf16[2,512,512]{2,1,0:T(8,128)(2,1)S(1)} %pad_maximum_fusion), channel_id=1, source_target_pairs={{0,32},{8,40},{16,48},{24,56},{32,64},{40,72},{48,80},{56,88},{64,... | collective-permute-start | bytes 3145736 | tf_op jit(solution)/shard_map/ppermute | solution.py:318
  171.9 24.0 %collective-permute-start.5 = (bf16[2,512,512]{2,1,0:T(8,128)(2,1)S(1)}, bf16[2,512,512]{2,1,0:T(8,128)(2,1)S(1)}, u32[]{:S(2)}, u32[]{:S(2)}) collective-permute-start(bf16[2,512,512]{2,1,0:T(8,128)(2,1)S(1)} %pad_maximum_fusion.1), channel_id=1, source_target_pairs={{0,96},{8,104},{16,112},{24,120},{32,0},{40,8},{48,16},{56,24},{64... | collective-permute-start | bytes 3145736 | tf_op jit(solution)/shard_map/ppermute | solution.py:318
  175.3 9.5 %collective-permute-start.25 = (bf16[192,768]{1,0:T(8,128)(2,1)S(1)}, bf16[192,768]{1,0:T(8,128)(2,1)S(1)}, u32[]{:S(2)}, u32[]{:S(2)}) collective-permute-start(bf16[192,768]{1,0:T(8,128)(2,1)S(1)} %bitcast.170), channel_id=1, source_target_pairs={{0,6},{2,0},{4,2},{6,4},{1,7},{3,1},{5,3},{7,5},{8,14},{10,8},{12,... | collective-permute-start | bytes 884744 | tf_op jit(solution)/shard_map/ppermute | solution.py:491
  179.4 24.7 %collective-permute-start.11 = (bf16[2,512,512]{2,1,0:T(8,128)(2,1)}, bf16[2,512,512]{2,1,0:T(8,128)(2,1)}, u32[]{:S(2)}, u32[]{:S(2)}) collective-permute-start(bf16[2,512,512]{2,1,0:T(8,128)(2,1)} %pad_maximum_fusion.2), channel_id=1, source_target_pairs={{0,8},{8,16},{16,24},{24,0},{32,40},{40,48},{48,56},{56,32},{64,72... | collective-permute-start | bytes 3145736 | tf_op jit(solution)/shard_map/ppermute | solution.py:318
  180.5 23.9 %collective-permute-start.13 = (bf16[2,512,512]{2,1,0:T(8,128)(2,1)}, bf16[2,512,512]{2,1,0:T(8,128)(2,1)}, u32[]{:S(2)}, u32[]{:S(2)}) collective-permute-start(bf16[2,512,512]{2,1,0:T(8,128)(2,1)} %pad_maximum_fusion.3), channel_id=1, source_target_pairs={{0,24},{8,0},{16,8},{24,16},{32,56},{40,32},{48,40},{56,48},{64,88... | collective-permute-start | bytes 3145736 | tf_op jit(solution)/shard_map/ppermute | solution.py:318
  184.8 12.8 %copy-start.4 = (bf16[4,192,768]{2,1,0:T(8,128)(2,1)}, bf16[4,192,768]{2,1,0:T(8,128)(2,1)S(1)}, u32[]{:S(2)}) copy-start(bf16[4,192,768]{2,1,0:T(8,128)(2,1)S(1)} %bitcast_dynamic-update-slice_fusion) | copy-start | bytes 3538948
  198.0 13.1 %collective-permute-start.6 = (bf16[128,512]{0,1:T(8,128)(2,1)S(1)}, bf16[128,512]{0,1:T(8,128)(2,1)S(1)}, u32[]{:S(2)}, u32[]{:S(2)}) collective-permute-start(bf16[128,512]{0,1:T(8,128)(2,1)S(1)} %bitcast.182), channel_id=1, source_target_pairs={{0,8},{8,16},{16,24},{24,0},{32,40},{40,48},{48,56},{56,32},{64,72... | collective-permute-start | bytes 393224 | tf_op jit(solution)/shard_map/ppermute | solution.py:318
  198.5 12.8 %collective-permute-start.8 = (bf16[128,512]{0,1:T(8,128)(2,1)S(1)}, bf16[128,512]{0,1:T(8,128)(2,1)S(1)}, u32[]{:S(2)}, u32[]{:S(2)}) collective-permute-start(bf16[128,512]{0,1:T(8,128)(2,1)S(1)} %bitcast.181), channel_id=1, source_target_pairs={{0,24},{8,0},{16,8},{24,16},{32,56},{40,32},{48,40},{56,48},{64,88... | collective-permute-start | bytes 393224 | tf_op jit(solution)/shard_map/ppermute | solution.py:318
  207.2 8.0 %collective-permute-start.14 = (bf16[128,512]{0,1:T(8,128)(2,1)S(1)}, bf16[128,512]{0,1:T(8,128)(2,1)S(1)}, u32[]{:S(2)}, u32[]{:S(2)}) collective-permute-start(bf16[128,512]{0,1:T(8,128)(2,1)S(1)} %bitcast.184), channel_id=1, source_target_pairs={{0,32},{8,40},{16,48},{24,56},{32,64},{40,72},{48,80},{56,88},{64,... | collective-permute-start | bytes 393224 | tf_op jit(solution)/shard_map/ppermute | solution.py:318
  207.6 7.7 %collective-permute-start.16 = (bf16[128,512]{0,1:T(8,128)(2,1)S(1)}, bf16[128,512]{0,1:T(8,128)(2,1)S(1)}, u32[]{:S(2)}, u32[]{:S(2)}) collective-permute-start(bf16[128,512]{0,1:T(8,128)(2,1)S(1)} %bitcast.183), channel_id=1, source_target_pairs={{0,96},{8,104},{16,112},{24,120},{32,0},{40,8},{48,16},{56,24},{64... | collective-permute-start | bytes 393224 | tf_op jit(solution)/shard_map/ppermute | solution.py:318
  211.3 8.1 %collective-permute-start.7 = (bf16[2,128,512]{1,2,0:T(8,128)(2,1)S(1)}, bf16[2,128,512]{1,2,0:T(8,128)(2,1)S(1)}, u32[]{:S(2)}, u32[]{:S(2)}) collective-permute-start(bf16[2,128,512]{1,2,0:T(8,128)(2,1)S(1)} %pad_maximum_fusion.5), channel_id=1, source_target_pairs={{0,8},{8,16},{16,24},{24,0},{32,40},{40,48},{48,56},{56,32},{64,72... | collective-permute-start | bytes 786440 | tf_op jit(solution)/shard_map/ppermute | solution.py:318
  211.4 7.9 %collective-permute-start.9 = (bf16[2,128,512]{1,2,0:T(8,128)(2,1)S(1)}, bf16[2,128,512]{1,2,0:T(8,128)(2,1)S(1)}, u32[]{:S(2)}, u32[]{:S(2)}) collective-permute-start(bf16[2,128,512]{1,2,0:T(8,128)(2,1)S(1)} %pad_maximum_fusion.6), channel_id=1, source_target_pairs={{0,24},{8,0},{16,8},{24,16},{32,56},{40,32},{48,40},{56,48},{64,88... | collective-permute-start | bytes 786440 | tf_op jit(solution)/shard_map/ppermute | solution.py:318
  215.3 7.7 %collective-permute-start.15 = (bf16[2,128,512]{1,2,0:T(8,128)(2,1)S(1)}, bf16[2,128,512]{1,2,0:T(8,128)(2,1)S(1)}, u32[]{:S(2)}, u32[]{:S(2)}) collective-permute-start(bf16[2,128,512]{1,2,0:T(8,128)(2,1)S(1)} %pad_maximum_fusion.7), channel_id=1, source_target_pairs={{0,32},{8,40},{16,48},{24,56},{32,64},{40,72},{48,80},{56,88},{64,... | collective-permute-start | bytes 786440 | tf_op jit(solution)/shard_map/ppermute | solution.py:318
  215.4 7.5 %collective-permute-start.17 = (bf16[2,128,512]{1,2,0:T(8,128)(2,1)S(1)}, bf16[2,128,512]{1,2,0:T(8,128)(2,1)S(1)}, u32[]{:S(2)}, u32[]{:S(2)}) collective-permute-start(bf16[2,128,512]{1,2,0:T(8,128)(2,1)S(1)} %pad_maximum_fusion.8), channel_id=1, source_target_pairs={{0,96},{8,104},{16,112},{24,120},{32,0},{40,8},{48,16},{56,24},{64... | collective-permute-start | bytes 786440 | tf_op jit(solution)/shard_map/ppermute | solution.py:318
  (10 other events, 35.3 us)

commit v2 on v1

v2 whole, which is shorter than its diff:
```python
import functools

import jax
import jax.numpy as jnp
from jax import lax
from jax.experimental import pallas as pl
from jax.experimental.pallas import tpu as pltpu
from jax.sharding import PartitionSpec as P

BLK = 128
PASS = 8
N_ENC = 16
SIDE = 4
N_DEC = 4
LQ = 128
HD = 64
SLOT = 256
F32 = jnp.float32
BF16 = jnp.bfloat16
VMEM = 60 << 20


def gelu_grad(pre_act, upstream):
    return jax.vjp(jax.nn.gelu, pre_act)[1](upstream)[0]


def project_kernel(x_ref, w_ref, o_ref):
    @pl.when(pl.program_id(0) == 0)
    def _():
        o_ref[...] = jnp.zeros_like(o_ref)

    rows = x_ref[...]
    by_head = jnp.swapaxes(w_ref[...], 0, 1)
    for pair in range(by_head.shape[0] // 2):
        both = jnp.concatenate([by_head[2 * pair], by_head[2 * pair + 1]], axis=1)
        part = jnp.dot(rows, both, preferred_element_type=F32)
        o_ref[2 * pair] += part[:, :128]
        o_ref[2 * pair + 1] += part[:, 128:]


def project(tok_rows, kv_weight, depth=512):
    tokens, width = tok_rows.shape
    heads, pair_width = kv_weight.shape[1:]
    return pl.pallas_call(
        project_kernel,
        grid=(width // depth,),
        out_shape=jax.ShapeDtypeStruct((heads, tokens, pair_width), F32),
        in_specs=[
            pl.BlockSpec((tokens, depth), lambda i: (0, i)),
            pl.BlockSpec((depth, heads, pair_width), lambda i: (i, 0, 0)),
        ],
        out_specs=pl.BlockSpec((heads, tokens, pair_width), lambda i: (0, 0, 0)),
        compiler_params=pltpu.CompilerParams(vmem_limit_bytes=VMEM),
        cost_estimate=pl.CostEstimate(
            flops=2 * tokens * width * heads * pair_width,
            bytes_accessed=24 << 20,
            transcendentals=0,
        ),
        name="project",
    )(tok_rows, kv_weight)


def turn_kernel(rank_ref, x_ref, mine_ref, send_ref):
    first = rank_ref[0] == 0
    for block in range(mine_ref.shape[0]):
        even = x_ref[:, block * 256 : block * 256 + 128].T
        odd = x_ref[:, block * 256 + 128 : block * 256 + 256].T
        mine_ref[block] = jnp.where(first, even, odd)
        send_ref[block] = jnp.where(first, odd, even)


def turn(ret_rank, tok_rows, per_step=8):
    tokens, width = tok_rows.shape
    half = jax.ShapeDtypeStruct((N_ENC, 128, tokens), BF16)
    return pl.pallas_call(
        turn_kernel,
        grid_spec=pltpu.PrefetchScalarGridSpec(
            num_scalar_prefetch=1,
            grid=(N_ENC // per_step,),
            in_specs=[pl.BlockSpec((tokens, 256 * per_step), lambda i, r: (0, i))],
            out_specs=[pl.BlockSpec((per_step, 128, tokens), lambda i, r: (i, 0, 0))] * 2,
        ),
        out_shape=[half, half],
        compiler_params=pltpu.CompilerParams(vmem_limit_bytes=VMEM),
        cost_estimate=pl.CostEstimate(flops=0, bytes_accessed=12 << 20, transcendentals=0),
        name="turn",
    )(ret_rank.reshape(1), tok_rows)


def local_scores(kv_ref, qd_ref, head, passage, question, blocks):
    pair = kv_ref[head, passage * SLOT : (passage + 1) * SLOT, :]
    high = pair.astype(BF16)
    low = (pair - high.astype(F32)).astype(BF16)
    rows = qd_ref[head, pl.ds(pl.multiple_of(question * LQ, LQ), LQ), :]
    lane = lax.broadcasted_iota(jnp.int32, rows.shape, 1)
    zero = jnp.zeros_like(rows)
    stacked = jnp.concatenate(
        [jnp.where(lane < HD, rows, zero), jnp.where(lane < HD, zero, rows)], axis=0
    )
    both = lax.dot_general(
        jnp.concatenate([high, low], axis=1),
        jnp.concatenate([stacked, stacked], axis=1),
        (((1,), (1,)), ((), ())),
        preferred_element_type=F32,
    )
    scores = both[:, :LQ]
    place = lax.broadcasted_iota(jnp.int32, scores.shape, 0)
    return jnp.where(place < BLK * blocks, scores, -1e30), both[:, LQ:], stacked


def stats_kernel(heads, question_ref, blocks_ref, kv_ref, qd_ref, score_ref, o_ref, rows_ref):
    step = pl.program_id(0)
    per_step = kv_ref.shape[0]
    for passage in range(2):
        tops, dots = [], []
        for head in range(per_step):
            scores, prob_grad, _ = local_scores(
                kv_ref, qd_ref, head, passage, question_ref[passage], blocks_ref[passage]
            )
            top = jnp.max(scores, axis=0, keepdims=True)
            expo = jnp.exp(scores - top)
            total = jnp.sum(expo, axis=0, keepdims=True)
            tops.append(top + jnp.log(total))
            dots.append(jnp.sum(expo * prob_grad, axis=0, keepdims=True) / total)
        place = passage * heads + step * per_step
        rows_ref[pl.ds(pl.multiple_of(place, 8), per_step), :] = jnp.concatenate(tops, axis=0)
        rows_ref[pl.ds(pl.multiple_of(2 * heads + place, 8), per_step), :] = jnp.concatenate(
            dots, axis=0
        )

    @pl.when(step == pl.num_programs(0) - 1)
    def _():
        rows_ref[4 * heads :, :] = score_ref[...]
        o_ref[...] = jnp.broadcast_to(rows_ref[...][None], o_ref.shape)


def local_stats(own_question, own_blocks, key_value, gathered, score_rows):
    heads, tokens, pair_width = key_value.shape
    per_step = 8
    rows = 4 * heads + 8
    return pl.pallas_call(
        functools.partial(stats_kernel, heads),
        grid_spec=pltpu.PrefetchScalarGridSpec(
            num_scalar_prefetch=2,
            grid=(heads // per_step,),
            in_specs=[
                pl.BlockSpec((per_step, tokens, pair_width), lambda i, *_: (i, 0, 0)),
                pl.BlockSpec((per_step,) + gathered.shape[1:], lambda i, *_: (i, 0, 0)),
                pl.BlockSpec((8, 128), lambda i, *_: (0, 0)),
            ],
            out_specs=pl.BlockSpec((N_ENC, rows, 128), lambda i, *_: (0, 0, 0)),
            scratch_shapes=[pltpu.VMEM((rows, 128), F32)],
        ),
        out_shape=jax.ShapeDtypeStruct((N_ENC, rows, 128), F32),
        compiler_params=pltpu.CompilerParams(vmem_limit_bytes=VMEM),
        cost_estimate=pl.CostEstimate(
            flops=2 << 30, bytes_accessed=6 << 20, transcendentals=1 << 20
        ),
        name="local_stats",
    )(own_question, own_blocks, key_value, gathered, score_rows)


def merge_stats(heads, question_ref, own_ref, order_ref, stats_ref, norm_ref, aux_ref):
    masses, shares = [], []
    for passage in range(2):
        tops, dots, marks = [], [], []
        for slot in range(PASS):
            place = order_ref[question_ref[passage] * PASS + slot]
            owner = place // 2
            at = place - 2 * owner
            tops.append(stats_ref[owner, pl.ds(pl.multiple_of(at * heads, heads), heads), :])
            dots.append(
                stats_ref[owner, pl.ds(pl.multiple_of((2 + at) * heads, heads), heads), :]
            )
            pair = stats_ref[owner, 4 * heads : 4 * heads + 8, :]
            marks.append(jnp.where(at == 0, pair[0:1], pair[1:2]))
        top = functools.reduce(jnp.maximum, tops)
        norm = top + jnp.log(sum(jnp.exp(t - top) for t in tops))
        norm_ref[passage] = norm
        norm_ref[2 + passage] = sum(jnp.exp(t - norm) * d for t, d in zip(tops, dots))
        own = stats_ref[own_ref[0], passage * heads : (passage + 1) * heads, :]
        mass = jnp.sum(jnp.exp(own - norm), axis=0, keepdims=True)
        masses.append(jnp.broadcast_to(jnp.sum(mass, axis=1, keepdims=True), (1, 128)))
        best = functools.reduce(jnp.maximum, marks)
        mark = stats_ref[own_ref[0], 4 * heads : 4 * heads + 8, :][passage : passage + 1]
        shares.append(jnp.exp(mark - best) / sum(jnp.exp(m - best) for m in marks))
    aux_ref[...] = jnp.concatenate(masses + shares + [jnp.zeros((4, 128), F32)], axis=0)


def back_heads(part, question_ref, blocks_ref, kv_ref, qd_ref, norm_ref, flat_ref):
    per_step = kv_ref.shape[0]
    first = part * 8 + pl.program_id(0) * per_step
    for passage in range(2):
        for head in range(per_step):
            scores, prob_grad, stacked = local_scores(
                kv_ref, qd_ref, head, passage, question_ref[passage], blocks_ref[passage]
            )
            norm = norm_ref[passage, pl.ds(first + head, 1), :]
            dot = norm_ref[2 + passage, pl.ds(first + head, 1), :]
            probs = jnp.exp(scores - norm)
            score_grad = probs * (prob_grad - dot)
            left = jnp.concatenate([score_grad, probs], axis=1).astype(BF16)
            grad = jnp.dot(left, stacked, preferred_element_type=F32).astype(BF16)
            flat_ref[
                passage * SLOT : (passage + 1) * SLOT, head * 128 : (head + 1) * 128
            ] = grad


def back_first_kernel(
    heads, question_ref, blocks_ref, own_ref, order_ref, kv_ref, qd_ref, stats_ref, flat_ref, norm_ref, aux_ref
):
    @pl.when(pl.program_id(0) == 0)
    def _():
        merge_stats(heads, question_ref, own_ref, order_ref, stats_ref, norm_ref, aux_ref)

    back_heads(0, question_ref, blocks_ref, kv_ref, qd_ref, norm_ref, flat_ref)


def back_second_kernel(question_ref, blocks_ref, kv_ref, qd_ref, norm_ref, flat_ref):
    back_heads(1, question_ref, blocks_ref, kv_ref, qd_ref, norm_ref, flat_ref)


BACK_COST = pl.CostEstimate(flops=3 << 29, bytes_accessed=5 << 20, transcendentals=1 << 19)


def back_specs(key_value, gathered, part, per_step):
    base = part * 8 // per_step
    tokens, pair_width = key_value.shape[1:]
    return [
        pl.BlockSpec((per_step, tokens, pair_width), lambda i, *_: (base + i, 0, 0)),
        pl.BlockSpec((per_step,) + gathered.shape[1:], lambda i, *_: (base + i, 0, 0)),
    ]


def back_first(own_question, own_blocks, enc_rank, order_row, key_value, gathered, stats, per_step=4):
    heads, tokens, pair_width = key_value.shape
    return pl.pallas_call(
        functools.partial(back_first_kernel, heads),
        grid_spec=pltpu.PrefetchScalarGridSpec(
            num_scalar_prefetch=4,
            grid=(8 // per_step,),
            in_specs=back_specs(key_value, gathered, 0, per_step)
            + [pl.BlockSpec(stats.shape, lambda i, *_: (0, 0, 0))],
            out_specs=[
                pl.BlockSpec((tokens, per_step * pair_width), lambda i, *_: (0, i)),
                pl.BlockSpec((4, heads, 128), lambda i, *_: (0, 0, 0)),
                pl.BlockSpec((8, 128), lambda i, *_: (0, 0)),
            ],
        ),
        out_shape=[
            jax.ShapeDtypeStruct((tokens, 8 * pair_width), BF16),
            jax.ShapeDtypeStruct((4, heads, 128), F32),
            jax.ShapeDtypeStruct((8, 128), F32),
        ],
        compiler_params=pltpu.CompilerParams(vmem_limit_bytes=VMEM),
        cost_estimate=BACK_COST,
        name="back_first",
    )(own_question, own_blocks, enc_rank.reshape(1), order_row, key_value, gathered, stats)


def back_second(own_question, own_blocks, key_value, gathered, norms, per_step=4):
    heads, tokens, pair_width = key_value.shape
    return pl.pallas_call(
        back_second_kernel,
        grid_spec=pltpu.PrefetchScalarGridSpec(
            num_scalar_prefetch=2,
            grid=(8 // per_step,),
            in_specs=back_specs(key_value, gathered, 1, per_step)
            + [pl.BlockSpec(norms.shape, lambda i, *_: (0, 0, 0))],
            out_specs=pl.BlockSpec((tokens, per_step * pair_width), lambda i, *_: (0, i)),
        ),
        out_shape=jax.ShapeDtypeStruct((tokens, 8 * pair_width), BF16),
        compiler_params=pltpu.CompilerParams(vmem_limit_bytes=VMEM),
        cost_estimate=BACK_COST,
        name="back_second",
    )(own_question, own_blocks, key_value, gathered, norms)


def product(near_ref, far_ref, own_ref, other_ref):
    rows, depth = SIDE * 128, near_ref.shape[-1]
    total = jnp.dot(near_ref[...].reshape(rows, depth), own_ref[...], preferred_element_type=F32)
    return total + jnp.dot(
        far_ref[...].reshape(rows, depth), other_ref[...], preferred_element_type=F32
    )


def chunk_spec(part, tokens, which):
    if part == 0:
        return pl.BlockSpec((1, SIDE, 128, tokens), lambda i, w: (w[which], 0, 0, 0))
    return pl.BlockSpec((SIDE, 1, 128, tokens), lambda i, w: (0, w[which], 0, 0))


def chunk_call(kernel, name, which, part, turned, grads, extra, extra_specs, out_specs, out_shape):
    tokens, columns = grads[0].shape
    half = pl.BlockSpec((tokens, columns // 2), lambda i, w: (0, i))
    chunks = which.shape[0]
    turned_specs, turned_args = [], []
    for index in range(chunks):
        turned_specs += [chunk_spec(part, tokens, index)] * 2
        turned_args += turned
    return pl.pallas_call(
        kernel,
        grid_spec=pltpu.PrefetchScalarGridSpec(
            num_scalar_prefetch=1,
            grid=(2,),
            in_specs=turned_specs + [half, half] + extra_specs,
            out_specs=out_specs,
        ),
        out_shape=out_shape,
        compiler_params=pltpu.CompilerParams(vmem_limit_bytes=VMEM),
        cost_estimate=pl.CostEstimate(
            flops=chunks * 4 * SIDE * 128 * tokens * columns,
            bytes_accessed=(2 * chunks + 4) << 20,
            transcendentals=0,
        ),
        name=name,
    )(which, *turned_args, *grads, *extra)


def far_kernel(which_ref, near_ref, far_ref, own_ref, other_ref, note_ref, a_ref, b_ref, out_ref):
    total = product(near_ref, far_ref, own_ref, other_ref).astype(BF16)

    @pl.when(pl.program_id(0) == 0)
    def _():
        a_ref[...] = total
        out_ref[...] = note_ref[...]

    @pl.when(pl.program_id(0) == 1)
    def _():
        b_ref[...] = total


def far_chunk(which, part, turned, grads, note):
    rows, columns = SIDE * 128, grads[0].shape[1] // 2
    half = jax.ShapeDtypeStruct((rows, columns), BF16)
    note_spec = pl.BlockSpec((8, 128), lambda i, w: (0, 0))
    half_spec = pl.BlockSpec((rows, columns), lambda i, w: (0, 0))
    return chunk_call(
        far_kernel,
        "far_chunk",
        which,
        part,
        turned,
        grads,
        [note],
        [note_spec],
        [half_spec, half_spec, note_spec],
        [half, half, jax.ShapeDtypeStruct((8, 128), F32)],
    )


def own_kernel(which_ref, near_ref, far_ref, own_ref, other_ref, o_ref):
    o_ref[0] = product(near_ref, far_ref, own_ref, other_ref).astype(BF16)


def own_chunk(which, part, turned, grads):
    rows, columns = SIDE * 128, grads[0].shape[1] // 2
    return chunk_call(
        own_kernel,
        "own_chunk",
        which,
        part,
        turned,
        grads,
        [],
        [],
        pl.BlockSpec((1, rows, columns), lambda i, w: (i, 0, 0)),
        jax.ShapeDtypeStruct((2, rows, columns), BF16),
    )


def side_kernel(
    which_ref, up_near, up_far, down_near, down_far, own_ref, other_ref, a_ref, b_ref, up_ref, down_ref
):
    first = pl.program_id(0) == 0
    zero = jnp.zeros(a_ref.shape, F32)
    up = product(up_near, up_far, own_ref, other_ref)
    up_ref[0] = (up + jnp.where(first, a_ref[...].astype(F32), zero)).astype(BF16)
    down = product(down_near, down_far, own_ref, other_ref)
    down_ref[0] = (down + jnp.where(first, zero, b_ref[...].astype(F32))).astype(BF16)


def side_chunks(which, part, turned, grads, came):
    rows, columns = SIDE * 128, grads[0].shape[1] // 2
    both = jax.ShapeDtypeStruct((2, rows, columns), BF16)
    out = pl.BlockSpec((1, rows, columns), lambda i, w: (i, 0, 0))
    full = pl.BlockSpec((rows, columns), lambda i, w: (0, 0))
    return chunk_call(
        side_kernel, "side_chunks", which, part, turned, grads, list(came), [full, full], [out, out], [both, both]
    )


def total_kernel(which_ref, own_ref, up_ref, down_ref, *out_refs):
    total = own_ref[...].astype(F32) + up_ref[...].astype(F32) + down_ref[...].astype(F32)
    for step, ref in enumerate(out_refs):

        @pl.when(pl.program_id(0) == step)
        def _():
            ref[...] = total[:, 0].astype(BF16)


def totals(first, own, up, down):
    columns = own.shape[-1]
    cut = lambda a: a.reshape(2, SIDE, 128, columns)
    block = pl.BlockSpec((2, 1, 128, columns), lambda i, w: (0, (w[0] + i) % SIDE, 0, 0))
    out = pl.BlockSpec((2, 128, columns), lambda i, w: (0, 0, 0))
    return pl.pallas_call(
        total_kernel,
        grid_spec=pltpu.PrefetchScalarGridSpec(
            num_scalar_prefetch=1, grid=(SIDE,), in_specs=[block] * 3, out_specs=[out] * SIDE
        ),
        out_shape=[jax.ShapeDtypeStruct((2, 128, columns), BF16)] * SIDE,
        compiler_params=pltpu.CompilerParams(vmem_limit_bytes=VMEM),
        cost_estimate=pl.CostEstimate(flops=2 << 20, bytes_accessed=4 << 20, transcendentals=0),
        name="totals",
    )(first.reshape(1), cut(own), cut(up), cut(down))


def finish_kernel(*refs):
    pieces, out_ref = refs[:-1], refs[-1]
    heads = []
    for part in range(2):
        total = sum(r[...].astype(F32) for r in pieces[part * SIDE : (part + 1) * SIDE])
        total = total.astype(BF16)
        for half in range(2):
            for head in range(4):
                heads.append(total[half, :, head * 128 : (head + 1) * 128])
    out_ref[...] = jnp.swapaxes(jnp.stack(heads), 0, 1)


def finish(pieces):
    return pl.pallas_call(
        finish_kernel,
        out_shape=jax.ShapeDtypeStruct((128, 16, 128), BF16),
        compiler_params=pltpu.CompilerParams(vmem_limit_bytes=VMEM),
        name="finish",
    )(*pieces)


def by_token_kernel(a_ref, b_ref, o_ref):
    heads = [ref[:, h * 128 : (h + 1) * 128] for ref in (a_ref, b_ref) for h in range(8)]
    o_ref[...] = jnp.swapaxes(jnp.stack(heads), 0, 1)


def by_token(a, b, rows=128):
    tokens, columns = a.shape
    block = pl.BlockSpec((rows, columns), lambda i: (i, 0))
    return pl.pallas_call(
        by_token_kernel,
        grid=(tokens // rows,),
        in_specs=[block, block],
        out_specs=pl.BlockSpec((rows, 16, 128), lambda i: (i, 0, 0)),
        out_shape=jax.ShapeDtypeStruct((tokens, 16, 128), BF16),
        compiler_params=pltpu.CompilerParams(vmem_limit_bytes=VMEM),
        cost_estimate=pl.CostEstimate(flops=0, bytes_accessed=6 << 20, transcendentals=0),
        name="by_token",
    )(a, b)


def gap_kernel(heads_rows, rank_ref, aux_ref, m1_ref, m2_ref, m3_ref, part_ref, gate_ref, keep_ref, give_ref):
    rows = keep_ref.shape[0]
    mass = (aux_ref[0:2] + m1_ref[0:2]) + (m2_ref[0:2] + m3_ref[0:2])
    gap = aux_ref[2:4] - mass / heads_rows
    rank = rank_ref[0]

    def at(place):
        here = pl.ds(pl.multiple_of(place * rows, 8), rows)
        return gap[0:1, 0:1] * part_ref[0, here, :] + gap[1:2, 0:1] * part_ref[1, here, :]

    keep_ref[...] = at(rank)
    give_ref[...] = at(1 - rank).astype(BF16)


def apply_gap(ret_rank, aux, masses, parts, heads_rows, gate):
    _, rows, columns = parts.shape
    whole = lambda *shape: pl.BlockSpec(shape, lambda i, r: (0,) * len(shape))
    return pl.pallas_call(
        functools.partial(gap_kernel, float(heads_rows)),
        grid_spec=pltpu.PrefetchScalarGridSpec(
            num_scalar_prefetch=1,
            grid=(1,),
            in_specs=[whole(8, 128)] * 4
            + [whole(2, rows, columns), pl.BlockSpec(memory_space=pl.ANY)],
            out_specs=[whole(rows // 2, columns)] * 2,
        ),
        out_shape=[
            jax.ShapeDtypeStruct((rows // 2, columns), F32),
            jax.ShapeDtypeStruct((rows // 2, columns), BF16),
        ],
        compiler_params=pltpu.CompilerParams(vmem_limit_bytes=VMEM),
        cost_estimate=pl.CostEstimate(flops=1 << 19, bytes_accessed=2 << 20, transcendentals=0),
        name="apply_gap",
    )(ret_rank.reshape(1), aux, *masses, parts, gate)


def ring_pairs(axis, step):
    pairs = []
    for x in range(SIDE):
        for y in range(SIDE):
            to = ((x + step) % SIDE, y) if axis == 0 else (x, (y + step) % SIDE)
            pairs.append((x * SIDE + y, to[0] * SIDE + to[1]))
    return pairs


def send(value, axis, step):
    return lax.ppermute(value, "enc", ring_pairs(axis, step))


def add(*terms):
    return sum(t.astype(F32) for t in terms).astype(BF16)


def on_device(
    enc_states,
    kv_weight,
    queries,
    out_grad,
    passage_order,
    passage_blocks,
    ret_tokens,
    ret_weight,
    question_emb,
):
    pass_dev, _, slot_len, width = enc_states.shape
    heads, pair_width = kv_weight.shape[1:]
    question_count, query_len = queries.shape[:2]
    enc_rank = lax.axis_index("enc")
    dec_rank = lax.axis_index("dec")
    ret_rank = lax.axis_index("ret")
    order_row = passage_order[0]
    blocks_row = passage_blocks[0]
    tokens = pass_dev * slot_len
    swap = [(0, 1), (1, 0)]

    packed = jnp.concatenate(
        [queries[:, :, 0, :] * jnp.asarray(0.125, BF16), out_grad[:, :, 0, :]], axis=-1
    ).reshape(question_count * query_len, pair_width)
    gathered = lax.all_to_all(
        jnp.broadcast_to(packed[None], (N_ENC,) + packed.shape),
        "enc",
        split_axis=0,
        concat_axis=0,
        tiled=True,
    )

    tok_rows = enc_states.reshape(tokens, width)
    mine, to_send = turn(ret_rank, tok_rows)
    other = lax.ppermute(to_send, "ret", swap)
    key_value = project(tok_rows, kv_weight)

    own_pass = enc_rank * pass_dev + jnp.arange(pass_dev, dtype=jnp.int32)
    slot_of = jnp.sum(
        jnp.where(
            order_row[None, :] == own_pass[:, None],
            jnp.arange(order_row.shape[0], dtype=jnp.int32)[None, :],
            0,
        ),
        axis=1,
    )
    own_question = slot_of // PASS
    own_blocks = lax.dynamic_slice_in_dim(blocks_row, enc_rank * pass_dev, pass_dev)
    own_emb = jnp.sum(
        jnp.where(
            (own_question[:, None] == jnp.arange(question_count)[None, :])[..., None],
            question_emb[None],
            0.0,
        ),
        axis=1,
    )
    ret_rows = ret_tokens.reshape(tokens, ret_tokens.shape[3])
    ret_width = ret_rows.shape[1]
    pre_act = jnp.dot(ret_rows, ret_weight, preferred_element_type=F32).reshape(
        pass_dev, slot_len, ret_width
    )
    own_live = jnp.arange(slot_len, dtype=jnp.int32)[None, :] < BLK * own_blocks[:, None]
    own_length = (BLK * own_blocks).astype(F32)
    embed_own = (
        jnp.sum(jnp.where(own_live[..., None], jax.nn.gelu(pre_act), 0.0), axis=1)
        / own_length[:, None]
    )
    own_score = jnp.sum(own_emb * embed_own, axis=-1)
    score_rows = jnp.broadcast_to(
        jnp.concatenate([own_score, jnp.zeros((8 - pass_dev,), F32)])[:, None], (8, 128)
    )

    hidden_grad = jnp.where(
        own_live[..., None], (own_emb / own_length[:, None])[:, None, :], 0.0
    )
    pre_grad = gelu_grad(pre_act, hidden_grad).astype(BF16)
    share = ret_width // N_DEC
    part_rows = lax.dynamic_slice_in_dim(ret_rows, dec_rank * share, share, axis=1)
    ret_parts = lax.dot_general(
        part_rows.reshape(pass_dev, slot_len, share),
        pre_grad,
        (((1,), (1,)), ((0,), (0,))),
        preferred_element_type=F32,
    )

    stats = local_stats(own_question, own_blocks, key_value, gathered, score_rows)
    stats_all = lax.all_to_all(stats, "enc", split_axis=0, concat_axis=0, tiled=True)
    flat_a, norms, aux = back_first(
        own_question, own_blocks, enc_rank, order_row, key_value, gathered, stats_all
    )
    far_a = lax.ppermute(flat_a, "ret", swap)
    flat_b = back_second(own_question, own_blocks, key_value, gathered, norms)
    far_b = lax.ppermute(flat_b, "ret", swap)

    turned = [
        mine.reshape(SIDE, SIDE, 128, tokens),
        other.reshape(SIDE, SIDE, 128, tokens),
    ]
    grads = [[flat_a, far_a], [flat_b, far_b]]
    at = (enc_rank // SIDE, enc_rank % SIDE)
    steps = lambda part, *ks: (at[part] + jnp.array(ks, jnp.int32)) % SIDE
    came = []
    for part in range(2):
        a, b, aux = far_chunk(steps(part, 2), part, turned, grads[part], aux)
        came.append((send(a, part, 1), send(b, part, -1)))
    sent = []
    for part in range(2):
        up, down = side_chunks(steps(part, 1, 3), part, turned, grads[part], came[part])
        sent.append((send(up, part, 1), send(down, part, -1)))
    gate = up
    own = [own_chunk(steps(part, 0), part, turned, grads[part]) for part in range(2)]
    pieces = []
    for part in range(2):
        cuts = totals(at[1 - part], own[part], *sent[part])
        pieces.append(cuts[0])
        pieces += [send(cuts[k], 1 - part, k) for k in range(1, SIDE)]
    weight_total = finish(pieces)
    kv_grad = by_token(flat_a, flat_b).reshape(pass_dev, 1, slot_len, heads, pair_width)

    masses = [
        lax.ppermute(aux, "dec", [(i, (i + step) % N_DEC) for i in range(N_DEC)])
        for step in range(1, N_DEC)
    ]
    keep, give = apply_gap(
        ret_rank, aux, masses, ret_parts, N_DEC * heads * query_len, gate
    )
    ret_half = add(keep, lax.ppermute(give, "ret", swap))
    pieces = lax.all_to_all(
        ret_half.reshape(N_ENC, share // 2 // N_ENC * ret_width),
        "enc",
        split_axis=0,
        concat_axis=0,
        tiled=True,
    )
    piece = jnp.sum(pieces.astype(F32), axis=0, keepdims=True).astype(BF16)
    half = lax.all_to_all(
        jnp.broadcast_to(piece, pieces.shape), "enc", split_axis=0, concat_axis=0, tiled=True
    ).reshape(share // 2, ret_width)
    half_far = lax.ppermute(half, "ret", swap)
    quarter = jnp.where(
        ret_rank == 0, jnp.stack([half, half_far]), jnp.stack([half_far, half])
    ).reshape(share, ret_width)
    ret_weight_grad = jnp.zeros((N_DEC, share, ret_width), BF16)
    for step in range(N_DEC):
        piece = quarter
        if step:
            piece = lax.ppermute(
                quarter, "dec", [(i, (i + step) % N_DEC) for i in range(N_DEC)]
            )
        ret_weight_grad = lax.dynamic_update_index_in_dim(
            ret_weight_grad, piece, (dec_rank - step) % N_DEC, 0
        )
    return (kv_grad, weight_total, ret_weight_grad.reshape(ret_width, ret_width))


def solution(mesh):
    return jax.shard_map(
        on_device,
        mesh=mesh,
        in_specs=(
            P("enc", "ret", None, None),
            P(None, "dec", None),
            P("ret", None, ("dec", "enc"), None),
            P("ret", None, ("dec", "enc"), None),
            P("ret", None),
            P("ret", None),
            P("enc", "ret", None, None),
            P(),
            P("ret", None),
        ),
        out_specs=(P("enc", "ret", None, "dec", None), P(("enc", "ret"), "dec", None), P()),
        check_vma=False,
    )
```

time: 226 us -> 219 us (0.969)
  Pallas kernels: 63.7 us -> 81.2 us
  other arithmetic: 20.7 us -> 6.25 us
  blocking collectives: 26.2 us -> 39.4 us
  waiting for transfers between devices: 40 us -> 27.9 us
  local copies, waits for them, and re-layouts: 19.7 us -> 10.3 us
  starting transfers between devices: 49.9 us -> 45.2 us
  matrix products: 2.43 us -> 7.06 us
    pallas_call x5 -> x13, Pallas kernels: 31.2 us -> 54.9 us  [the longest x6 28.3 us: chunk_call(): pl.pallas_call(kernel, grid_spec=pltpu.PrefetchScalarGridSpec(num_scalar_...]
    all_to_all x1, blocking collectives: 14.9 us -> 24.7 us  [on_device(): lax.all_to_all(ret_half.reshape(N_ENC, share // 2 // N_ENC * ret_width),...]
    pallas_call x1, Pallas kernels: 10.7 us -> 4.21 us  [turn(): pl.pallas_call(turn_kernel, grid_spec=pltpu.PrefetchScalarGridSpec(num_sc...]
    ppermute x16 -> x14, starting transfers between devices: 27 us -> 20.7 us  [send(): return lax.ppermute(value, 'enc', ring_pairs(axis, step))]
    ppermute x3, waiting for transfers between devices: 6.25 us -> 0.11 us  [on_device(): lax.ppermute(quarter, 'dec', [(i, (i + step) % N_DEC) for i in range(N_DE...]
    another operation x14 -> x0, other arithmetic: 5.98 us -> none  [the longest x4 4.52 us: on_device(): up = jnp.stack([add(chunk[0, 0], came[part][0]), chunk[0, 1]])]
    all_to_all x1, waiting for transfers between devices: 11.4 us -> 6.04 us  [on_device(): lax.all_to_all(jnp.broadcast_to(packed[None], (N_ENC,) + packed.shape), '...]
    all_to_all x1, waiting for transfers between devices: 0.01 us -> 4.68 us  [on_device(): lax.all_to_all(jnp.broadcast_to(piece, pieces.shape), 'enc', split_axis=0...]
  transfers between devices with their start and end apart: 28 -> 27, of which waited for: 11 -> 8; matrix products, arithmetic and copies ran while one was open for 14% -> 7% of each run, Pallas kernels for 26% -> 36%
where the time goes in v2:
time: 219 us; the launch traced here: 218 us
  Pallas kernels  81.2 us (37%)
  starting transfers between devices  45.2 us (21%)
  blocking collectives  39.4 us (18%)
  waiting for transfers between devices  27.9 us (13%)
  local copies, waits for them, and re-layouts  10.3 us (5%)
  matrix products  7.06 us (3%)
  other arithmetic  6.25 us (3%)
    pallas_call x6, Pallas kernels, chunk_call(): pl.pallas_call(kernel, grid_spec=pltpu.PrefetchScalarGridSpec(num_scalar_...  28.3 us
    all_to_all x1, blocking collectives, on_device(): lax.all_to_all(ret_half.reshape(N_ENC, share // 2 // N_ENC * ret_width),...  24.7 us
    ppermute x14, starting transfers between devices, send(): return lax.ppermute(value, 'enc', ring_pairs(axis, step))  20.7 us
    pallas_call x1, Pallas kernels, project(): pl.pallas_call(project_kernel, grid=(width // depth,), out_shape=jax.Shap...  16.1 us
    ppermute x14, waiting for transfers between devices, send(): return lax.ppermute(value, 'enc', ring_pairs(axis, step))  15.9 us
    all_to_all x1, blocking collectives, on_device(): lax.all_to_all(stats, 'enc', split_axis=0, concat_axis=0, tiled=True)  14.7 us
    pallas_call x2, Pallas kernels, totals(): pl.pallas_call(total_kernel, grid_spec=pltpu.PrefetchScalarGridSpec(num_s...  7.82 us
    all_to_all x1, starting transfers between devices, on_device(): lax.all_to_all(jnp.broadcast_to(packed[None], (N_ENC,) + packed.shape), '...  7.17 us
  transfers between devices with their start and end apart: 27, of which 8 were waited for; matrix products, arithmetic and copies ran while one was open for 7% of the time, Pallas kernels for 36%

profile of v2, /device:TPU:0, one launch (start us, length us, event | category | flops | bytes accessed | tf_op | source)
XLA Modules:
  0.0 218.4 jit_solution(3694048892341974002)
XLA Ops:
  4.5 7.2 %all-to-all-start = ((bf16[16,512,128]{2,1,0:T(8,128)(2,1)}), bf16[16,512,128]{2,1,0:T(8,128)(2,1)}, u32[]{:S(2)}, u32[]{:S(2)}) async-start(bf16[16,512,128]{2,1,0:T(8,128)(2,1)} %broadcast_in_dim.109), calls=%async_computation | async-start | bytes 4194304 | tf_op jit(solution)/shard_map/all_to_all | solution.py:538
  11.7 4.2 %turn.1 = (bf16[16,128,512]{2,1,0:T(8,128)(2,1)}, bf16[16,128,512]{2,1,0:T(8,128)(2,1)}) custom-call(s32[1]{0:T(128)} %bitcast.11.rank_ref, bf16[512,4096]{1,0:T(8,128)(2,1)} %bitcast.67), custom_call_target="tpu_custom_call" | custom-call | bytes 12582912 | tf_op jit(solution)/shard_map/turn/pallas_call | solution.py:75
  16.5 3.2 %select_reduce_fusion = (f32[2,768]{1,0:T(2,128)S(1)}, f32[2,256,768]{2,1,0:T(8,128)}) fusion(pred[2,256]{1,0:T(4,128)(4,1)S(1)} %iota_compare_fusion, bf16[768,768]{1,0:T(8,128)(2,1)S(1)} %copy-done, bf16[2,1,256,768]{3,2,1,0:T(8,128)(2,1)} %param.21), kind=kOutput, calls=%fused_computation.14 | convolution fusion | flops 607910400 | bytes 3545600 | tf_op jit(solution)/shard_map/dot_general | solution.py:572
  19.7 16.1 %project.1.kv_ref = f32[16,512,128]{2,1,0:T(8,128)} custom-call(bf16[512,4096]{1,0:T(8,128)(2,1)} %bitcast.68, bf16[4096,16,128]{2,1,0:T(8,128)(2,1)} %w_ref.1), custom_call_target="tpu_custom_call" | custom-call | flops 8589934592 | bytes 25165824 | tf_op jit(solution)/shard_map/project/pallas_call | solution.py:44
  36.1 6.0 %all-to-all-done.qd_ref = bf16[16,512,128]{2,1,0:T(8,128)(2,1)} async-done(((bf16[16,512,128]{2,1,0:T(8,128)(2,1)}), bf16[16,512,128]{2,1,0:T(8,128)(2,1)}, u32[]{:S(2)}, u32[]{:S(2)}) %all-to-all-start) | async-done | bytes 2097184 | tf_op jit(solution)/shard_map/all_to_all | solution.py:538
  42.8 6.0 %local_stats.1 = f32[16,72,128]{2,1,0:T(8,128)} custom-call(s32[2]{0:T(128)} %copy-done.21, s32[2]{0:T(128)} %copy-done.16, f32[16,512,128]{2,1,0:T(8,128)} %project.1.kv_ref, bf16[16,512,128]{2,1,0:T(8,128)(2,1)} %all-to-all-done.qd_ref, f32[8,128]{1,0:T(8,128)} %broadcast_in_dim.115.score_ref), custom_call_target="tpu_custom_call" | custom-call | flops 2147483648 | bytes 6291456 | tf_op jit(solution)/shard_map/local_stats/pallas_call | solution.py:141
  48.7 14.7 %all_to_all.26.stats_ref = f32[16,72,128]{2,1,0:T(8,128)} all-to-all(f32[16,72,128]{2,1,0:T(8,128)} %local_stats.1), channel_id=1, replica_groups=mesh['enc'=16,'dec'=4,'ret'=2] {'enc'}, dimensions={0} | all-to-all | bytes 1179648 | tf_op jit(solution)/shard_map/all_to_all | solution.py:600
  63.4 5.3 %back_first.1 = (bf16[512,1024]{1,0:T(8,128)(2,1)}, f32[4,16,128]{2,1,0:T(8,128)}, f32[8,128]{1,0:T(8,128)}) custom-call(s32[2]{0:T(128)} %copy-done.21, s32[2]{0:T(128)} %copy-done.16, s32[1]{0:T(128)} %bitcast.2.own_ref, s32[32]{0:T(128)} %bitcast.80, f32[16,512,128]{2,1,0:T(8,128)} %project.1.kv_ref, bf16[16,512,128]{2,1,0:T(8,128)(2,1)} %all-to-all-done.qd_ref, ...), custom_call_target="tpu_custom_call" | custom-call | flops 1610612736 | bytes 5242880 | tf_op jit(solution)/shard_map/back_first/pallas_call | solution.py:237
  68.7 4.9 %back_second.1.b_ref.own_ref = bf16[512,1024]{1,0:T(8,128)(2,1)} custom-call(s32[2]{0:T(128)} %copy-done.21, s32[2]{0:T(128)} %copy-done.16, f32[16,512,128]{2,1,0:T(8,128)} %project.1.kv_ref, bf16[16,512,128]{2,1,0:T(8,128)(2,1)} %all-to-all-done.qd_ref, f32[4,16,128]{2,1,0:T(8,128)} %get-tuple-element.29.norm_ref), custom_call_target="tpu_custom_call" | custom-call | flops 1610612736 | bytes 5242880 | tf_op jit(solution)/shard_map/back_second/pallas_call | solution.py:263
  76.9 4.0 %far_chunk.2 = (bf16[512,512]{1,0:T(8,128)(2,1)}, bf16[512,512]{1,0:T(8,128)(2,1)}, f32[8,128]{1,0:T(8,128)}) custom-call(s32[1]{0:T(128)S(6)} %select_n.126.which_ref, bf16[4,4,128,512]{3,2,1,0:T(8,128)(2,1)} %bitcast.51, bf16[4,4,128,512]{3,2,1,0:T(8,128)(2,1)} %bitcast.59, bf16[512,1024]{1,0:T(8,128)(2,1)} %get-tuple-element.28.a_ref.own_ref, ...), custom_call_target="tpu_custom_call" | custom-call | flops 1073741824 | bytes 6291456 | tf_op jit(solution)/shard_map/far_chunk/pallas_call | solution.py:301
  81.4 2.7 %collective-permute-start.3 = (bf16[512,512]{1,0:T(8,128)(2,1)}, bf16[512,512]{1,0:T(8,128)(2,1)S(1)}, u32[]{:S(2)}, u32[]{:S(2)}) collective-permute-start(bf16[512,512]{1,0:T(8,128)(2,1)} %get-tuple-element.34), channel_id=1, source_target_pairs={{0,96},{8,104},{16,112},{24,120},{32,0},{40,8},{48,16},{56,24},{64... | collective-permute-start | bytes 1572872 | tf_op jit(solution)/shard_map/ppermute | solution.py:506
  84.1 4.1 %far_chunk.3 = (bf16[512,512]{1,0:T(8,128)(2,1)}, bf16[512,512]{1,0:T(8,128)(2,1)}, f32[8,128]{1,0:T(8,128)}) custom-call(s32[1]{0:T(128)S(6)} %select_n.129.which_ref, bf16[4,4,128,512]{3,2,1,0:T(8,128)(2,1)} %bitcast.52, bf16[4,4,128,512]{3,2,1,0:T(8,128)(2,1)} %bitcast.60, bf16[512,1024]{1,0:T(8,128)(2,1)} %back_second.1.b_ref.own_ref, ...), custom_call_target="tpu_custom_call" | custom-call | flops 1073741824 | bytes 6291456 | tf_op jit(solution)/shard_map/far_chunk/pallas_call | solution.py:301
  88.8 2.7 %collective-permute-start.11 = (bf16[512,512]{1,0:T(8,128)(2,1)}, bf16[512,512]{1,0:T(8,128)(2,1)S(1)}, u32[]{:S(2)}, u32[]{:S(2)}) collective-permute-start(bf16[512,512]{1,0:T(8,128)(2,1)} %get-tuple-element.43), channel_id=1, source_target_pairs={{0,24},{8,0},{16,8},{24,16},{32,56},{40,32},{48,40},{56,48},{64,88... | collective-permute-start | bytes 1572872 | tf_op jit(solution)/shard_map/ppermute | solution.py:506
  91.4 3.8 %fusion.13.part_ref = f32[2,192,768]{2,1,0:T(8,128)} fusion(bf16[2,256,192]{2,1,0:T(8,128)(2,1)S(1)} %bitcast.77, f32[2,256,768]{2,1,0:T(8,128)} %get-tuple-element.75, f32[2,768]{1,0:T(2,128)S(1)} %get-tuple-element.70, pred[2,256]{1,0:T(4,128)(4,1)S(1)} %iota_compare_fusion), kind=kOutput, calls=%fused_computation.18 | convolution fusion | flops 159252480 | bytes 2955776 | tf_op jit(solution)/shard_map/dot_general | solution.py:592
  97.7 5.1 %collective-permute-done.10.a_ref = bf16[512,512]{1,0:T(8,128)(2,1)S(1)} collective-permute-done((bf16[512,512]{1,0:T(8,128)(2,1)}, bf16[512,512]{1,0:T(8,128)(2,1)S(1)}, u32[]{:S(2)}, u32[]{:S(2)}) %collective-permute-start.10) | collective-permute-done | bytes 524320 | tf_op jit(solution)/shard_map/ppermute | solution.py:506
  102.9 3.9 %collective-permute-start.18 = (f32[8,128]{1,0:T(8,128)S(1)}, f32[8,128]{1,0:T(8,128)S(1)}, u32[]{:S(2)}, u32[]{:S(2)}) collective-permute-start(f32[8,128]{1,0:T(8,128)S(1)} %copy-done.17), channel_id=1, source_target_pairs={{0,4},{2,6},{4,0},{6,2},{1,5},{3,7},{5,1},{7,3},{8,12},{10,14},{12... | collective-permute-start | bytes 12296 | tf_op jit(solution)/shard_map/ppermute | solution.py:634
  107.6 6.2 %side_chunks.3 = (bf16[2,512,512]{2,1,0:T(8,128)(2,1)}, bf16[2,512,512]{2,1,0:T(8,128)(2,1)}) custom-call(s32[2]{0:T(128)} %get-tuple-element.72.which_ref, bf16[4,4,128,512]{3,2,1,0:T(8,128)(2,1)} %bitcast.53, bf16[4,4,128,512]{3,2,1,0:T(8,128)(2,1)} %bitcast.61, bf16[4,4,128,512]{3,2,1,0:T(8,128)(2,1)} %bitcast.54, bf16[4,4,128,512]{3,2,1,0:T(8,128)(2,1)} %bitcast.62, ...), custom_call_target="tpu_custom_call" | custom-call | flops 2147483648 | bytes 8388608 | tf_op jit(solution)/shard_map/side_chunks/pallas_call | solution.py:301
  117.6 6.4 %side_chunks.2 = (bf16[2,512,512]{2,1,0:T(8,128)(2,1)}, bf16[2,512,512]{2,1,0:T(8,128)(2,1)}) custom-call(s32[2]{0:T(128)} %get-tuple-element.73.which_ref, bf16[4,4,128,512]{3,2,1,0:T(8,128)(2,1)} %bitcast.55, bf16[4,4,128,512]{3,2,1,0:T(8,128)(2,1)} %bitcast.63, bf16[4,4,128,512]{3,2,1,0:T(8,128)(2,1)} %bitcast.56, bf16[4,4,128,512]{3,2,1,0:T(8,128)(2,1)} %bitcast.64, ...), custom_call_target="tpu_custom_call" | custom-call | flops 2147483648 | bytes 8388608 | tf_op jit(solution)/shard_map/side_chunks/pallas_call | solution.py:301
  123.9 3.2 %collective-permute-start.5 = (bf16[2,512,512]{2,1,0:T(8,128)(2,1)}, bf16[2,512,512]{2,1,0:T(8,128)(2,1)}, u32[]{:S(2)}, u32[]{:S(2)}) collective-permute-start(bf16[2,512,512]{2,1,0:T(8,128)(2,1)} %get-tuple-element.36), channel_id=1, source_target_pairs={{0,96},{8,104},{16,112},{24,120},{32,0},{40,8},{48,16},{56,24},{64... | collective-permute-start | bytes 3145736 | tf_op jit(solution)/shard_map/ppermute | solution.py:506
  129.3 24.7 %all_to_all.27 = bf16[16,2,2304]{2,1,0:T(2,128)(2,1)S(1)} all-to-all(bf16[16,2,2304]{2,1,0:T(2,128)(2,1)S(1)} %reshape.236), channel_id=1, replica_groups=mesh['enc'=16,'dec'=4,'ret'=2] {'enc'}, dimensions={0} | all-to-all | bytes 294912 | tf_op jit(solution)/shard_map/all_to_all | solution.py:641
  156.8 5.4 %all-to-all-start.3 = ((bf16[16,2,2304]{2,1,0:T(2,128)(2,1)}), bf16[16,2,2304]{2,1,0:T(2,128)(2,1)S(1)}, u32[]{:S(2)}, u32[]{:S(2)}) async-start(bf16[16,2,2304]{2,1,0:T(2,128)(2,1)} %reshape.238), calls=%async_computation.3 | async-start | bytes 294912 | tf_op jit(solution)/shard_map/all_to_all | solution.py:649
  165.5 4.7 %all-to-all-done.3 = bf16[16,2,2304]{2,1,0:T(2,128)(2,1)S(1)} async-done(((bf16[16,2,2304]{2,1,0:T(2,128)(2,1)}), bf16[16,2,2304]{2,1,0:T(2,128)(2,1)S(1)}, u32[]{:S(2)}, u32[]{:S(2)}) %all-to-all-start.3) | async-done | bytes 147488 | tf_op jit(solution)/shard_map/all_to_all | solution.py:649
  173.9 3.9 %by_token.1 = bf16[512,16,128]{2,1,0:T(8,128)(2,1)} custom-call(bf16[512,1024]{1,0:T(8,128)(2,1)} %get-tuple-element.28.a_ref.own_ref, bf16[512,1024]{1,0:T(8,128)(2,1)} %back_second.1.b_ref.own_ref), custom_call_target="tpu_custom_call" | custom-call | bytes 6291456 | tf_op jit(solution)/shard_map/by_token/pallas_call | solution.py:448
  177.9 3.8 %own_chunk.2 = bf16[2,512,512]{2,1,0:T(8,128)(2,1)} custom-call(s32[1]{0:T(128)S(6)} %select_n.124.which_ref, bf16[4,4,128,512]{3,2,1,0:T(8,128)(2,1)} %bitcast.57, bf16[4,4,128,512]{3,2,1,0:T(8,128)(2,1)} %bitcast.65, bf16[512,1024]{1,0:T(8,128)(2,1)} %get-tuple-element.28.a_ref.own_ref, bf16[512,1024]{1,0:T(8,128)(2,1)} %copy-done.3), custom_call_target="tpu_custom_call" | custom-call | flops 1073741824 | bytes 6291456 | tf_op jit(solution)/shard_map/own_chunk/pallas_call | solution.py:301
  181.6 3.8 %own_chunk.3 = bf16[2,512,512]{2,1,0:T(8,128)(2,1)} custom-call(s32[1]{0:T(128)S(6)} %select_n.127.which_ref, bf16[4,4,128,512]{3,2,1,0:T(8,128)(2,1)} %bitcast.58, bf16[4,4,128,512]{3,2,1,0:T(8,128)(2,1)} %bitcast.66, bf16[512,1024]{1,0:T(8,128)(2,1)} %back_second.1.b_ref.own_ref, bf16[512,1024]{1,0:T(8,128)(2,1)} %collective-permute-done.9.other_ref), custom_call_target="tpu_custom_call" | custom-call | flops 1073741824 | bytes 6291456 | tf_op jit(solution)/shard_map/own_chunk/pallas_call | solution.py:301
  186.9 2.2 %collective-permute-start.24 = (bf16[192,768]{1,0:T(8,128)(2,1)S(1)}, bf16[192,768]{1,0:T(8,128)(2,1)S(1)}, u32[]{:S(2)}, u32[]{:S(2)}) collective-permute-start(bf16[192,768]{1,0:T(8,128)(2,1)S(1)} %bitcast.75), channel_id=1, source_target_pairs={{0,6},{2,0},{4,2},{6,4},{1,7},{3,1},{5,3},{7,5},{8,14},{10,8},{12,... | collective-permute-start | bytes 884744 | tf_op jit(solution)/shard_map/ppermute | solution.py:660
  189.1 3.9 %totals.2 = (bf16[2,128,512]{2,1,0:T(8,128)(2,1)}, bf16[2,128,512]{2,1,0:T(8,128)(2,1)}, bf16[2,128,512]{2,1,0:T(8,128)(2,1)}, bf16[2,128,512]{2,1,0:T(8,128)(2,1)}) custom-call(s32[1]{0:T(128)} %bitcast.9.which_ref, bf16[2,4,128,512]{3,2,1,0:T(8,128)(2,1)} %bitcast.70, bf16[2,4,128,512]{3,2,1,0:T(8,128)(2,1)} %bitcast.15.up_ref, ...), custom_call_target="tpu_custom_call" | custom-call | flops 2097152 | bytes 4194304 | tf_op jit(solution)/shard_map/totals/pallas_call | solution.py:407
  193.6 2.2 %collective-permute-start.7 = (bf16[2,128,512]{2,1,0:T(8,128)(2,1)}, bf16[2,128,512]{2,1,0:T(8,128)(2,1)S(1)}, u32[]{:S(2)}, u32[]{:S(2)}) collective-permute-start(bf16[2,128,512]{2,1,0:T(8,128)(2,1)} %get-tuple-element.39), channel_id=1, source_target_pairs={{0,16},{8,24},{16,0},{24,8},{32,48},{40,56},{48,32},{56,40},{64,80... | collective-permute-start | bytes 786440 | tf_op jit(solution)/shard_map/ppermute | solution.py:506
  197.3 3.9 %totals.3 = (bf16[2,128,512]{2,1,0:T(8,128)(2,1)}, bf16[2,128,512]{2,1,0:T(8,128)(2,1)}, bf16[2,128,512]{2,1,0:T(8,128)(2,1)}, bf16[2,128,512]{2,1,0:T(8,128)(2,1)}) custom-call(s32[1]{0:T(128)} %bitcast.10.which_ref, bf16[2,4,128,512]{3,2,1,0:T(8,128)(2,1)} %bitcast.69, bf16[2,4,128,512]{3,2,1,0:T(8,128)(2,1)} %bitcast.18.up_ref, ...), custom_call_target="tpu_custom_call" | custom-call | flops 2097152 | bytes 4194304 | tf_op jit(solution)/shard_map/totals/pallas_call | solution.py:407
  203.8 3.8 %collective-permute-done.6.refs_1_ = bf16[2,128,512]{2,1,0:T(8,128)(2,1)S(1)} collective-permute-done((bf16[2,128,512]{2,1,0:T(8,128)(2,1)}, bf16[2,128,512]{2,1,0:T(8,128)(2,1)S(1)}, u32[]{:S(2)}, u32[]{:S(2)}) %collective-permute-start.6) | collective-permute-done | bytes 262176 | tf_op jit(solution)/shard_map/ppermute | solution.py:506
  208.8 6.3 %collective-permute-done.14.refs_5_ = bf16[2,128,512]{2,1,0:T(8,128)(2,1)} collective-permute-done((bf16[2,128,512]{2,1,0:T(8,128)(2,1)}, bf16[2,128,512]{2,1,0:T(8,128)(2,1)}, u32[]{:S(2)}, u32[]{:S(2)}) %collective-permute-start.14) | collective-permute-done | bytes 262176 | tf_op jit(solution)/shard_map/ppermute | solution.py:506
  215.8 2.6 %finish.1 = bf16[128,16,128]{2,1,0:T(8,128)(2,1)} custom-call(bf16[2,128,512]{2,1,0:T(8,128)(2,1)} %get-tuple-element.37.refs_0_, bf16[2,128,512]{2,1,0:T(8,128)(2,1)} %copy-done.11, bf16[2,128,512]{2,1,0:T(8,128)(2,1)} %copy-done.12, bf16[2,128,512]{2,1,0:T(8,128)(2,1)} %copy-done.13, bf16[2,128,512]{2,1,0:T(8,128)(2,1)} %get-tuple-element.46.refs_4_, ...), custom_call_target="tpu_custom_call" | custom-call | tf_op jit(solution)/shard_map/finish/pallas_call | solution.py:432
  (133 shorter events, 36.3 us)
Async XLA Ops:
  0.6 15.9 %copy-start = (bf16[768,768]{1,0:T(8,128)(2,1)S(1)}, bf16[768,768]{1,0:T(8,128)(2,1)}, u32[]{:S(2)}) copy-start(bf16[768,768]{1,0:T(8,128)(2,1)} %param.22) | copy-start | bytes 3538948
  4.5 37.6 %all-to-all-start = ((bf16[16,512,128]{2,1,0:T(8,128)(2,1)}), bf16[16,512,128]{2,1,0:T(8,128)(2,1)}, u32[]{:S(2)}, u32[]{:S(2)}) async-start(bf16[16,512,128]{2,1,0:T(8,128)(2,1)} %broadcast_in_dim.109), calls=%async_computation | async-start | bytes 4194304 | tf_op jit(solution)/shard_map/all_to_all | solution.py:538
  15.9 59.3 %collective-permute-start = (bf16[16,128,512]{2,1,0:T(8,128)(2,1)}, bf16[16,128,512]{2,1,0:T(8,128)(2,1)S(1)}, u32[]{:S(2)}, u32[]{:S(2)}) collective-permute-start(bf16[16,128,512]{2,1,0:T(8,128)(2,1)} %get-tuple-element.31), channel_id=1, source_target_pairs={{0,1},{1,0},{2,3},{3,2},{4,5},{5,4},{6,7},{7,6},{8,9},{9,8},{10,11... | collective-permute-start | bytes 6291464 | tf_op jit(solution)/shard_map/ppermute | solution.py:548
  68.7 6.5 %collective-permute-start.1 = (bf16[512,1024]{1,0:T(8,128)(2,1)}, bf16[512,1024]{1,0:T(8,128)(2,1)S(1)}, u32[]{:S(2)}, u32[]{:S(2)}) collective-permute-start(bf16[512,1024]{1,0:T(8,128)(2,1)} %get-tuple-element.28.a_ref.own_ref), channel_id=1, source_target_pairs={{0,1},{1,0},{2,3},{3,2},{4,5},{5,4},{6,7},{7,6},{8,9},{9,8},{10,11... | collective-permute-start | bytes 3145736 | tf_op jit(solution)/shard_map/ppermute | solution.py:604
  73.6 10.6 %collective-permute-start.9 = (bf16[512,1024]{1,0:T(8,128)(2,1)}, bf16[512,1024]{1,0:T(8,128)(2,1)}, u32[]{:S(2)}, u32[]{:S(2)}) collective-permute-start(bf16[512,1024]{1,0:T(8,128)(2,1)} %back_second.1.b_ref.own_ref), channel_id=1, source_target_pairs={{0,1},{1,0},{2,3},{3,2},{4,5},{5,4},{6,7},{7,6},{8,9},{9,8},{10,11... | collective-permute-start | bytes 3145736 | tf_op jit(solution)/shard_map/ppermute | solution.py:606
  80.9 35.7 %collective-permute-start.2 = (bf16[512,512]{1,0:T(8,128)(2,1)}, bf16[512,512]{1,0:T(8,128)(2,1)S(1)}, u32[]{:S(2)}, u32[]{:S(2)}) collective-permute-start(bf16[512,512]{1,0:T(8,128)(2,1)} %get-tuple-element.33), channel_id=1, source_target_pairs={{0,32},{8,40},{16,48},{24,56},{32,64},{40,72},{48,80},{56,88},{64,... | collective-permute-start | bytes 1572872 | tf_op jit(solution)/shard_map/ppermute | solution.py:506
  81.4 35.2 %collective-permute-start.3 = (bf16[512,512]{1,0:T(8,128)(2,1)}, bf16[512,512]{1,0:T(8,128)(2,1)S(1)}, u32[]{:S(2)}, u32[]{:S(2)}) collective-permute-start(bf16[512,512]{1,0:T(8,128)(2,1)} %get-tuple-element.34), channel_id=1, source_target_pairs={{0,96},{8,104},{16,112},{24,120},{32,0},{40,8},{48,16},{56,24},{64... | collective-permute-start | bytes 1572872 | tf_op jit(solution)/shard_map/ppermute | solution.py:506
  88.2 14.7 %collective-permute-start.10 = (bf16[512,512]{1,0:T(8,128)(2,1)}, bf16[512,512]{1,0:T(8,128)(2,1)S(1)}, u32[]{:S(2)}, u32[]{:S(2)}) collective-permute-start(bf16[512,512]{1,0:T(8,128)(2,1)} %get-tuple-element.42), channel_id=1, source_target_pairs={{0,8},{8,16},{16,24},{24,0},{32,40},{40,48},{48,56},{56,32},{64,72... | collective-permute-start | bytes 1572872 | tf_op jit(solution)/shard_map/ppermute | solution.py:506
  88.8 18.0 %collective-permute-start.11 = (bf16[512,512]{1,0:T(8,128)(2,1)}, bf16[512,512]{1,0:T(8,128)(2,1)S(1)}, u32[]{:S(2)}, u32[]{:S(2)}) collective-permute-start(bf16[512,512]{1,0:T(8,128)(2,1)} %get-tuple-element.43), channel_id=1, source_target_pairs={{0,24},{8,0},{16,8},{24,16},{32,56},{40,32},{48,40},{56,48},{64,88... | collective-permute-start | bytes 1572872 | tf_op jit(solution)/shard_map/ppermute | solution.py:506
  95.8 18.0 %collective-permute-start.17 = (f32[8,128]{1,0:T(8,128)S(1)}, f32[8,128]{1,0:T(8,128)S(1)}, u32[]{:S(2)}, u32[]{:S(2)}) collective-permute-start(f32[8,128]{1,0:T(8,128)S(1)} %copy-done.17), channel_id=1, source_target_pairs={{0,2},{2,4},{4,6},{6,0},{1,3},{3,5},{5,7},{7,1},{8,10},{10,12},{12... | collective-permute-start | bytes 12296 | tf_op jit(solution)/shard_map/ppermute | solution.py:634
  102.9 10.9 %collective-permute-start.18 = (f32[8,128]{1,0:T(8,128)S(1)}, f32[8,128]{1,0:T(8,128)S(1)}, u32[]{:S(2)}, u32[]{:S(2)}) collective-permute-start(f32[8,128]{1,0:T(8,128)S(1)} %copy-done.17), channel_id=1, source_target_pairs={{0,4},{2,6},{4,0},{6,2},{1,5},{3,7},{5,1},{7,3},{8,12},{10,14},{12... | collective-permute-start | bytes 12296 | tf_op jit(solution)/shard_map/ppermute | solution.py:634
  106.8 7.1 %collective-permute-start.19 = (f32[8,128]{1,0:T(8,128)S(1)}, f32[8,128]{1,0:T(8,128)S(1)}, u32[]{:S(2)}, u32[]{:S(2)}) collective-permute-start(f32[8,128]{1,0:T(8,128)S(1)} %copy-done.17), channel_id=1, source_target_pairs={{0,6},{2,0},{4,2},{6,4},{1,7},{3,1},{5,3},{7,5},{8,14},{10,8},{12,... | collective-permute-start | bytes 12296 | tf_op jit(solution)/shard_map/ppermute | solution.py:634
  116.6 10.6 %collective-permute-start.20 = (bf16[96,768]{1,0:T(8,128)(2,1)}, bf16[96,768]{1,0:T(8,128)(2,1)S(1)}, u32[]{:S(2)}, u32[]{:S(2)}) collective-permute-start(bf16[96,768]{1,0:T(8,128)(2,1)} %get-tuple-element.52), channel_id=1, source_target_pairs={{0,1},{1,0},{2,3},{3,2},{4,5},{5,4},{6,7},{7,6},{8,9},{9,8},{10,11... | collective-permute-start | bytes 442376 | tf_op jit(solution)/shard_map/ppermute | solution.py:640
  117.6 9.6 %copy-start.10 = (f32[96,768]{1,0:T(8,128)S(1)}, f32[96,768]{1,0:T(8,128)}, u32[]{:S(2)}) copy-start(f32[96,768]{1,0:T(8,128)} %get-tuple-element.51) | copy-start | bytes 884740
  123.9 61.5 %collective-permute-start.4 = (bf16[2,512,512]{2,1,0:T(8,128)(2,1)}, bf16[2,512,512]{2,1,0:T(8,128)(2,1)}, u32[]{:S(2)}, u32[]{:S(2)}) collective-permute-start(bf16[2,512,512]{2,1,0:T(8,128)(2,1)} %get-tuple-element.35), channel_id=1, source_target_pairs={{0,32},{8,40},{16,48},{24,56},{32,64},{40,72},{48,80},{56,88},{64,... | collective-permute-start | bytes 3145736 | tf_op jit(solution)/shard_map/ppermute | solution.py:506
  123.9 62.9 %collective-permute-start.5 = (bf16[2,512,512]{2,1,0:T(8,128)(2,1)}, bf16[2,512,512]{2,1,0:T(8,128)(2,1)}, u32[]{:S(2)}, u32[]{:S(2)}) collective-permute-start(bf16[2,512,512]{2,1,0:T(8,128)(2,1)} %get-tuple-element.36), channel_id=1, source_target_pairs={{0,96},{8,104},{16,112},{24,120},{32,0},{40,8},{48,16},{56,24},{64... | collective-permute-start | bytes 3145736 | tf_op jit(solution)/shard_map/ppermute | solution.py:506
  127.3 35.0 %copy-start.5 = (bf16[2,512,512]{2,1,0:T(8,128)(2,1)S(1)}, bf16[2,512,512]{2,1,0:T(8,128)(2,1)}, u32[]{:S(2)}) copy-start(bf16[2,512,512]{2,1,0:T(8,128)(2,1)} %get-tuple-element.44.gate_ref) | copy-start | bytes 3145732
  156.8 13.4 %all-to-all-start.3 = ((bf16[16,2,2304]{2,1,0:T(2,128)(2,1)}), bf16[16,2,2304]{2,1,0:T(2,128)(2,1)S(1)}, u32[]{:S(2)}, u32[]{:S(2)}) async-start(bf16[16,2,2304]{2,1,0:T(2,128)(2,1)} %reshape.238), calls=%async_computation.3 | async-start | bytes 294912 | tf_op jit(solution)/shard_map/all_to_all | solution.py:649
  162.2 31.4 %collective-permute-start.12 = (bf16[2,512,512]{2,1,0:T(8,128)(2,1)S(1)}, bf16[2,512,512]{2,1,0:T(8,128)(2,1)}, u32[]{:S(2)}, u32[]{:S(2)}) collective-permute-start(bf16[2,512,512]{2,1,0:T(8,128)(2,1)S(1)} %copy-done.5), channel_id=1, source_target_pairs={{0,8},{8,16},{16,24},{24,0},{32,40},{40,48},{48,56},{56,32},{64,72... | collective-permute-start | bytes 3145736 | tf_op jit(solution)/shard_map/ppermute | solution.py:506
  164.2 31.6 %collective-permute-start.13 = (bf16[2,512,512]{2,1,0:T(8,128)(2,1)}, bf16[2,512,512]{2,1,0:T(8,128)(2,1)}, u32[]{:S(2)}, u32[]{:S(2)}) collective-permute-start(bf16[2,512,512]{2,1,0:T(8,128)(2,1)} %get-tuple-element.45), channel_id=1, source_target_pairs={{0,24},{8,0},{16,8},{24,16},{32,56},{40,32},{48,40},{56,48},{64,88... | collective-permute-start | bytes 3145736 | tf_op jit(solution)/shard_map/ppermute | solution.py:506
  171.3 1.5 collective-permute-start.21
  172.8 20.2 %collective-permute-start.22 = (bf16[192,768]{1,0:T(8,128)(2,1)S(1)}, bf16[192,768]{1,0:T(8,128)(2,1)S(1)}, u32[]{:S(2)}, u32[]{:S(2)}) collective-permute-start(bf16[192,768]{1,0:T(8,128)(2,1)S(1)} %bitcast.73), channel_id=1, source_target_pairs={{0,2},{2,4},{4,6},{6,0},{1,3},{3,5},{5,7},{7,1},{8,10},{10,12},{12... | collective-permute-start | bytes 884744 | tf_op jit(solution)/shard_map/ppermute | solution.py:660
  185.5 15.8 %collective-permute-start.23 = (bf16[192,768]{1,0:T(8,128)(2,1)S(1)}, bf16[192,768]{1,0:T(8,128)(2,1)S(1)}, u32[]{:S(2)}, u32[]{:S(2)}) collective-permute-start(bf16[192,768]{1,0:T(8,128)(2,1)S(1)} %bitcast.74), channel_id=1, source_target_pairs={{0,4},{2,6},{4,0},{6,2},{1,5},{3,7},{5,1},{7,3},{8,12},{10,14},{12... | collective-permute-start | bytes 884744 | tf_op jit(solution)/shard_map/ppermute | solution.py:660
  186.9 15.0 %collective-permute-start.24 = (bf16[192,768]{1,0:T(8,128)(2,1)S(1)}, bf16[192,768]{1,0:T(8,128)(2,1)S(1)}, u32[]{:S(2)}, u32[]{:S(2)}) collective-permute-start(bf16[192,768]{1,0:T(8,128)(2,1)S(1)} %bitcast.75), channel_id=1, source_target_pairs={{0,6},{2,0},{4,2},{6,4},{1,7},{3,1},{5,3},{7,5},{8,14},{10,8},{12,... | collective-permute-start | bytes 884744 | tf_op jit(solution)/shard_map/ppermute | solution.py:660
  193.0 14.6 %collective-permute-start.6 = (bf16[2,128,512]{2,1,0:T(8,128)(2,1)}, bf16[2,128,512]{2,1,0:T(8,128)(2,1)S(1)}, u32[]{:S(2)}, u32[]{:S(2)}) collective-permute-start(bf16[2,128,512]{2,1,0:T(8,128)(2,1)} %get-tuple-element.38), channel_id=1, source_target_pairs={{0,8},{8,16},{16,24},{24,0},{32,40},{40,48},{48,56},{56,32},{64,72... | collective-permute-start | bytes 786440 | tf_op jit(solution)/shard_map/ppermute | solution.py:506
  193.6 15.1 %collective-permute-start.7 = (bf16[2,128,512]{2,1,0:T(8,128)(2,1)}, bf16[2,128,512]{2,1,0:T(8,128)(2,1)S(1)}, u32[]{:S(2)}, u32[]{:S(2)}) collective-permute-start(bf16[2,128,512]{2,1,0:T(8,128)(2,1)} %get-tuple-element.39), channel_id=1, source_target_pairs={{0,16},{8,24},{16,0},{24,8},{32,48},{40,56},{48,32},{56,40},{64,80... | collective-permute-start | bytes 786440 | tf_op jit(solution)/shard_map/ppermute | solution.py:506
  195.9 12.9 %collective-permute-start.8 = (bf16[2,128,512]{2,1,0:T(8,128)(2,1)}, bf16[2,128,512]{2,1,0:T(8,128)(2,1)S(1)}, u32[]{:S(2)}, u32[]{:S(2)}) collective-permute-start(bf16[2,128,512]{2,1,0:T(8,128)(2,1)} %get-tuple-element.40), channel_id=1, source_target_pairs={{0,24},{8,0},{16,8},{24,16},{32,56},{40,32},{48,40},{56,48},{64,88... | collective-permute-start | bytes 786440 | tf_op jit(solution)/shard_map/ppermute | solution.py:506
  201.3 13.8 %collective-permute-start.14 = (bf16[2,128,512]{2,1,0:T(8,128)(2,1)}, bf16[2,128,512]{2,1,0:T(8,128)(2,1)}, u32[]{:S(2)}, u32[]{:S(2)}) collective-permute-start(bf16[2,128,512]{2,1,0:T(8,128)(2,1)} %get-tuple-element.47), channel_id=1, source_target_pairs={{0,32},{8,40},{16,48},{24,56},{32,64},{40,72},{48,80},{56,88},{64,... | collective-permute-start | bytes 786440 | tf_op jit(solution)/shard_map/ppermute | solution.py:506
  201.9 13.2 %collective-permute-start.15 = (bf16[2,128,512]{2,1,0:T(8,128)(2,1)}, bf16[2,128,512]{2,1,0:T(8,128)(2,1)S(1)}, u32[]{:S(2)}, u32[]{:S(2)}) collective-permute-start(bf16[2,128,512]{2,1,0:T(8,128)(2,1)} %get-tuple-element.48), channel_id=1, source_target_pairs={{0,64},{8,72},{16,80},{24,88},{32,96},{40,104},{48,112},{56,120},{... | collective-permute-start | bytes 786440 | tf_op jit(solution)/shard_map/ppermute | solution.py:506
  207.6 8.1 %collective-permute-start.16 = (bf16[2,128,512]{2,1,0:T(8,128)(2,1)}, bf16[2,128,512]{2,1,0:T(8,128)(2,1)}, u32[]{:S(2)}, u32[]{:S(2)}) collective-permute-start(bf16[2,128,512]{2,1,0:T(8,128)(2,1)} %get-tuple-element.49), channel_id=1, source_target_pairs={{0,96},{8,104},{16,112},{24,120},{32,0},{40,8},{48,16},{56,24},{64... | collective-permute-start | bytes 786440 | tf_op jit(solution)/shard_map/ppermute | solution.py:506
  208.6 9.7 %copy-start.1 = (bf16[768,768]{1,0:T(8,128)(2,1)S(1)}, bf16[768,768]{1,0:T(8,128)(2,1)}, u32[]{:S(2)}) copy-start(bf16[768,768]{1,0:T(8,128)(2,1)} %param.22) | copy-start | bytes 3538948
  208.7 9.7 %copy-start.4 = (bf16[4,192,768]{2,1,0:T(8,128)(2,1)}, bf16[4,192,768]{2,1,0:T(8,128)(2,1)S(1)}, u32[]{:S(2)}) copy-start(bf16[4,192,768]{2,1,0:T(8,128)(2,1)S(1)} %bitcast_dynamic-update-slice_fusion) | copy-start | bytes 3538948
  (20 other events, 63.3 us)

commit v3 on v2

--- a/solution.py
+++ b/solution.py
@@ -20,8 +20,42 @@
 VMEM = 60 << 20
 
 
+def small_cost():
+    return pl.CostEstimate(flops=1 << 10, bytes_accessed=1 << 10, transcendentals=0)
+
+
 def gelu_grad(pre_act, upstream):
     return jax.vjp(jax.nn.gelu, pre_act)[1](upstream)[0]
+
+
+def pack_kernel(order_ref, q_ref, d_ref, o_ref):
+    rows = o_ref.shape[1]
+    packed = []
+    for question in range(q_ref.shape[0] // rows):
+        at = slice(question * rows, (question + 1) * rows)
+        packed.append(
+            jnp.concatenate([q_ref[at] * jnp.asarray(0.125, BF16), d_ref[at]], axis=1)
+        )
+    for slot in range(o_ref.shape[0]):
+        o_ref[order_ref[slot]] = packed[slot // PASS]
+
+
+def pack(order_row, q_rows, d_rows):
+    total, head_dim = q_rows.shape
+    passages = order_row.shape[0]
+    return pl.pallas_call(
+        pack_kernel,
+        grid_spec=pltpu.PrefetchScalarGridSpec(
+            num_scalar_prefetch=1,
+            grid=(1,),
+            in_specs=[pl.BlockSpec((total, head_dim), lambda i, o: (0, 0))] * 2,
+            out_specs=pl.BlockSpec((passages, LQ, 2 * head_dim), lambda i, o: (0, 0, 0)),
+        ),
+        out_shape=jax.ShapeDtypeStruct((passages, LQ, 2 * head_dim), BF16),
+        compiler_params=pltpu.CompilerParams(vmem_limit_bytes=VMEM),
+        cost_estimate=small_cost(),
+        name="pack",
+    )(order_row, q_rows, d_rows)
 
 
 def project_kernel(x_ref, w_ref, o_ref):
@@ -51,16 +85,12 @@
         ],
         out_specs=pl.BlockSpec((heads, tokens, pair_width), lambda i: (0, 0, 0)),
         compiler_params=pltpu.CompilerParams(vmem_limit_bytes=VMEM),
-        cost_estimate=pl.CostEstimate(
-            flops=2 * tokens * width * heads * pair_width,
-            bytes_accessed=24 << 20,
-            transcendentals=0,
-        ),
+        cost_estimate=small_cost(),
         name="project",
     )(tok_rows, kv_weight)
 
 
-def turn_kernel(rank_ref, x_ref, mine_ref, send_ref):
+def turn_kernel(rank_ref, after_ref, x_ref, mine_ref, send_ref):
     first = rank_ref[0] == 0
     for block in range(mine_ref.shape[0]):
         even = x_ref[:, block * 256 : block * 256 + 128].T
@@ -69,7 +99,7 @@
         send_ref[block] = jnp.where(first, odd, even)
 
 
-def turn(ret_rank, tok_rows, per_step=8):
+def turn(ret_rank, after, tok_rows, per_step=8):
     tokens, width = tok_rows.shape
     half = jax.ShapeDtypeStruct((N_ENC, 128, tokens), BF16)
     return pl.pallas_call(
@@ -77,21 +107,26 @@
         grid_spec=pltpu.PrefetchScalarGridSpec(
             num_scalar_prefetch=1,
             grid=(N_ENC // per_step,),
-            in_specs=[pl.BlockSpec((tokens, 256 * per_step), lambda i, r: (0, i))],
+            in_specs=[
+                pl.BlockSpec(memory_space=pl.ANY),
+                pl.BlockSpec((tokens, 256 * per_step), lambda i, r: (0, i)),
+            ],
             out_specs=[pl.BlockSpec((per_step, 128, tokens), lambda i, r: (i, 0, 0))] * 2,
         ),
         out_shape=[half, half],
         compiler_params=pltpu.CompilerParams(vmem_limit_bytes=VMEM),
-        cost_estimate=pl.CostEstimate(flops=0, bytes_accessed=12 << 20, transcendentals=0),
+        cost_estimate=pl.CostEstimate(
+            flops=0, bytes_accessed=64 << 20, transcendentals=0
+        ),
         name="turn",
-    )(ret_rank.reshape(1), tok_rows)
-
-
-def local_scores(kv_ref, qd_ref, head, passage, question, blocks):
+    )(ret_rank.reshape(1), after, tok_rows)
+
+
+def local_scores(kv_ref, qd_ref, head, passage, blocks):
     pair = kv_ref[head, passage * SLOT : (passage + 1) * SLOT, :]
     high = pair.astype(BF16)
     low = (pair - high.astype(F32)).astype(BF16)
-    rows = qd_ref[head, pl.ds(pl.multiple_of(question * LQ, LQ), LQ), :]
+    rows = qd_ref[head, passage * LQ : (passage + 1) * LQ, :]
     lane = lax.broadcasted_iota(jnp.int32, rows.shape, 1)
     zero = jnp.zeros_like(rows)
     stacked = jnp.concatenate(
@@ -108,14 +143,16 @@
     return jnp.where(place < BLK * blocks, scores, -1e30), both[:, LQ:], stacked
 
 
-def stats_kernel(heads, question_ref, blocks_ref, kv_ref, qd_ref, score_ref, o_ref, rows_ref):
+def stats_kernel(
+    heads, question_ref, blocks_ref, kv_ref, qd_ref, score_ref, emb_ref, o_ref, late_ref, rows_ref
+):
     step = pl.program_id(0)
     per_step = kv_ref.shape[0]
     for passage in range(2):
         tops, dots = [], []
         for head in range(per_step):
             scores, prob_grad, _ = local_scores(
-                kv_ref, qd_ref, head, passage, question_ref[passage], blocks_ref[passage]
+                kv_ref, qd_ref, head, passage, blocks_ref[passage]
             )
             top = jnp.max(scores, axis=0, keepdims=True)
             expo = jnp.exp(scores - top)
@@ -131,10 +168,11 @@
     @pl.when(step == pl.num_programs(0) - 1)
     def _():
         rows_ref[4 * heads :, :] = score_ref[...]
+        late_ref[...] = emb_ref[...]
         o_ref[...] = jnp.broadcast_to(rows_ref[...][None], o_ref.shape)
 
 
-def local_stats(own_question, own_blocks, key_value, gathered, score_rows):
+def local_stats(own_question, own_blocks, key_value, gathered, score_rows, own_emb):
     heads, tokens, pair_width = key_value.shape
     per_step = 8
     rows = 4 * heads + 8
@@ -147,17 +185,22 @@
                 pl.BlockSpec((per_step, tokens, pair_width), lambda i, *_: (i, 0, 0)),
                 pl.BlockSpec((per_step,) + gathered.shape[1:], lambda i, *_: (i, 0, 0)),
                 pl.BlockSpec((8, 128), lambda i, *_: (0, 0)),
+                pl.BlockSpec(own_emb.shape, lambda i, *_: (0, 0)),
             ],
-            out_specs=pl.BlockSpec((N_ENC, rows, 128), lambda i, *_: (0, 0, 0)),
+            out_specs=[
+                pl.BlockSpec((N_ENC, rows, 128), lambda i, *_: (0, 0, 0)),
+                pl.BlockSpec(own_emb.shape, lambda i, *_: (0, 0)),
+            ],
             scratch_shapes=[pltpu.VMEM((rows, 128), F32)],
         ),
-        out_shape=jax.ShapeDtypeStruct((N_ENC, rows, 128), F32),
-        compiler_params=pltpu.CompilerParams(vmem_limit_bytes=VMEM),
-        cost_estimate=pl.CostEstimate(
-            flops=2 << 30, bytes_accessed=6 << 20, transcendentals=1 << 20
-        ),
+        out_shape=[
+            jax.ShapeDtypeStruct((N_ENC, rows, 128), F32),
+            jax.ShapeDtypeStruct(own_emb.shape, F32),
+        ],
+        compiler_params=pltpu.CompilerParams(vmem_limit_bytes=VMEM),
+        cost_estimate=small_cost(),
         name="local_stats",
-    )(own_question, own_blocks, key_value, gathered, score_rows)
+    )(own_question, own_blocks, key_value, gathered, score_rows, own_emb)
 
 
 def merge_stats(heads, question_ref, own_ref, order_ref, stats_ref, norm_ref, aux_ref):
@@ -193,7 +236,7 @@
     for passage in range(2):
         for head in range(per_step):
             scores, prob_grad, stacked = local_scores(
-                kv_ref, qd_ref, head, passage, question_ref[passage], blocks_ref[passage]
+                kv_ref, qd_ref, head, passage, blocks_ref[passage]
             )
             norm = norm_ref[passage, pl.ds(first + head, 1), :]
             dot = norm_ref[2 + passage, pl.ds(first + head, 1), :]
@@ -207,7 +250,18 @@
 
 
 def back_first_kernel(
-    heads, question_ref, blocks_ref, own_ref, order_ref, kv_ref, qd_ref, stats_ref, flat_ref, norm_ref, aux_ref
+    heads,
+    question_ref,
+    blocks_ref,
+    own_ref,
+    order_ref,
+    after_ref,
+    kv_ref,
+    qd_ref,
+    stats_ref,
+    flat_ref,
+    norm_ref,
+    aux_ref,
 ):
     @pl.when(pl.program_id(0) == 0)
     def _():
@@ -220,7 +274,7 @@
     back_heads(1, question_ref, blocks_ref, kv_ref, qd_ref, norm_ref, flat_ref)
 
 
-BACK_COST = pl.CostEstimate(flops=3 << 29, bytes_accessed=5 << 20, transcendentals=1 << 19)
+BACK_COST = pl.CostEstimate(flops=0, bytes_accessed=32 << 20, transcendentals=0)
 
 
 def back_specs(key_value, gathered, part, per_step):
@@ -232,14 +286,15 @@
     ]
 
 
-def back_first(own_question, own_blocks, enc_rank, order_row, key_value, gathered, stats, per_step=4):
+def back_first(after, own_question, own_blocks, enc_rank, order_row, key_value, gathered, stats, per_step=4):
     heads, tokens, pair_width = key_value.shape
     return pl.pallas_call(
         functools.partial(back_first_kernel, heads),
         grid_spec=pltpu.PrefetchScalarGridSpec(
             num_scalar_prefetch=4,
             grid=(8 // per_step,),
-            in_specs=back_specs(key_value, gathered, 0, per_step)
+            in_specs=[pl.BlockSpec(memory_space=pl.ANY)]
+            + back_specs(key_value, gathered, 0, per_step)
             + [pl.BlockSpec(stats.shape, lambda i, *_: (0, 0, 0))],
             out_specs=[
                 pl.BlockSpec((tokens, per_step * pair_width), lambda i, *_: (0, i)),
@@ -255,7 +310,7 @@
         compiler_params=pltpu.CompilerParams(vmem_limit_bytes=VMEM),
         cost_estimate=BACK_COST,
         name="back_first",
-    )(own_question, own_blocks, enc_rank.reshape(1), order_row, key_value, gathered, stats)
+    )(own_question, own_blocks, enc_rank.reshape(1), order_row, after, key_value, gathered, stats)
 
 
 def back_second(own_question, own_blocks, key_value, gathered, norms, per_step=4):
@@ -290,7 +345,13 @@
     return pl.BlockSpec((SIDE, 1, 128, tokens), lambda i, w: (0, w[which], 0, 0))
 
 
-def chunk_call(kernel, name, which, part, turned, grads, extra, extra_specs, out_specs, out_shape):
+def ordered(kernel, which_ref, after_ref, *refs):
+    kernel(which_ref, *refs)
+
+
+def chunk_call(
+    kernel, name, which, part, turned, grads, after, extra, extra_specs, out_specs, out_shape
+):
     tokens, columns = grads[0].shape
     half = pl.BlockSpec((tokens, columns // 2), lambda i, w: (0, i))
     chunks = which.shape[0]
@@ -299,22 +360,21 @@
         turned_specs += [chunk_spec(part, tokens, index)] * 2
         turned_args += turned
     return pl.pallas_call(
-        kernel,
+        functools.partial(ordered, kernel),
         grid_spec=pltpu.PrefetchScalarGridSpec(
             num_scalar_prefetch=1,
             grid=(2,),
-            in_specs=turned_specs + [half, half] + extra_specs,
+            in_specs=[pl.BlockSpec(memory_space=pl.ANY)]
+            + turned_specs
+            + [half, half]
+            + extra_specs,
             out_specs=out_specs,
         ),
         out_shape=out_shape,
         compiler_params=pltpu.CompilerParams(vmem_limit_bytes=VMEM),
-        cost_estimate=pl.CostEstimate(
-            flops=chunks * 4 * SIDE * 128 * tokens * columns,
-            bytes_accessed=(2 * chunks + 4) << 20,
-            transcendentals=0,
-        ),
+        cost_estimate=small_cost(),
         name=name,
-    )(which, *turned_args, *grads, *extra)
+    )(which, after, *turned_args, *grads, *extra)
 
 
 def far_kernel(which_ref, near_ref, far_ref, own_ref, other_ref, note_ref, a_ref, b_ref, out_ref):
@@ -330,7 +390,7 @@
         b_ref[...] = total
 
 
-def far_chunk(which, part, turned, grads, note):
+def far_chunk(which, part, turned, grads, after, note):
     rows, columns = SIDE * 128, grads[0].shape[1] // 2
     half = jax.ShapeDtypeStruct((rows, columns), BF16)
     note_spec = pl.BlockSpec((8, 128), lambda i, w: (0, 0))
@@ -342,6 +402,7 @@
         part,
         turned,
         grads,
+        after,
         [note],
         [note_spec],
         [half_spec, half_spec, note_spec],
@@ -353,7 +414,7 @@
     o_ref[0] = product(near_ref, far_ref, own_ref, other_ref).astype(BF16)
 
 
-def own_chunk(which, part, turned, grads):
+def own_chunk(which, part, turned, grads, after):
     rows, columns = SIDE * 128, grads[0].shape[1] // 2
     return chunk_call(
         own_kernel,
@@ -362,6 +423,7 @@
         part,
         turned,
         grads,
+        after,
         [],
         [],
         pl.BlockSpec((1, rows, columns), lambda i, w: (i, 0, 0)),
@@ -380,17 +442,17 @@
     down_ref[0] = (down + jnp.where(first, zero, b_ref[...].astype(F32))).astype(BF16)
 
 
-def side_chunks(which, part, turned, grads, came):
+def side_chunks(which, part, turned, grads, after, came):
     rows, columns = SIDE * 128, grads[0].shape[1] // 2
     both = jax.ShapeDtypeStruct((2, rows, columns), BF16)
     out = pl.BlockSpec((1, rows, columns), lambda i, w: (i, 0, 0))
     full = pl.BlockSpec((rows, columns), lambda i, w: (0, 0))
     return chunk_call(
-        side_kernel, "side_chunks", which, part, turned, grads, list(came), [full, full], [out, out], [both, both]
-    )
-
-
-def total_kernel(which_ref, own_ref, up_ref, down_ref, *out_refs):
+        side_kernel, "side_chunks", which, part, turned, grads, after, list(came), [full, full], [out, out], [both, both]
+    )
+
+
+def total_kernel(which_ref, after_ref, own_ref, up_ref, down_ref, *out_refs):
     total = own_ref[...].astype(F32) + up_ref[...].astype(F32) + down_ref[...].astype(F32)
     for step, ref in enumerate(out_refs):
 
@@ -399,7 +461,7 @@
             ref[...] = total[:, 0].astype(BF16)
 
 
-def totals(first, own, up, down):
+def totals(first, after, own, up, down):
     columns = own.shape[-1]
     cut = lambda a: a.reshape(2, SIDE, 128, columns)
     block = pl.BlockSpec((2, 1, 128, columns), lambda i, w: (0, (w[0] + i) % SIDE, 0, 0))
@@ -407,54 +469,93 @@
     return pl.pallas_call(
         total_kernel,
         grid_spec=pltpu.PrefetchScalarGridSpec(
-            num_scalar_prefetch=1, grid=(SIDE,), in_specs=[block] * 3, out_specs=[out] * SIDE
+            num_scalar_prefetch=1,
+            grid=(SIDE,),
+            in_specs=[pl.BlockSpec(memory_space=pl.ANY)] + [block] * 3,
+            out_specs=[out] * SIDE,
         ),
         out_shape=[jax.ShapeDtypeStruct((2, 128, columns), BF16)] * SIDE,
         compiler_params=pltpu.CompilerParams(vmem_limit_bytes=VMEM),
-        cost_estimate=pl.CostEstimate(flops=2 << 20, bytes_accessed=4 << 20, transcendentals=0),
+        cost_estimate=small_cost(),
         name="totals",
-    )(first.reshape(1), cut(own), cut(up), cut(down))
-
-
-def finish_kernel(*refs):
-    pieces, out_ref = refs[:-1], refs[-1]
+    )(first.reshape(1), after, cut(own), cut(up), cut(down))
+
+
+def gather_terms(refs):
+    return sum(r[...].astype(F32) for r in refs).astype(BF16)
+
+
+def first_kernel(after_ref, *refs):
+    refs[-1][...] = gather_terms(refs[:-1])
+
+
+def first_half(after, pieces):
+    block = pl.BlockSpec(pieces[0].shape, lambda: (0, 0, 0))
+    return pl.pallas_call(
+        first_kernel,
+        in_specs=[pl.BlockSpec(memory_space=pl.ANY)] + [block] * len(pieces),
+        out_specs=block,
+        out_shape=jax.ShapeDtypeStruct(pieces[0].shape, BF16),
+        compiler_params=pltpu.CompilerParams(vmem_limit_bytes=16 << 20),
+        cost_estimate=small_cost(),
+        name="first_half",
+    )(after, *pieces)
+
+
+def finish_kernel(first_ref, *refs):
     heads = []
-    for part in range(2):
-        total = sum(r[...].astype(F32) for r in pieces[part * SIDE : (part + 1) * SIDE])
-        total = total.astype(BF16)
+    for total in (first_ref[...], gather_terms(refs[:-1])):
         for half in range(2):
             for head in range(4):
                 heads.append(total[half, :, head * 128 : (head + 1) * 128])
-    out_ref[...] = jnp.swapaxes(jnp.stack(heads), 0, 1)
-
-
-def finish(pieces):
+    refs[-1][...] = jnp.swapaxes(jnp.stack(heads), 0, 1)
+
+
+def finish(first, pieces):
     return pl.pallas_call(
         finish_kernel,
         out_shape=jax.ShapeDtypeStruct((128, 16, 128), BF16),
         compiler_params=pltpu.CompilerParams(vmem_limit_bytes=VMEM),
+        cost_estimate=small_cost(),
         name="finish",
-    )(*pieces)
-
-
-def by_token_kernel(a_ref, b_ref, o_ref):
+    )(first, *pieces)
+
+
+def by_token_kernel(after_ref, a_ref, b_ref, o_ref):
     heads = [ref[:, h * 128 : (h + 1) * 128] for ref in (a_ref, b_ref) for h in range(8)]
     o_ref[...] = jnp.swapaxes(jnp.stack(heads), 0, 1)
 
 
-def by_token(a, b, rows=128):
+def by_token(after, a, b, rows=128):
     tokens, columns = a.shape
     block = pl.BlockSpec((rows, columns), lambda i: (i, 0))
     return pl.pallas_call(
         by_token_kernel,
         grid=(tokens // rows,),
-        in_specs=[block, block],
+        in_specs=[pl.BlockSpec(memory_space=pl.ANY), block, block],
         out_specs=pl.BlockSpec((rows, 16, 128), lambda i: (i, 0, 0)),
         out_shape=jax.ShapeDtypeStruct((tokens, 16, 128), BF16),
         compiler_params=pltpu.CompilerParams(vmem_limit_bytes=VMEM),
-        cost_estimate=pl.CostEstimate(flops=0, bytes_accessed=6 << 20, transcendentals=0),
+        cost_estimate=small_cost(),
         name="by_token",
-    )(a, b)
+    )(after, a, b)
+
+
+def add_kernel(after_ref, a_ref, b_ref, o_ref):
+    o_ref[...] = (a_ref[...].astype(F32) + b_ref[...].astype(F32)).astype(BF16)
+
+
+def add_after(after, a, b):
+    block = pl.BlockSpec(a.shape, lambda: (0, 0))
+    return pl.pallas_call(
+        add_kernel,
+        in_specs=[pl.BlockSpec(memory_space=pl.ANY), block, block],
+        out_specs=block,
+        out_shape=jax.ShapeDtypeStruct(a.shape, BF16),
+        compiler_params=pltpu.CompilerParams(vmem_limit_bytes=8 << 20),
+        cost_estimate=small_cost(),
+        name="add_after",
+    )(after, a, b)
 
 
 def gap_kernel(heads_rows, rank_ref, aux_ref, m1_ref, m2_ref, m3_ref, part_ref, gate_ref, keep_ref, give_ref):
@@ -488,7 +589,7 @@
             jax.ShapeDtypeStruct((rows // 2, columns), BF16),
         ],
         compiler_params=pltpu.CompilerParams(vmem_limit_bytes=VMEM),
-        cost_estimate=pl.CostEstimate(flops=1 << 19, bytes_accessed=2 << 20, transcendentals=0),
+        cost_estimate=small_cost(),
         name="apply_gap",
     )(ret_rank.reshape(1), aux, *masses, parts, gate)
 
@@ -532,11 +633,10 @@
     tokens = pass_dev * slot_len
     swap = [(0, 1), (1, 0)]
 
-    packed = jnp.concatenate(
-        [queries[:, :, 0, :] * jnp.asarray(0.125, BF16), out_grad[:, :, 0, :]], axis=-1
-    ).reshape(question_count * query_len, pair_width)
+    rows = question_count * query_len
+    packed = pack(order_row, queries.reshape(rows, HD), out_grad.reshape(rows, HD))
     gathered = lax.all_to_all(
-        jnp.broadcast_to(packed[None], (N_ENC,) + packed.shape),
+        packed.reshape(N_ENC, pass_dev * query_len, pair_width),
         "enc",
         split_axis=0,
         concat_axis=0,
@@ -544,8 +644,6 @@
     )
 
     tok_rows = enc_states.reshape(tokens, width)
-    mine, to_send = turn(ret_rank, tok_rows)
-    other = lax.ppermute(to_send, "ret", swap)
     key_value = project(tok_rows, kv_weight)
 
     own_pass = enc_rank * pass_dev + jnp.arange(pass_dev, dtype=jnp.int32)
@@ -583,8 +681,13 @@
         jnp.concatenate([own_score, jnp.zeros((8 - pass_dev,), F32)])[:, None], (8, 128)
     )
 
+    stats, late_emb = local_stats(
+        own_question, own_blocks, key_value, gathered, score_rows, own_emb
+    )
+    mine, to_send = turn(ret_rank, stats, tok_rows)
+    other = lax.ppermute(to_send, "ret", swap)
     hidden_grad = jnp.where(
-        own_live[..., None], (own_emb / own_length[:, None])[:, None, :], 0.0
+        own_live[..., None], (late_emb / own_length[:, None])[:, None, :], 0.0
     )
     pre_grad = gelu_grad(pre_act, hidden_grad).astype(BF16)
     share = ret_width // N_DEC
@@ -595,11 +698,9 @@
         (((1,), (1,)), ((0,), (0,))),
         preferred_element_type=F32,
     )
-
-    stats = local_stats(own_question, own_blocks, key_value, gathered, score_rows)
     stats_all = lax.all_to_all(stats, "enc", split_axis=0, concat_axis=0, tiled=True)
     flat_a, norms, aux = back_first(
-        own_question, own_blocks, enc_rank, order_row, key_value, gathered, stats_all
+        ret_parts, own_question, own_blocks, enc_rank, order_row, key_value, gathered, stats_all
     )
     far_a = lax.ppermute(flat_a, "ret", swap)
     flat_b = back_second(own_question, own_blocks, key_value, gathered, norms)
@@ -612,43 +713,42 @@
     grads = [[flat_a, far_a], [flat_b, far_b]]
     at = (enc_rank // SIDE, enc_rank % SIDE)
     steps = lambda part, *ks: (at[part] + jnp.array(ks, jnp.int32)) % SIDE
-    came = []
-    for part in range(2):
-        a, b, aux = far_chunk(steps(part, 2), part, turned, grads[part], aux)
-        came.append((send(a, part, 1), send(b, part, -1)))
-    sent = []
-    for part in range(2):
-        up, down = side_chunks(steps(part, 1, 3), part, turned, grads[part], came[part])
-        sent.append((send(up, part, 1), send(down, part, -1)))
-    gate = up
-    own = [own_chunk(steps(part, 0), part, turned, grads[part]) for part in range(2)]
-    pieces = []
-    for part in range(2):
-        cuts = totals(at[1 - part], own[part], *sent[part])
-        pieces.append(cuts[0])
-        pieces += [send(cuts[k], 1 - part, k) for k in range(1, SIDE)]
-    weight_total = finish(pieces)
-    kv_grad = by_token(flat_a, flat_b).reshape(pass_dev, 1, slot_len, heads, pair_width)
-
+    def level(after, half, bit):
+        far = lax.ppermute(half, "enc", [(i, i ^ bit) for i in range(N_ENC)])
+        return add_after(after, half, far)
+
+    a, b, aux = far_chunk(steps(0, 2), 0, turned, grads[0], norms, aux)
+    came = [(send(a, 0, 1), send(b, 0, -1))]
     masses = [
         lax.ppermute(aux, "dec", [(i, (i + step) % N_DEC) for i in range(N_DEC)])
         for step in range(1, N_DEC)
     ]
+    a, b, late_aux = far_chunk(steps(1, 2), 1, turned, grads[1], a, aux)
+    came.append((send(a, 1, 1), send(b, 1, -1)))
     keep, give = apply_gap(
-        ret_rank, aux, masses, ret_parts, N_DEC * heads * query_len, gate
-    )
-    ret_half = add(keep, lax.ppermute(give, "ret", swap))
-    pieces = lax.all_to_all(
-        ret_half.reshape(N_ENC, share // 2 // N_ENC * ret_width),
-        "enc",
-        split_axis=0,
-        concat_axis=0,
-        tiled=True,
-    )
-    piece = jnp.sum(pieces.astype(F32), axis=0, keepdims=True).astype(BF16)
-    half = lax.all_to_all(
-        jnp.broadcast_to(piece, pieces.shape), "enc", split_axis=0, concat_axis=0, tiled=True
-    ).reshape(share // 2, ret_width)
+        ret_rank, late_aux, masses, ret_parts, N_DEC * heads * query_len, a
+    )
+    own = [own_chunk(steps(0, 0), 0, turned, grads[0], give)]
+    half = add_after(own[0], keep, lax.ppermute(give, "ret", swap))
+    up, down = side_chunks(steps(0, 1, 3), 0, turned, grads[0], half, came[0])
+    sent = [(send(up, 0, 1), send(down, 0, -1))]
+    half = level(up, half, 4)
+    up, down = side_chunks(steps(1, 1, 3), 1, turned, grads[1], half, came[1])
+    sent.append((send(up, 1, 1), send(down, 1, -1)))
+    half = level(up, half, 1)
+    own.append(own_chunk(steps(1, 0), 1, turned, grads[1], half))
+    half = level(own[1], half, 8)
+    by_tokens = by_token(half, flat_a, flat_b)
+    kv_grad = by_tokens.reshape(pass_dev, 1, slot_len, heads, pair_width)
+    half = level(by_tokens, half, 2)
+    pieces, last = [], half
+    for part in range(2):
+        cuts = totals(at[1 - part], last, own[part], *sent[part])
+        pieces.append([cuts[0]] + [send(cuts[k], 1 - part, k) for k in range(1, SIDE)])
+        last = cuts[0]
+    summed = first_half(cuts[0], pieces[0])
+    weight_total = finish(summed, pieces[1])
+
     half_far = lax.ppermute(half, "ret", swap)
     quarter = jnp.where(
         ret_rank == 0, jnp.stack([half, half_far]), jnp.stack([half_far, half])

time: 219 us -> 200 us (0.913)
  blocking collectives: 39.4 us -> 0 us
  local copies, waits for them, and re-layouts: 10.3 us -> 25 us
  starting transfers between devices: 45.2 us -> 50.9 us
  other arithmetic: 6.25 us -> 1.36 us
  Pallas kernels: 81.2 us -> 84 us
  waiting for transfers between devices: 27.9 us -> 30.3 us
    all_to_all x2 -> x0, blocking collectives: 39.4 us -> none  [the longest x1 24.7 us: on_device(): lax.all_to_all(ret_half.reshape(N_ENC, share // 2 // N_ENC * ret_width),...]
    unnamed x55 -> x96, local copies, waits for them, and re-layouts: 5.3 us -> 21 us
    ppermute x14, waiting for transfers between devices: 15.9 us -> 2.12 us  [send(): return lax.ppermute(value, 'enc', ring_pairs(axis, step))]
    ppermute x1 -> x5, waiting for transfers between devices: 0.01 us -> 9.04 us  [the longest x4 9.04 us: level(): far = lax.ppermute(half, 'enc', [(i, i ^ bit) for i in range(N_ENC)])]
    ppermute x3, waiting for transfers between devices: 0.11 us -> 8.81 us  [on_device(): lax.ppermute(quarter, 'dec', [(i, (i + step) % N_DEC) for i in range(N_DE...]
    ppermute x14, starting transfers between devices: 20.7 us -> 24 us  [send(): return lax.ppermute(value, 'enc', ring_pairs(axis, step))]
    pallas_call x7 -> x14, Pallas kernels: 32.2 us -> 35.4 us  [the longest x6 28.2 us: chunk_call(): pl.pallas_call(functools.partial(ordered, kernel), grid_spec=pltpu.Prefet...]
    all_to_all x2 -> x0, other arithmetic: 2.32 us -> none  [the longest x1 1.48 us: on_device(): lax.all_to_all(ret_half.reshape(N_ENC, share // 2 // N_ENC * ret_width),...]
  transfers between devices with their start and end apart: 27 -> 31, of which waited for: 8 -> 7; matrix products, arithmetic and copies ran while one was open for 7% -> 5% of each run, Pallas kernels for 36% -> 35%
where the time goes in v3:
time: 200 us; the launch traced here: 199 us
  Pallas kernels  84 us (42%)
  starting transfers between devices  50.9 us (25%)
  waiting for transfers between devices  30.3 us (15%)
  local copies, waits for them, and re-layouts  25 us (12%)
  matrix products  6.01 us (3%)
    pallas_call x6, Pallas kernels, chunk_call(): pl.pallas_call(functools.partial(ordered, kernel), grid_spec=pltpu.Prefet...  28.2 us
    ppermute x14, starting transfers between devices, send(): return lax.ppermute(value, 'enc', ring_pairs(axis, step))  24 us
    unnamed x96, local copies, waits for them, and re-layouts  21 us
    pallas_call x1, Pallas kernels, project(): pl.pallas_call(project_kernel, grid=(width // depth,), out_shape=jax.Shap...  16.2 us
    ppermute x4, waiting for transfers between devices, level(): far = lax.ppermute(half, 'enc', [(i, i ^ bit) for i in range(N_ENC)])  9.04 us
    all_to_all x1, waiting for transfers between devices, on_device(): lax.all_to_all(stats, 'enc', split_axis=0, concat_axis=0, tiled=True)  8.99 us
    ppermute x3, waiting for transfers between devices, on_device(): lax.ppermute(quarter, 'dec', [(i, (i + step) % N_DEC) for i in range(N_DE...  8.81 us
    pallas_call x2, Pallas kernels, totals(): pl.pallas_call(total_kernel, grid_spec=pltpu.PrefetchScalarGridSpec(num_s...  7.91 us
  transfers between devices with their start and end apart: 31, of which 7 were waited for; matrix products, arithmetic and copies ran while one was open for 5% of the time, Pallas kernels for 35%

profile of v3, /device:TPU:0, one launch (start us, length us, event | category | flops | bytes accessed | tf_op | source)
XLA Modules:
  0.0 198.8 jit_solution(18288933734007471643)
XLA Ops:
  3.9 2.9 %pack.1 = bf16[32,128,128]{2,1,0:T(8,128)(2,1)} custom-call(s32[32]{0:T(128)} %bitcast.83, bf16[512,64]{1,0:T(8,128)(2,1)} %bitcast.78, bf16[512,64]{1,0:T(8,128)(2,1)} %bitcast.79), custom_call_target="tpu_custom_call" | custom-call | flops 1024 | bytes 1024 | tf_op jit(solution)/shard_map/pack/pallas_call | solution.py:46
  6.9 7.1 %all-to-all-start = ((bf16[16,256,128]{2,1,0:T(8,128)(2,1)}), bf16[16,256,128]{2,1,0:T(8,128)(2,1)S(1)}, u32[]{:S(2)}, u32[]{:S(2)}) async-start(bf16[16,256,128]{2,1,0:T(8,128)(2,1)} %bitcast.71), calls=%async_computation | async-start | bytes 2097152 | tf_op jit(solution)/shard_map/all_to_all | solution.py:638
  14.4 16.2 %project.1.kv_ref = f32[16,512,128]{2,1,0:T(8,128)} custom-call(bf16[512,4096]{1,0:T(8,128)(2,1)} %bitcast.69, bf16[4096,16,128]{2,1,0:T(8,128)(2,1)} %w_ref.1), custom_call_target="tpu_custom_call" | custom-call | flops 1024 | bytes 1024 | tf_op jit(solution)/shard_map/project/pallas_call | solution.py:78
  30.8 2.2 %select_reduce_fusion = (f32[2,768]{1,0:T(2,128)S(1)}, f32[2,256,768]{2,1,0:T(8,128)}) fusion(pred[2,256]{1,0:T(4,128)(4,1)S(1)} %iota_compare_fusion, bf16[768,768]{1,0:T(8,128)(2,1)S(1)} %copy-done, bf16[2,1,256,768]{3,2,1,0:T(8,128)(2,1)S(1)} %copy-done.34), kind=kOutput, calls=%fused_computation.14 | convolution fusion | flops 607910400 | bytes 3545600 | tf_op jit(solution)/shard_map/dot_general | solution.py:670
  34.2 5.8 %local_stats.1 = (f32[16,72,128]{2,1,0:T(8,128)}, f32[2,768]{1,0:T(2,128)}) custom-call(s32[2]{0:T(128)} %copy-done.38, s32[2]{0:T(128)} %copy-done.37, f32[16,512,128]{2,1,0:T(8,128)} %project.1.kv_ref, bf16[16,256,128]{2,1,0:T(8,128)(2,1)} %copy-done.22, f32[8,128]{1,0:T(8,128)} %broadcast_in_dim.100.score_ref, f32[2,768]{1,0:T(2,128)} %copy-done.35), custom_call_target="tpu_custom_call" | custom-call | flops 1024 | bytes 1024 | tf_op jit(solution)/shard_map/local_stats/pallas_call | solution.py:179
  40.0 4.2 %turn.1 = (bf16[16,128,512]{2,1,0:T(8,128)(2,1)}, bf16[16,128,512]{2,1,0:T(8,128)(2,1)}) custom-call(s32[1]{0:T(128)} %bitcast.2.rank_ref, f32[16,72,128]{2,1,0:T(8,128)} %get-tuple-element.31.after_ref, bf16[512,4096]{1,0:T(8,128)(2,1)} %bitcast.70), custom_call_target="tpu_custom_call" | custom-call | bytes 67108864 | tf_op jit(solution)/shard_map/turn/pallas_call | solution.py:105
  45.4 7.2 %all-to-all-start.1 = ((f32[16,72,128]{2,1,0:T(8,128)}), f32[16,72,128]{2,1,0:T(8,128)S(1)}, u32[]{:S(2)}, u32[]{:S(2)}) async-start(f32[16,72,128]{2,1,0:T(8,128)} %get-tuple-element.31.after_ref), calls=%async_computation.1 | async-start | bytes 1179648 | tf_op jit(solution)/shard_map/all_to_all | solution.py:701
  52.7 3.8 %fusion.13.after_ref.part_ref = f32[2,192,768]{2,1,0:T(8,128)} fusion(bf16[2,256,192]{2,1,0:T(8,128)(2,1)S(1)} %bitcast.80, f32[2,256,768]{2,1,0:T(8,128)} %get-tuple-element.71, f32[2,768]{1,0:T(2,128)S(1)} %broadcast_divide_fusion, pred[2,256]{1,0:T(4,128)(4,1)S(1)} %iota_compare_fusion), kind=kOutput, calls=%fused_computation.18 | convolution fusion | flops 159252480 | bytes 2955776 | tf_op jit(solution)/shard_map/dot_general | solution.py:695
  56.5 9.0 %all-to-all-done.1.stats_ref = f32[16,72,128]{2,1,0:T(8,128)S(1)} async-done(((f32[16,72,128]{2,1,0:T(8,128)}), f32[16,72,128]{2,1,0:T(8,128)S(1)}, u32[]{:S(2)}, u32[]{:S(2)}) %all-to-all-start.1) | async-done | bytes 589856 | tf_op jit(solution)/shard_map/all_to_all | solution.py:701
  66.4 5.2 %back_first.1 = (bf16[512,1024]{1,0:T(8,128)(2,1)}, f32[4,16,128]{2,1,0:T(8,128)}, f32[8,128]{1,0:T(8,128)}) custom-call(s32[2]{0:T(128)} %copy-done.38, s32[2]{0:T(128)} %copy-done.37, s32[1]{0:T(128)} %bitcast.5.own_ref, s32[32]{0:T(128)} %bitcast.84, f32[2,192,768]{2,1,0:T(8,128)} %fusion.13.after_ref.part_ref, f32[16,512,128]{2,1,0:T(8,128)} %project.1.kv_ref, ...), custom_call_target="tpu_custom_call" | custom-call | bytes 33554432 | tf_op jit(solution)/shard_map/back_first/pallas_call | solution.py:291
  71.6 4.8 %back_second.1.refs_2_.refs_4_.b_ref = bf16[512,1024]{1,0:T(8,128)(2,1)} custom-call(s32[2]{0:T(128)} %copy-done.38, s32[2]{0:T(128)} %copy-done.37, f32[16,512,128]{2,1,0:T(8,128)} %project.1.kv_ref, bf16[16,256,128]{2,1,0:T(8,128)(2,1)} %copy-done.22, f32[4,16,128]{2,1,0:T(8,128)} %get-tuple-element.32.after_ref.norm_ref), custom_call_target="tpu_custom_call" | custom-call | bytes 33554432 | tf_op jit(solution)/shard_map/back_second/pallas_call | solution.py:318
  78.2 4.0 %far_chunk.2 = (bf16[512,512]{1,0:T(8,128)(2,1)}, bf16[512,512]{1,0:T(8,128)(2,1)}, f32[8,128]{1,0:T(8,128)}) custom-call(s32[1]{0:T(128)S(6)} %select_n.124.which_ref, f32[4,16,128]{2,1,0:T(8,128)} %get-tuple-element.32.after_ref.norm_ref, bf16[4,4,128,512]{3,2,1,0:T(8,128)(2,1)} %bitcast.53, bf16[4,4,128,512]{3,2,1,0:T(8,128)(2,1)} %bitcast.61, ...), custom_call_target="tpu_custom_call" | custom-call | flops 1024 | bytes 1024 | tf_op jit(solution)/shard_map/far_chunk/pallas_call | solution.py:362
  82.3 3.2 %collective-permute-start.8 = (bf16[512,512]{1,0:T(8,128)(2,1)}, bf16[512,512]{1,0:T(8,128)(2,1)S(1)}, u32[]{:S(2)}, u32[]{:S(2)}) collective-permute-start(bf16[512,512]{1,0:T(8,128)(2,1)} %get-tuple-element.43), channel_id=1, source_target_pairs={{0,96},{8,104},{16,112},{24,120},{32,0},{40,8},{48,16},{56,24},{64... | collective-permute-start | bytes 1572872 | tf_op jit(solution)/shard_map/ppermute | solution.py:607
  87.4 3.5 %collective-permute-start.4 = (f32[8,128]{1,0:T(8,128)}, f32[8,128]{1,0:T(8,128)S(1)}, u32[]{:S(2)}, u32[]{:S(2)}) collective-permute-start(f32[8,128]{1,0:T(8,128)} %get-tuple-element.38.refs_4_), channel_id=1, source_target_pairs={{0,4},{2,6},{4,0},{6,2},{1,5},{3,7},{5,1},{7,3},{8,12},{10,14},{12... | collective-permute-start | bytes 12296 | tf_op jit(solution)/shard_map/ppermute | solution.py:723
  92.0 4.1 %far_chunk.3 = (bf16[512,512]{1,0:T(8,128)(2,1)}, bf16[512,512]{1,0:T(8,128)(2,1)}, f32[8,128]{1,0:T(8,128)}) custom-call(s32[1]{0:T(128)S(6)} %select_n.123.which_ref, bf16[512,512]{1,0:T(8,128)(2,1)} %get-tuple-element.37.after_ref, bf16[4,4,128,512]{3,2,1,0:T(8,128)(2,1)} %bitcast.54, bf16[4,4,128,512]{3,2,1,0:T(8,128)(2,1)} %bitcast.62, ...), custom_call_target="tpu_custom_call" | custom-call | flops 1024 | bytes 1024 | tf_op jit(solution)/shard_map/far_chunk/pallas_call | solution.py:362
  96.8 2.2 %apply_gap.1 = (f32[96,768]{1,0:T(8,128)}, bf16[96,768]{1,0:T(8,128)(2,1)}) custom-call(s32[1]{0:T(128)} %bitcast.2.rank_ref, f32[8,128]{1,0:T(8,128)} %get-tuple-element.39.aux_ref, f32[8,128]{1,0:T(8,128)} %copy-done.40, f32[8,128]{1,0:T(8,128)} %copy-done.41, f32[8,128]{1,0:T(8,128)} %copy-done.42, f32[2,192,768]{2,1,0:T(8,128)} %fusion.13.after_ref.part_ref, ...), custom_call_target="tpu_custom_call" | custom-call | flops 1024 | bytes 1024 | tf_op jit(solution)/shard_map/apply_gap/pallas_call | solution.py:578
  99.6 2.7 %collective-permute-start.11 = (bf16[512,512]{1,0:T(8,128)(2,1)S(1)}, bf16[512,512]{1,0:T(8,128)(2,1)S(1)}, u32[]{:S(2)}, u32[]{:S(2)}) collective-permute-start(bf16[512,512]{1,0:T(8,128)(2,1)S(1)} %copy-done.46), channel_id=1, source_target_pairs={{0,24},{8,0},{16,8},{24,16},{32,56},{40,32},{48,40},{56,48},{64,88... | collective-permute-start | bytes 1572872 | tf_op jit(solution)/shard_map/ppermute | solution.py:607
  102.2 3.8 %own_chunk.2.after_ref = bf16[2,512,512]{2,1,0:T(8,128)(2,1)} custom-call(s32[1]{0:T(128)S(6)} %select_n.122.which_ref, bf16[96,768]{1,0:T(8,128)(2,1)} %get-tuple-element.41.after_ref, bf16[4,4,128,512]{3,2,1,0:T(8,128)(2,1)} %bitcast.55, bf16[4,4,128,512]{3,2,1,0:T(8,128)(2,1)} %bitcast.63, bf16[512,1024]{1,0:T(8,128)(2,1)} %get-tuple-element.35.refs_2_.refs_4_.a_ref, ...), custom_call_target="tpu_custom_call" | custom-call | flops 1024 | bytes 1024 | tf_op jit(solution)/shard_map/own_chunk/pallas_call | solution.py:362
  108.9 6.2 %side_chunks.2 = (bf16[2,512,512]{2,1,0:T(8,128)(2,1)}, bf16[2,512,512]{2,1,0:T(8,128)(2,1)}) custom-call(s32[2]{0:T(128)} %get-tuple-element.68.which_ref, bf16[96,768]{1,0:T(8,128)(2,1)} %copy-done.10, bf16[4,4,128,512]{3,2,1,0:T(8,128)(2,1)} %bitcast.56, bf16[4,4,128,512]{3,2,1,0:T(8,128)(2,1)} %bitcast.64, bf16[4,4,128,512]{3,2,1,0:T(8,128)(2,1)} %bitcast.57, ...), custom_call_target="tpu_custom_call" | custom-call | flops 1024 | bytes 1024 | tf_op jit(solution)/shard_map/side_chunks/pallas_call | solution.py:362
  115.1 2.0 %collective-permute-start.15 = (bf16[2,512,512]{2,1,0:T(8,128)(2,1)}, bf16[2,512,512]{2,1,0:T(8,128)(2,1)S(1)}, u32[]{:S(2)}, u32[]{:S(2)}) collective-permute-start(bf16[2,512,512]{2,1,0:T(8,128)(2,1)} %get-tuple-element.44.after_ref), channel_id=1, source_target_pairs={{0,32},{8,40},{16,48},{24,56},{32,64},{40,72},{48,80},{56,88},{64,... | collective-permute-start | bytes 3145736 | tf_op jit(solution)/shard_map/ppermute | solution.py:607
  121.6 6.2 %side_chunks.3 = (bf16[2,512,512]{2,1,0:T(8,128)(2,1)}, bf16[2,512,512]{2,1,0:T(8,128)(2,1)}) custom-call(s32[2]{0:T(128)} %get-tuple-element.69.which_ref, bf16[96,768]{1,0:T(8,128)(2,1)} %copy-done.12, bf16[4,4,128,512]{3,2,1,0:T(8,128)(2,1)} %bitcast.58, bf16[4,4,128,512]{3,2,1,0:T(8,128)(2,1)} %bitcast.66, bf16[4,4,128,512]{3,2,1,0:T(8,128)(2,1)} %bitcast.59, ...), custom_call_target="tpu_custom_call" | custom-call | flops 1024 | bytes 1024 | tf_op jit(solution)/shard_map/side_chunks/pallas_call | solution.py:362
  131.1 3.9 %own_chunk.3.after_ref = bf16[2,512,512]{2,1,0:T(8,128)(2,1)} custom-call(s32[1]{0:T(128)S(6)} %select_n.118.which_ref, bf16[96,768]{1,0:T(8,128)(2,1)} %copy-done.8, bf16[4,4,128,512]{3,2,1,0:T(8,128)(2,1)} %bitcast.60, bf16[4,4,128,512]{3,2,1,0:T(8,128)(2,1)} %bitcast.68, bf16[512,1024]{1,0:T(8,128)(2,1)} %back_second.1.refs_2_.refs_4_.b_ref, ...), custom_call_target="tpu_custom_call" | custom-call | flops 1024 | bytes 1024 | tf_op jit(solution)/shard_map/own_chunk/pallas_call | solution.py:362
  135.0 8.3 %collective-permute-done.13.b_ref = bf16[96,768]{1,0:T(8,128)(2,1)S(1)} collective-permute-done((bf16[96,768]{1,0:T(8,128)(2,1)S(1)}, bf16[96,768]{1,0:T(8,128)(2,1)S(1)}, u32[]{:S(2)}, u32[]{:S(2)}) %collective-permute-start.13) | collective-permute-done | bytes 147488 | tf_op jit(solution)/shard_map/ppermute | solution.py:717
  146.7 2.4 %collective-permute-start.18 = (bf16[2,512,512]{2,1,0:T(8,128)(2,1)}, bf16[2,512,512]{2,1,0:T(8,128)(2,1)}, u32[]{:S(2)}, u32[]{:S(2)}) collective-permute-start(bf16[2,512,512]{2,1,0:T(8,128)(2,1)} %get-tuple-element.49), channel_id=1, source_target_pairs={{0,24},{8,0},{16,8},{24,16},{32,56},{40,32},{48,40},{56,48},{64,88... | collective-permute-start | bytes 3145736 | tf_op jit(solution)/shard_map/ppermute | solution.py:607
  149.1 3.9 %by_token.1.after_ref = bf16[512,16,128]{2,1,0:T(8,128)(2,1)} custom-call(bf16[96,768]{1,0:T(8,128)(2,1)} %copy-done.5, bf16[512,1024]{1,0:T(8,128)(2,1)} %get-tuple-element.35.refs_2_.refs_4_.a_ref, bf16[512,1024]{1,0:T(8,128)(2,1)} %back_second.1.refs_2_.refs_4_.b_ref), custom_call_target="tpu_custom_call" | custom-call | flops 1024 | bytes 1024 | tf_op jit(solution)/shard_map/by_token/pallas_call | solution.py:532
  161.8 3.9 %totals.2 = (bf16[2,128,512]{2,1,0:T(8,128)(2,1)}, bf16[2,128,512]{2,1,0:T(8,128)(2,1)}, bf16[2,128,512]{2,1,0:T(8,128)(2,1)}, bf16[2,128,512]{2,1,0:T(8,128)(2,1)}) custom-call(s32[1]{0:T(128)} %bitcast.which_ref, bf16[96,768]{1,0:T(8,128)(2,1)} %copy-done.7, bf16[2,4,128,512]{3,2,1,0:T(8,128)(2,1)} %bitcast.49, bf16[2,4,128,512]{3,2,1,0:T(8,128)(2,1)} %bitcast.77, ...), custom_call_target="tpu_custom_call" | custom-call | flops 1024 | bytes 1024 | tf_op jit(solution)/shard_map/totals/pallas_call | solution.py:469
  165.7 8.8 %collective-permute-done.26 = bf16[192,768]{1,0:T(8,128)(2,1)S(1)} collective-permute-done((bf16[192,768]{1,0:T(8,128)(2,1)S(1)}, bf16[192,768]{1,0:T(8,128)(2,1)S(1)}, u32[]{:S(2)}, u32[]{:S(2)}) %collective-permute-start.26) | collective-permute-done | bytes 294944 | tf_op jit(solution)/shard_map/ppermute | solution.py:760
  176.4 2.2 %collective-permute-start.21 = (bf16[2,128,512]{2,1,0:T(8,128)(2,1)}, bf16[2,128,512]{2,1,0:T(8,128)(2,1)S(1)}, u32[]{:S(2)}, u32[]{:S(2)}) collective-permute-start(bf16[2,128,512]{2,1,0:T(8,128)(2,1)} %get-tuple-element.53), channel_id=1, source_target_pairs={{0,24},{8,0},{16,8},{24,16},{32,56},{40,32},{48,40},{56,48},{64,88... | collective-permute-start | bytes 786440 | tf_op jit(solution)/shard_map/ppermute | solution.py:607
  178.6 4.0 %totals.3 = (bf16[2,128,512]{2,1,0:T(8,128)(2,1)}, bf16[2,128,512]{2,1,0:T(8,128)(2,1)}, bf16[2,128,512]{2,1,0:T(8,128)(2,1)}, bf16[2,128,512]{2,1,0:T(8,128)(2,1)}) custom-call(s32[1]{0:T(128)} %bitcast.1.which_ref, bf16[2,128,512]{2,1,0:T(8,128)(2,1)} %get-tuple-element.48.after_ref.refs_0_, bf16[2,4,128,512]{3,2,1,0:T(8,128)(2,1)} %bitcast.50, ...), custom_call_target="tpu_custom_call" | custom-call | flops 1024 | bytes 1024 | tf_op jit(solution)/shard_map/totals/pallas_call | solution.py:469
  182.6 2.3 %collective-permute-start.22 = (bf16[2,128,512]{2,1,0:T(8,128)(2,1)}, bf16[2,128,512]{2,1,0:T(8,128)(2,1)S(1)}, u32[]{:S(2)}, u32[]{:S(2)}) collective-permute-start(bf16[2,128,512]{2,1,0:T(8,128)(2,1)} %get-tuple-element.54), channel_id=1, source_target_pairs={{0,32},{8,40},{16,48},{24,56},{32,64},{40,72},{48,80},{56,88},{64,... | collective-permute-start | bytes 786440 | tf_op jit(solution)/shard_map/ppermute | solution.py:607
  184.9 3.6 %collective-permute-start.23 = (bf16[2,128,512]{2,1,0:T(8,128)(2,1)}, bf16[2,128,512]{2,1,0:T(8,128)(2,1)S(1)}, u32[]{:S(2)}, u32[]{:S(2)}) collective-permute-start(bf16[2,128,512]{2,1,0:T(8,128)(2,1)} %get-tuple-element.55), channel_id=1, source_target_pairs={{0,64},{8,72},{16,80},{24,88},{32,96},{40,104},{48,112},{56,120},{... | collective-permute-start | bytes 786440 | tf_op jit(solution)/shard_map/ppermute | solution.py:607
  196.5 2.3 %finish.1 = bf16[128,16,128]{2,1,0:T(8,128)(2,1)} custom-call(bf16[2,128,512]{2,1,0:T(8,128)(2,1)} %copy-done.19, bf16[2,128,512]{2,1,0:T(8,128)(2,1)} %get-tuple-element.50.after_ref.refs_0_, bf16[2,128,512]{2,1,0:T(8,128)(2,1)} %copy-done.32, bf16[2,128,512]{2,1,0:T(8,128)(2,1)} %copy-done.33, bf16[2,128,512]{2,1,0:T(8,128)(2,1)} %collective-permute-done.24.refs_3_), custom_call_target="tpu_custom_call" | custom-call | flops 1024 | bytes 1024 | tf_op jit(solution)/shard_map/finish/pallas_call | solution.py:515
  (170 shorter events, 45.6 us)
Async XLA Ops:
  0.6 30.2 %copy-start = (bf16[768,768]{1,0:T(8,128)(2,1)S(1)}, bf16[768,768]{1,0:T(8,128)(2,1)}, u32[]{:S(2)}) copy-start(bf16[768,768]{1,0:T(8,128)(2,1)} %param.22) | copy-start | bytes 3538948
  6.9 26.3 %all-to-all-start = ((bf16[16,256,128]{2,1,0:T(8,128)(2,1)}), bf16[16,256,128]{2,1,0:T(8,128)(2,1)S(1)}, u32[]{:S(2)}, u32[]{:S(2)}) async-start(bf16[16,256,128]{2,1,0:T(8,128)(2,1)} %bitcast.71), calls=%async_computation | async-start | bytes 2097152 | tf_op jit(solution)/shard_map/all_to_all | solution.py:638
  44.2 32.7 %collective-permute-start = (bf16[16,128,512]{2,1,0:T(8,128)(2,1)}, bf16[16,128,512]{2,1,0:T(8,128)(2,1)S(1)}, u32[]{:S(2)}, u32[]{:S(2)}) collective-permute-start(bf16[16,128,512]{2,1,0:T(8,128)(2,1)} %get-tuple-element.34), channel_id=1, source_target_pairs={{0,1},{1,0},{2,3},{3,2},{4,5},{5,4},{6,7},{7,6},{8,9},{9,8},{10,11... | collective-permute-start | bytes 6291464 | tf_op jit(solution)/shard_map/ppermute | solution.py:688
  45.4 20.1 %all-to-all-start.1 = ((f32[16,72,128]{2,1,0:T(8,128)}), f32[16,72,128]{2,1,0:T(8,128)S(1)}, u32[]{:S(2)}, u32[]{:S(2)}) async-start(f32[16,72,128]{2,1,0:T(8,128)} %get-tuple-element.31.after_ref), calls=%async_computation.1 | async-start | bytes 1179648 | tf_op jit(solution)/shard_map/all_to_all | solution.py:701
  71.6 5.3 %collective-permute-start.1 = (bf16[512,1024]{1,0:T(8,128)(2,1)}, bf16[512,1024]{1,0:T(8,128)(2,1)}, u32[]{:S(2)}, u32[]{:S(2)}) collective-permute-start(bf16[512,1024]{1,0:T(8,128)(2,1)} %get-tuple-element.35.refs_2_.refs_4_.a_ref), channel_id=1, source_target_pairs={{0,1},{1,0},{2,3},{3,2},{4,5},{5,4},{6,7},{7,6},{8,9},{9,8},{10,11... | collective-permute-start | bytes 3145736 | tf_op jit(solution)/shard_map/ppermute | solution.py:705
  76.4 14.5 %collective-permute-start.2 = (bf16[512,1024]{1,0:T(8,128)(2,1)}, bf16[512,1024]{1,0:T(8,128)(2,1)S(1)}, u32[]{:S(2)}, u32[]{:S(2)}) collective-permute-start(bf16[512,1024]{1,0:T(8,128)(2,1)} %back_second.1.refs_2_.refs_4_.b_ref), channel_id=1, source_target_pairs={{0,1},{1,0},{2,3},{3,2},{4,5},{5,4},{6,7},{7,6},{8,9},{9,8},{10,11... | collective-permute-start | bytes 3145736 | tf_op jit(solution)/shard_map/ppermute | solution.py:707
  82.3 25.7 %collective-permute-start.7 = (bf16[512,512]{1,0:T(8,128)(2,1)}, bf16[512,512]{1,0:T(8,128)(2,1)S(1)}, u32[]{:S(2)}, u32[]{:S(2)}) collective-permute-start(bf16[512,512]{1,0:T(8,128)(2,1)} %get-tuple-element.37.after_ref), channel_id=1, source_target_pairs={{0,32},{8,40},{16,48},{24,56},{32,64},{40,72},{48,80},{56,88},{64,... | collective-permute-start | bytes 1572872 | tf_op jit(solution)/shard_map/ppermute | solution.py:607
  82.3 25.7 %collective-permute-start.8 = (bf16[512,512]{1,0:T(8,128)(2,1)}, bf16[512,512]{1,0:T(8,128)(2,1)S(1)}, u32[]{:S(2)}, u32[]{:S(2)}) collective-permute-start(bf16[512,512]{1,0:T(8,128)(2,1)} %get-tuple-element.43), channel_id=1, source_target_pairs={{0,96},{8,104},{16,112},{24,120},{32,0},{40,8},{48,16},{56,24},{64... | collective-permute-start | bytes 1572872 | tf_op jit(solution)/shard_map/ppermute | solution.py:607
  85.5 10.6 %collective-permute-start.3 = (f32[8,128]{1,0:T(8,128)}, f32[8,128]{1,0:T(8,128)S(1)}, u32[]{:S(2)}, u32[]{:S(2)}) collective-permute-start(f32[8,128]{1,0:T(8,128)} %get-tuple-element.38.refs_4_), channel_id=1, source_target_pairs={{0,2},{2,4},{4,6},{6,0},{1,3},{3,5},{5,7},{7,1},{8,10},{10,12},{12... | collective-permute-start | bytes 12296 | tf_op jit(solution)/shard_map/ppermute | solution.py:723
  87.4 8.7 %collective-permute-start.4 = (f32[8,128]{1,0:T(8,128)}, f32[8,128]{1,0:T(8,128)S(1)}, u32[]{:S(2)}, u32[]{:S(2)}) collective-permute-start(f32[8,128]{1,0:T(8,128)} %get-tuple-element.38.refs_4_), channel_id=1, source_target_pairs={{0,4},{2,6},{4,0},{6,2},{1,5},{3,7},{5,1},{7,3},{8,12},{10,14},{12... | collective-permute-start | bytes 12296 | tf_op jit(solution)/shard_map/ppermute | solution.py:723
  91.0 5.2 %collective-permute-start.5 = (f32[8,128]{1,0:T(8,128)}, f32[8,128]{1,0:T(8,128)S(1)}, u32[]{:S(2)}, u32[]{:S(2)}) collective-permute-start(f32[8,128]{1,0:T(8,128)} %get-tuple-element.38.refs_4_), channel_id=1, source_target_pairs={{0,6},{2,0},{4,2},{6,4},{1,7},{3,1},{5,3},{7,5},{8,14},{10,8},{12,... | collective-permute-start | bytes 12296 | tf_op jit(solution)/shard_map/ppermute | solution.py:723
  98.9 7.1 %collective-permute-start.6 = (bf16[96,768]{1,0:T(8,128)(2,1)}, bf16[96,768]{1,0:T(8,128)(2,1)S(1)}, u32[]{:S(2)}, u32[]{:S(2)}) collective-permute-start(bf16[96,768]{1,0:T(8,128)(2,1)} %get-tuple-element.41.after_ref), channel_id=1, source_target_pairs={{0,1},{1,0},{2,3},{3,2},{4,5},{5,4},{6,7},{7,6},{8,9},{9,8},{10,11... | collective-permute-start | bytes 442376 | tf_op jit(solution)/shard_map/ppermute | solution.py:732
  98.9 21.7 %collective-permute-start.10 = (bf16[512,512]{1,0:T(8,128)(2,1)S(1)}, bf16[512,512]{1,0:T(8,128)(2,1)S(1)}, u32[]{:S(2)}, u32[]{:S(2)}) collective-permute-start(bf16[512,512]{1,0:T(8,128)(2,1)S(1)} %copy-done.31), channel_id=1, source_target_pairs={{0,8},{8,16},{16,24},{24,0},{32,40},{40,48},{48,56},{56,32},{64,72... | collective-permute-start | bytes 1572872 | tf_op jit(solution)/shard_map/ppermute | solution.py:607
  99.6 21.1 %collective-permute-start.11 = (bf16[512,512]{1,0:T(8,128)(2,1)S(1)}, bf16[512,512]{1,0:T(8,128)(2,1)S(1)}, u32[]{:S(2)}, u32[]{:S(2)}) collective-permute-start(bf16[512,512]{1,0:T(8,128)(2,1)S(1)} %copy-done.46), channel_id=1, source_target_pairs={{0,24},{8,0},{16,8},{24,16},{32,56},{40,32},{48,40},{56,48},{64,88... | collective-permute-start | bytes 1572872 | tf_op jit(solution)/shard_map/ppermute | solution.py:607
  107.3 11.1 %collective-permute-start.9 = (bf16[96,768]{1,0:T(8,128)(2,1)S(1)}, bf16[96,768]{1,0:T(8,128)(2,1)S(1)}, u32[]{:S(2)}, u32[]{:S(2)}) collective-permute-start(bf16[96,768]{1,0:T(8,128)(2,1)S(1)} %add_after.5.after_ref.a_ref), channel_id=1, source_target_pairs={{0,32},{8,40},{16,48},{24,56},{32,0},{40,8},{48,16},{56,24},{64,96... | collective-permute-start | bytes 442376 | tf_op jit(solution)/shard_map/ppermute | solution.py:717
  115.1 43.8 %collective-permute-start.15 = (bf16[2,512,512]{2,1,0:T(8,128)(2,1)}, bf16[2,512,512]{2,1,0:T(8,128)(2,1)S(1)}, u32[]{:S(2)}, u32[]{:S(2)}) collective-permute-start(bf16[2,512,512]{2,1,0:T(8,128)(2,1)} %get-tuple-element.44.after_ref), channel_id=1, source_target_pairs={{0,32},{8,40},{16,48},{24,56},{32,64},{40,72},{48,80},{56,88},{64,... | collective-permute-start | bytes 3145736 | tf_op jit(solution)/shard_map/ppermute | solution.py:607
  117.1 43.2 %collective-permute-start.16 = (bf16[2,512,512]{2,1,0:T(8,128)(2,1)}, bf16[2,512,512]{2,1,0:T(8,128)(2,1)}, u32[]{:S(2)}, u32[]{:S(2)}) collective-permute-start(bf16[2,512,512]{2,1,0:T(8,128)(2,1)} %get-tuple-element.47), channel_id=1, source_target_pairs={{0,96},{8,104},{16,112},{24,120},{32,0},{40,8},{48,16},{56,24},{64... | collective-permute-start | bytes 3145736 | tf_op jit(solution)/shard_map/ppermute | solution.py:607
  120.6 7.3 %collective-permute-start.12 = (bf16[96,768]{1,0:T(8,128)(2,1)S(1)}, bf16[96,768]{1,0:T(8,128)(2,1)S(1)}, u32[]{:S(2)}, u32[]{:S(2)}) collective-permute-start(bf16[96,768]{1,0:T(8,128)(2,1)S(1)} %add_after.6.after_ref.a_ref), channel_id=1, source_target_pairs={{0,8},{8,0},{16,24},{24,16},{32,40},{40,32},{48,56},{56,48},{64,72... | collective-permute-start | bytes 442376 | tf_op jit(solution)/shard_map/ppermute | solution.py:717
  130.1 13.2 %collective-permute-start.13 = (bf16[96,768]{1,0:T(8,128)(2,1)S(1)}, bf16[96,768]{1,0:T(8,128)(2,1)S(1)}, u32[]{:S(2)}, u32[]{:S(2)}) collective-permute-start(bf16[96,768]{1,0:T(8,128)(2,1)S(1)} %add_after.7.after_ref.a_ref), channel_id=1, source_target_pairs={{0,64},{8,72},{16,80},{24,88},{32,96},{40,104},{48,112},{56,120},{... | collective-permute-start | bytes 442376 | tf_op jit(solution)/shard_map/ppermute | solution.py:717
  145.4 8.4 %collective-permute-start.14 = (bf16[96,768]{1,0:T(8,128)(2,1)S(1)}, bf16[96,768]{1,0:T(8,128)(2,1)S(1)}, u32[]{:S(2)}, u32[]{:S(2)}) collective-permute-start(bf16[96,768]{1,0:T(8,128)(2,1)S(1)} %add_after.8.after_ref.a_ref), channel_id=1, source_target_pairs={{0,16},{8,24},{16,0},{24,8},{32,48},{40,56},{48,32},{56,40},{64,80... | collective-permute-start | bytes 442376 | tf_op jit(solution)/shard_map/ppermute | solution.py:717
  145.9 29.0 %collective-permute-start.17 = (bf16[2,512,512]{2,1,0:T(8,128)(2,1)S(1)}, bf16[2,512,512]{2,1,0:T(8,128)(2,1)}, u32[]{:S(2)}, u32[]{:S(2)}) collective-permute-start(bf16[2,512,512]{2,1,0:T(8,128)(2,1)S(1)} %copy-done.15), channel_id=1, source_target_pairs={{0,8},{8,16},{16,24},{24,0},{32,40},{40,48},{48,56},{56,32},{64,72... | collective-permute-start | bytes 3145736 | tf_op jit(solution)/shard_map/ppermute | solution.py:607
  146.7 29.8 %collective-permute-start.18 = (bf16[2,512,512]{2,1,0:T(8,128)(2,1)}, bf16[2,512,512]{2,1,0:T(8,128)(2,1)}, u32[]{:S(2)}, u32[]{:S(2)}) collective-permute-start(bf16[2,512,512]{2,1,0:T(8,128)(2,1)} %get-tuple-element.49), channel_id=1, source_target_pairs={{0,24},{8,0},{16,8},{24,16},{32,56},{40,32},{48,40},{56,48},{64,88... | collective-permute-start | bytes 3145736 | tf_op jit(solution)/shard_map/ppermute | solution.py:607
  156.4 1.5 collective-permute-start.25
  157.8 16.7 %collective-permute-start.26 = (bf16[192,768]{1,0:T(8,128)(2,1)S(1)}, bf16[192,768]{1,0:T(8,128)(2,1)S(1)}, u32[]{:S(2)}, u32[]{:S(2)}) collective-permute-start(bf16[192,768]{1,0:T(8,128)(2,1)S(1)} %bitcast.73), channel_id=1, source_target_pairs={{0,2},{2,4},{4,6},{6,0},{1,3},{3,5},{5,7},{7,1},{8,10},{10,12},{12... | collective-permute-start | bytes 884744 | tf_op jit(solution)/shard_map/ppermute | solution.py:760
  158.9 23.7 %collective-permute-start.27 = (bf16[192,768]{1,0:T(8,128)(2,1)S(1)}, bf16[192,768]{1,0:T(8,128)(2,1)}, u32[]{:S(2)}, u32[]{:S(2)}) collective-permute-start(bf16[192,768]{1,0:T(8,128)(2,1)S(1)} %bitcast.74), channel_id=1, source_target_pairs={{0,4},{2,6},{4,0},{6,2},{1,5},{3,7},{5,1},{7,3},{8,12},{10,14},{12... | collective-permute-start | bytes 884744 | tf_op jit(solution)/shard_map/ppermute | solution.py:760
  160.4 24.5 %collective-permute-start.28 = (bf16[192,768]{1,0:T(8,128)(2,1)S(1)}, bf16[192,768]{1,0:T(8,128)(2,1)}, u32[]{:S(2)}, u32[]{:S(2)}) collective-permute-start(bf16[192,768]{1,0:T(8,128)(2,1)S(1)} %bitcast.75), channel_id=1, source_target_pairs={{0,6},{2,0},{4,2},{6,4},{1,7},{3,1},{5,3},{7,5},{8,14},{10,8},{12,... | collective-permute-start | bytes 884744 | tf_op jit(solution)/shard_map/ppermute | solution.py:760
  174.5 13.9 %collective-permute-start.19 = (bf16[2,128,512]{2,1,0:T(8,128)(2,1)}, bf16[2,128,512]{2,1,0:T(8,128)(2,1)S(1)}, u32[]{:S(2)}, u32[]{:S(2)}) collective-permute-start(bf16[2,128,512]{2,1,0:T(8,128)(2,1)} %get-tuple-element.51), channel_id=1, source_target_pairs={{0,8},{8,16},{16,24},{24,0},{32,40},{40,48},{48,56},{56,32},{64,72... | collective-permute-start | bytes 786440 | tf_op jit(solution)/shard_map/ppermute | solution.py:607
  174.9 16.9 %collective-permute-start.20 = (bf16[2,128,512]{2,1,0:T(8,128)(2,1)}, bf16[2,128,512]{2,1,0:T(8,128)(2,1)S(1)}, u32[]{:S(2)}, u32[]{:S(2)}) collective-permute-start(bf16[2,128,512]{2,1,0:T(8,128)(2,1)} %get-tuple-element.52), channel_id=1, source_target_pairs={{0,16},{8,24},{16,0},{24,8},{32,48},{40,56},{48,32},{56,40},{64,80... | collective-permute-start | bytes 786440 | tf_op jit(solution)/shard_map/ppermute | solution.py:607
  176.4 15.4 %collective-permute-start.21 = (bf16[2,128,512]{2,1,0:T(8,128)(2,1)}, bf16[2,128,512]{2,1,0:T(8,128)(2,1)S(1)}, u32[]{:S(2)}, u32[]{:S(2)}) collective-permute-start(bf16[2,128,512]{2,1,0:T(8,128)(2,1)} %get-tuple-element.53), channel_id=1, source_target_pairs={{0,24},{8,0},{16,8},{24,16},{32,56},{40,32},{48,40},{56,48},{64,88... | collective-permute-start | bytes 786440 | tf_op jit(solution)/shard_map/ppermute | solution.py:607
  182.6 11.3 %collective-permute-start.22 = (bf16[2,128,512]{2,1,0:T(8,128)(2,1)}, bf16[2,128,512]{2,1,0:T(8,128)(2,1)S(1)}, u32[]{:S(2)}, u32[]{:S(2)}) collective-permute-start(bf16[2,128,512]{2,1,0:T(8,128)(2,1)} %get-tuple-element.54), channel_id=1, source_target_pairs={{0,32},{8,40},{16,48},{24,56},{32,64},{40,72},{48,80},{56,88},{64,... | collective-permute-start | bytes 786440 | tf_op jit(solution)/shard_map/ppermute | solution.py:607
  184.9 10.9 %collective-permute-start.23 = (bf16[2,128,512]{2,1,0:T(8,128)(2,1)}, bf16[2,128,512]{2,1,0:T(8,128)(2,1)S(1)}, u32[]{:S(2)}, u32[]{:S(2)}) collective-permute-start(bf16[2,128,512]{2,1,0:T(8,128)(2,1)} %get-tuple-element.55), channel_id=1, source_target_pairs={{0,64},{8,72},{16,80},{24,88},{32,96},{40,104},{48,112},{56,120},{... | collective-permute-start | bytes 786440 | tf_op jit(solution)/shard_map/ppermute | solution.py:607
  188.4 7.4 %collective-permute-start.24 = (bf16[2,128,512]{2,1,0:T(8,128)(2,1)}, bf16[2,128,512]{2,1,0:T(8,128)(2,1)}, u32[]{:S(2)}, u32[]{:S(2)}) collective-permute-start(bf16[2,128,512]{2,1,0:T(8,128)(2,1)} %get-tuple-element.56), channel_id=1, source_target_pairs={{0,96},{8,104},{16,112},{24,120},{32,0},{40,8},{48,16},{56,24},{64... | collective-permute-start | bytes 786440 | tf_op jit(solution)/shard_map/ppermute | solution.py:607
  (46 other events, 188.4 us)

commit v4 on v3

--- a/solution.py
+++ b/solution.py
@@ -256,6 +256,7 @@
     own_ref,
     order_ref,
     after_ref,
+    also_ref,
     kv_ref,
     qd_ref,
     stats_ref,
@@ -293,7 +294,7 @@
         grid_spec=pltpu.PrefetchScalarGridSpec(
             num_scalar_prefetch=4,
             grid=(8 // per_step,),
-            in_specs=[pl.BlockSpec(memory_space=pl.ANY)]
+            in_specs=[pl.BlockSpec(memory_space=pl.ANY)] * 2
             + back_specs(key_value, gathered, 0, per_step)
             + [pl.BlockSpec(stats.shape, lambda i, *_: (0, 0, 0))],
             out_specs=[
@@ -310,7 +311,7 @@
         compiler_params=pltpu.CompilerParams(vmem_limit_bytes=VMEM),
         cost_estimate=BACK_COST,
         name="back_first",
-    )(own_question, own_blocks, enc_rank.reshape(1), order_row, after, key_value, gathered, stats)
+    )(own_question, own_blocks, enc_rank.reshape(1), order_row, *after, key_value, gathered, stats)
 
 
 def back_second(own_question, own_blocks, key_value, gathered, norms, per_step=4):
@@ -345,13 +346,14 @@
     return pl.BlockSpec((SIDE, 1, 128, tokens), lambda i, w: (0, w[which], 0, 0))
 
 
-def ordered(kernel, which_ref, after_ref, *refs):
+def ordered(kernel, which_ref, after_ref, also_ref, *refs):
     kernel(which_ref, *refs)
 
 
 def chunk_call(
     kernel, name, which, part, turned, grads, after, extra, extra_specs, out_specs, out_shape
 ):
+    after = after if isinstance(after, tuple) else (after, after)
     tokens, columns = grads[0].shape
     half = pl.BlockSpec((tokens, columns // 2), lambda i, w: (0, i))
     chunks = which.shape[0]
@@ -364,7 +366,7 @@
         grid_spec=pltpu.PrefetchScalarGridSpec(
             num_scalar_prefetch=1,
             grid=(2,),
-            in_specs=[pl.BlockSpec(memory_space=pl.ANY)]
+            in_specs=[pl.BlockSpec(memory_space=pl.ANY)] * 2
             + turned_specs
             + [half, half]
             + extra_specs,
@@ -374,39 +376,27 @@
         compiler_params=pltpu.CompilerParams(vmem_limit_bytes=VMEM),
         cost_estimate=small_cost(),
         name=name,
-    )(which, after, *turned_args, *grads, *extra)
-
-
-def far_kernel(which_ref, near_ref, far_ref, own_ref, other_ref, note_ref, a_ref, b_ref, out_ref):
+    )(which, *after, *turned_args, *grads, *extra)
+
+
+def far_kernel(which_ref, near_ref, far_ref, own_ref, other_ref, a_ref, b_ref):
     total = product(near_ref, far_ref, own_ref, other_ref).astype(BF16)
 
     @pl.when(pl.program_id(0) == 0)
     def _():
         a_ref[...] = total
-        out_ref[...] = note_ref[...]
 
     @pl.when(pl.program_id(0) == 1)
     def _():
         b_ref[...] = total
 
 
-def far_chunk(which, part, turned, grads, after, note):
+def far_chunk(which, part, turned, grads, after):
     rows, columns = SIDE * 128, grads[0].shape[1] // 2
     half = jax.ShapeDtypeStruct((rows, columns), BF16)
-    note_spec = pl.BlockSpec((8, 128), lambda i, w: (0, 0))
     half_spec = pl.BlockSpec((rows, columns), lambda i, w: (0, 0))
     return chunk_call(
-        far_kernel,
-        "far_chunk",
-        which,
-        part,
-        turned,
-        grads,
-        after,
-        [note],
-        [note_spec],
-        [half_spec, half_spec, note_spec],
-        [half, half, jax.ShapeDtypeStruct((8, 128), F32)],
+        far_kernel, "far_chunk", which, part, turned, grads, after, [], [], [half_spec] * 2, [half] * 2
     )
 
 
@@ -452,7 +442,7 @@
     )
 
 
-def total_kernel(which_ref, after_ref, own_ref, up_ref, down_ref, *out_refs):
+def total_kernel(which_ref, after_ref, also_ref, own_ref, up_ref, down_ref, *out_refs):
     total = own_ref[...].astype(F32) + up_ref[...].astype(F32) + down_ref[...].astype(F32)
     for step, ref in enumerate(out_refs):
 
@@ -471,14 +461,14 @@
         grid_spec=pltpu.PrefetchScalarGridSpec(
             num_scalar_prefetch=1,
             grid=(SIDE,),
-            in_specs=[pl.BlockSpec(memory_space=pl.ANY)] + [block] * 3,
+            in_specs=[pl.BlockSpec(memory_space=pl.ANY)] * 2 + [block] * 3,
             out_specs=[out] * SIDE,
         ),
         out_shape=[jax.ShapeDtypeStruct((2, 128, columns), BF16)] * SIDE,
         compiler_params=pltpu.CompilerParams(vmem_limit_bytes=VMEM),
         cost_estimate=small_cost(),
         name="totals",
-    )(first.reshape(1), after, cut(own), cut(up), cut(down))
+    )(first.reshape(1), *after, cut(own), cut(up), cut(down))
 
 
 def gather_terms(refs):
@@ -496,7 +486,7 @@
         in_specs=[pl.BlockSpec(memory_space=pl.ANY)] + [block] * len(pieces),
         out_specs=block,
         out_shape=jax.ShapeDtypeStruct(pieces[0].shape, BF16),
-        compiler_params=pltpu.CompilerParams(vmem_limit_bytes=16 << 20),
+        compiler_params=pltpu.CompilerParams(vmem_limit_bytes=VMEM),
         cost_estimate=small_cost(),
         name="first_half",
     )(after, *pieces)
@@ -541,21 +531,9 @@
     )(after, a, b)
 
 
-def add_kernel(after_ref, a_ref, b_ref, o_ref):
-    o_ref[...] = (a_ref[...].astype(F32) + b_ref[...].astype(F32)).astype(BF16)
-
-
 def add_after(after, a, b):
-    block = pl.BlockSpec(a.shape, lambda: (0, 0))
-    return pl.pallas_call(
-        add_kernel,
-        in_specs=[pl.BlockSpec(memory_space=pl.ANY), block, block],
-        out_specs=block,
-        out_shape=jax.ShapeDtypeStruct(a.shape, BF16),
-        compiler_params=pltpu.CompilerParams(vmem_limit_bytes=8 << 20),
-        cost_estimate=small_cost(),
-        name="add_after",
-    )(after, a, b)
+    a, after = lax.optimization_barrier((a, after))
+    return add(a, b)
 
 
 def gap_kernel(heads_rows, rank_ref, aux_ref, m1_ref, m2_ref, m3_ref, part_ref, gate_ref, keep_ref, give_ref):
@@ -609,6 +587,40 @@
 
 def add(*terms):
     return sum(t.astype(F32) for t in terms).astype(BF16)
+
+
+def join_kernel(low_ref, after_ref, own_ref, far_ref, o_ref):
+    rows = own_ref.shape[0]
+    low = low_ref[0] == 1
+    own, far = own_ref[...], far_ref[...]
+    o_ref[:rows] = jnp.where(low, own, far)
+    o_ref[rows:] = jnp.where(low, far, own)
+
+
+def joined(after, block, far, bit, rank):
+    rows, columns = block.shape
+    low = ((rank & bit) == 0).astype(jnp.int32).reshape(1)
+    half = pl.BlockSpec((rows, columns), lambda i, r: (0, 0))
+    return pl.pallas_call(
+        join_kernel,
+        grid_spec=pltpu.PrefetchScalarGridSpec(
+            num_scalar_prefetch=1,
+            grid=(1,),
+            in_specs=[pl.BlockSpec(memory_space=pl.ANY), half, half],
+            out_specs=pl.BlockSpec((2 * rows, columns), lambda i, r: (0, 0)),
+        ),
+        out_shape=jax.ShapeDtypeStruct((2 * rows, columns), block.dtype),
+        compiler_params=pltpu.CompilerParams(vmem_limit_bytes=VMEM),
+        cost_estimate=small_cost(),
+        name="join",
+    )(low, after, block, far)
+
+
+def doubled(block, axis, bit, rank):
+    size = lax.axis_size(axis)
+    far = lax.ppermute(block, axis, [(i, i ^ bit) for i in range(size)])
+    low = (rank & bit) == 0
+    return jnp.concatenate([jnp.where(low, block, far), jnp.where(low, far, block)])
 
 
 def on_device(
@@ -700,7 +712,7 @@
     )
     stats_all = lax.all_to_all(stats, "enc", split_axis=0, concat_axis=0, tiled=True)
     flat_a, norms, aux = back_first(
-        ret_parts, own_question, own_blocks, enc_rank, order_row, key_value, gathered, stats_all
+        (ret_parts, other), own_question, own_blocks, enc_rank, order_row, key_value, gathered, stats_all
     )
     far_a = lax.ppermute(flat_a, "ret", swap)
     flat_b = back_second(own_question, own_blocks, key_value, gathered, norms)
@@ -717,53 +729,45 @@
         far = lax.ppermute(half, "enc", [(i, i ^ bit) for i in range(N_ENC)])
         return add_after(after, half, far)
 
-    a, b, aux = far_chunk(steps(0, 2), 0, turned, grads[0], norms, aux)
-    came = [(send(a, 0, 1), send(b, 0, -1))]
     masses = [
         lax.ppermute(aux, "dec", [(i, (i + step) % N_DEC) for i in range(N_DEC)])
         for step in range(1, N_DEC)
     ]
-    a, b, late_aux = far_chunk(steps(1, 2), 1, turned, grads[1], a, aux)
+    keep, give = apply_gap(
+        ret_rank, aux, masses, ret_parts, N_DEC * heads * query_len, flat_b
+    )
+    half = add(keep, lax.ppermute(give, "ret", swap))
+    a, b = far_chunk(steps(0, 2), 0, turned, grads[0], half)
+    came = [(send(a, 0, 1), send(b, 0, -1))]
+    half = level(a, half, 1)
+    a, b = far_chunk(steps(1, 2), 1, turned, grads[1], half)
     came.append((send(a, 1, 1), send(b, 1, -1)))
-    keep, give = apply_gap(
-        ret_rank, late_aux, masses, ret_parts, N_DEC * heads * query_len, a
-    )
-    own = [own_chunk(steps(0, 0), 0, turned, grads[0], give)]
-    half = add_after(own[0], keep, lax.ppermute(give, "ret", swap))
+    half = level(a, half, 4)
     up, down = side_chunks(steps(0, 1, 3), 0, turned, grads[0], half, came[0])
     sent = [(send(up, 0, 1), send(down, 0, -1))]
-    half = level(up, half, 4)
+    half = level(up, half, 8)
     up, down = side_chunks(steps(1, 1, 3), 1, turned, grads[1], half, came[1])
     sent.append((send(up, 1, 1), send(down, 1, -1)))
-    half = level(up, half, 1)
-    own.append(own_chunk(steps(1, 0), 1, turned, grads[1], half))
-    half = level(own[1], half, 8)
-    by_tokens = by_token(half, flat_a, flat_b)
-    kv_grad = by_tokens.reshape(pass_dev, 1, slot_len, heads, pair_width)
-    half = level(by_tokens, half, 2)
-    pieces, last = [], half
+    half = level(up, half, 2)
+    own = [own_chunk(steps(0, 0), 0, turned, grads[0], up)]
+    own.append(own_chunk(steps(1, 0), 1, turned, grads[1], own[0]))
+    quarter = doubled(half, "ret", 1, ret_rank)
+    far = lax.ppermute(quarter, "dec", [(i, i ^ 1) for i in range(N_DEC)])
+    pieces, last = [], (own[1], own[1])
     for part in range(2):
         cuts = totals(at[1 - part], last, own[part], *sent[part])
         pieces.append([cuts[0]] + [send(cuts[k], 1 - part, k) for k in range(1, SIDE)])
-        last = cuts[0]
-    summed = first_half(cuts[0], pieces[0])
+        if part == 0:
+            ret_half = joined(cuts[0], quarter, far, 1, dec_rank)
+        last = (cuts[0], ret_half)
+    ret_weight_grad = doubled(ret_half, "dec", 2, dec_rank)
+    kv_grad = by_token(cuts[0], flat_a, flat_b).reshape(
+        pass_dev, 1, slot_len, heads, pair_width
+    )
+    summed = first_half(ret_weight_grad, pieces[0])
     weight_total = finish(summed, pieces[1])
 
-    half_far = lax.ppermute(half, "ret", swap)
-    quarter = jnp.where(
-        ret_rank == 0, jnp.stack([half, half_far]), jnp.stack([half_far, half])
-    ).reshape(share, ret_width)
-    ret_weight_grad = jnp.zeros((N_DEC, share, ret_width), BF16)
-    for step in range(N_DEC):
-        piece = quarter
-        if step:
-            piece = lax.ppermute(
-                quarter, "dec", [(i, (i + step) % N_DEC) for i in range(N_DEC)]
-            )
-        ret_weight_grad = lax.dynamic_update_index_in_dim(
-            ret_weight_grad, piece, (dec_rank - step) % N_DEC, 0
-        )
-    return (kv_grad, weight_total, ret_weight_grad.reshape(ret_width, ret_width))
+    return (kv_grad, weight_total, ret_weight_grad)
 
 
 def solution(mesh):

time: 200 us -> 196 us (0.980)
  local copies, waits for them, and re-layouts: 25 us -> 15.8 us
  other arithmetic: 1.36 us -> 7.35 us
  starting transfers between devices: 50.9 us -> 46.8 us
  Pallas kernels: 84 us -> 87.5 us
    ppermute x14, waiting for transfers between devices: 2.12 us -> 16.7 us  [send(): return lax.ppermute(value, 'enc', ring_pairs(axis, step))]
    ppermute x4, waiting for transfers between devices: 9.04 us -> 0.27 us  [level(): far = lax.ppermute(half, 'enc', [(i, i ^ bit) for i in range(N_ENC)])]
    ppermute x5 -> x4, waiting for transfers between devices: 10.2 us -> 1.59 us  [the longest x1 1.58 us: on_device(): half = add(keep, lax.ppermute(give, 'ret', swap))]
    unnamed x96 -> x84, local copies, waits for them, and re-layouts: 21 us -> 13.9 us
    ppermute x14, starting transfers between devices: 24 us -> 19.1 us  [send(): return lax.ppermute(value, 'enc', ring_pairs(axis, step))]
    convert_element_type x0 -> x5, other arithmetic: none -> 4.78 us  [add(): return sum((t.astype(F32) for t in terms)).astype(BF16)]
    ppermute x3, waiting for transfers between devices: 0.01 us -> 2.56 us  [on_device(): lax.ppermute(aux, 'dec', [(i, (i + step) % N_DEC) for i in range(N_DEC)])]
    dynamic_update_slice x4 -> x0, local copies, waits for them, and re-layouts: 2.02 us -> none  [on_device(): lax.dynamic_update_index_in_dim(ret_weight_grad, piece, (dec_rank - step)...]
  transfers between devices with their start and end apart: 31 -> 30, of which waited for: 7 -> 12; matrix products, arithmetic and copies ran while one was open for 5% -> 7% of each run, Pallas kernels for 35% -> 35%
where the time goes in v4:
time: 196 us; the launch traced here: 195 us
  Pallas kernels  87.5 us (45%)
  starting transfers between devices  46.8 us (24%)
  waiting for transfers between devices  30.1 us (15%)
  local copies, waits for them, and re-layouts  15.8 us (8%)
  other arithmetic  7.35 us (4%)
  matrix products  6.02 us (3%)
    pallas_call x6, Pallas kernels, chunk_call(): pl.pallas_call(functools.partial(ordered, kernel), grid_spec=pltpu.Prefet...  28.1 us
    ppermute x14, starting transfers between devices, send(): return lax.ppermute(value, 'enc', ring_pairs(axis, step))  19.1 us
    ppermute x14, waiting for transfers between devices, send(): return lax.ppermute(value, 'enc', ring_pairs(axis, step))  16.7 us
    pallas_call x1, Pallas kernels, project(): pl.pallas_call(project_kernel, grid=(width // depth,), out_shape=jax.Shap...  16.2 us
    unnamed x84, local copies, waits for them, and re-layouts  13.9 us
    all_to_all x1, waiting for transfers between devices, on_device(): lax.all_to_all(stats, 'enc', split_axis=0, concat_axis=0, tiled=True)  8.99 us
    pallas_call x2, Pallas kernels, totals(): pl.pallas_call(total_kernel, grid_spec=pltpu.PrefetchScalarGridSpec(num_s...  7.83 us
    all_to_all x1, starting transfers between devices, on_device(): lax.all_to_all(stats, 'enc', split_axis=0, concat_axis=0, tiled=True)  7.22 us
  transfers between devices with their start and end apart: 30, of which 12 were waited for; matrix products, arithmetic and copies ran while one was open for 7% of the time, Pallas kernels for 35%

profile of v4, /device:TPU:0, one launch (start us, length us, event | category | flops | bytes accessed | tf_op | source)
XLA Modules:
  0.0 194.5 jit_solution(16373816818972588587)
XLA Ops:
  3.9 2.9 %pack.1 = bf16[32,128,128]{2,1,0:T(8,128)(2,1)} custom-call(s32[32]{0:T(128)} %bitcast.65, bf16[512,64]{1,0:T(8,128)(2,1)} %bitcast.61, bf16[512,64]{1,0:T(8,128)(2,1)} %bitcast.62), custom_call_target="tpu_custom_call" | custom-call | flops 1024 | bytes 1024 | tf_op jit(solution)/shard_map/pack/pallas_call | solution.py:46
  6.9 7.1 %all-to-all-start = ((bf16[16,256,128]{2,1,0:T(8,128)(2,1)}), bf16[16,256,128]{2,1,0:T(8,128)(2,1)S(1)}, u32[]{:S(2)}, u32[]{:S(2)}) async-start(bf16[16,256,128]{2,1,0:T(8,128)(2,1)} %bitcast.57), calls=%async_computation | async-start | bytes 2097152 | tf_op jit(solution)/shard_map/all_to_all | solution.py:650
  14.4 16.2 %project.1.kv_ref = f32[16,512,128]{2,1,0:T(8,128)} custom-call(bf16[512,4096]{1,0:T(8,128)(2,1)} %bitcast.54, bf16[4096,16,128]{2,1,0:T(8,128)(2,1)} %w_ref.1), custom_call_target="tpu_custom_call" | custom-call | flops 1024 | bytes 1024 | tf_op jit(solution)/shard_map/project/pallas_call | solution.py:78
  30.8 2.2 %select_reduce_fusion = (f32[2,768]{1,0:T(2,128)S(1)}, f32[2,256,768]{2,1,0:T(8,128)}) fusion(pred[2,256]{1,0:T(4,128)(4,1)S(1)} %iota_compare_fusion, bf16[768,768]{1,0:T(8,128)(2,1)S(1)} %copy-done, bf16[2,1,256,768]{3,2,1,0:T(8,128)(2,1)S(1)} %copy-done.26), kind=kOutput, calls=%fused_computation.14 | convolution fusion | flops 607910400 | bytes 3545600 | tf_op jit(solution)/shard_map/dot_general | solution.py:682
  34.2 5.7 %local_stats.1 = (f32[16,72,128]{2,1,0:T(8,128)}, f32[2,768]{1,0:T(2,128)}) custom-call(s32[2]{0:T(128)} %copy-done.30, s32[2]{0:T(128)} %copy-done.29, f32[16,512,128]{2,1,0:T(8,128)} %project.1.kv_ref, bf16[16,256,128]{2,1,0:T(8,128)(2,1)} %copy-done.3, f32[8,128]{1,0:T(8,128)} %broadcast_in_dim.86.score_ref, f32[2,768]{1,0:T(2,128)} %copy-done.27), custom_call_target="tpu_custom_call" | custom-call | flops 1024 | bytes 1024 | tf_op jit(solution)/shard_map/local_stats/pallas_call | solution.py:179
  40.0 4.2 %turn.1 = (bf16[16,128,512]{2,1,0:T(8,128)(2,1)}, bf16[16,128,512]{2,1,0:T(8,128)(2,1)}) custom-call(s32[1]{0:T(128)} %bitcast.2.rank_ref, f32[16,72,128]{2,1,0:T(8,128)} %get-tuple-element.33.after_ref, bf16[512,4096]{1,0:T(8,128)(2,1)} %bitcast.55), custom_call_target="tpu_custom_call" | custom-call | bytes 67108864 | tf_op jit(solution)/shard_map/turn/pallas_call | solution.py:105
  45.3 7.2 %all-to-all-start.1 = ((f32[16,72,128]{2,1,0:T(8,128)}), f32[16,72,128]{2,1,0:T(8,128)S(1)}, u32[]{:S(2)}, u32[]{:S(2)}) async-start(f32[16,72,128]{2,1,0:T(8,128)} %get-tuple-element.33.after_ref), calls=%async_computation.1 | async-start | bytes 1179648 | tf_op jit(solution)/shard_map/all_to_all | solution.py:713
  52.7 3.8 %fusion.13.after_ref.part_ref = f32[2,192,768]{2,1,0:T(8,128)} fusion(bf16[2,256,192]{2,1,0:T(8,128)(2,1)S(1)} %bitcast.63, f32[2,256,768]{2,1,0:T(8,128)} %get-tuple-element.79, f32[2,768]{1,0:T(2,128)S(1)} %broadcast_divide_fusion, pred[2,256]{1,0:T(4,128)(4,1)S(1)} %iota_compare_fusion), kind=kOutput, calls=%fused_computation.19 | convolution fusion | flops 159252480 | bytes 2955776 | tf_op jit(solution)/shard_map/dot_general | solution.py:707
  56.5 9.0 %all-to-all-done.1.stats_ref = f32[16,72,128]{2,1,0:T(8,128)S(1)} async-done(((f32[16,72,128]{2,1,0:T(8,128)}), f32[16,72,128]{2,1,0:T(8,128)S(1)}, u32[]{:S(2)}, u32[]{:S(2)}) %all-to-all-start.1) | async-done | bytes 589856 | tf_op jit(solution)/shard_map/all_to_all | solution.py:713
  67.0 5.2 %back_first.1 = (bf16[512,1024]{1,0:T(8,128)(2,1)}, f32[4,16,128]{2,1,0:T(8,128)}, f32[8,128]{1,0:T(8,128)}) custom-call(s32[2]{0:T(128)} %copy-done.30, s32[2]{0:T(128)} %copy-done.29, s32[1]{0:T(128)} %bitcast.5.own_ref, s32[32]{0:T(128)} %bitcast.66, f32[2,192,768]{2,1,0:T(8,128)} %fusion.13.after_ref.part_ref, bf16[16,128,512]{2,1,0:T(8,128)(2,1)} %copy-done.2, ...), custom_call_target="tpu_custom_call" | custom-call | bytes 33554432 | tf_op jit(solution)/shard_map/back_first/pallas_call | solution.py:292
  72.2 4.8 %back_second.1.gate_ref.refs_2_.refs_4_.b_ref = bf16[512,1024]{1,0:T(8,128)(2,1)} custom-call(s32[2]{0:T(128)} %copy-done.30, s32[2]{0:T(128)} %copy-done.29, f32[16,512,128]{2,1,0:T(8,128)} %project.1.kv_ref, bf16[16,256,128]{2,1,0:T(8,128)(2,1)} %copy-done.3, f32[4,16,128]{2,1,0:T(8,128)} %get-tuple-element.36.norm_ref), custom_call_target="tpu_custom_call" | custom-call | bytes 33554432 | tf_op jit(solution)/shard_map/back_second/pallas_call | solution.py:319
  79.6 3.5 %collective-permute-start.2 = (f32[8,128]{1,0:T(8,128)S(1)}, f32[8,128]{1,0:T(8,128)S(1)}, u32[]{:S(2)}, u32[]{:S(2)}) collective-permute-start(f32[8,128]{1,0:T(8,128)S(1)} %copy-done.32), channel_id=1, source_target_pairs={{0,4},{2,6},{4,0},{6,2},{1,5},{3,7},{5,1},{7,3},{8,12},{10,14},{12... | collective-permute-start | bytes 12296 | tf_op jit(solution)/shard_map/ppermute | solution.py:733
  87.3 2.1 %apply_gap.1 = (f32[96,768]{1,0:T(8,128)}, bf16[96,768]{1,0:T(8,128)(2,1)}) custom-call(s32[1]{0:T(128)} %bitcast.2.rank_ref, f32[8,128]{1,0:T(8,128)} %get-tuple-element.35.aux_ref, f32[8,128]{1,0:T(8,128)} %copy-done.33, f32[8,128]{1,0:T(8,128)} %copy-done.34, f32[8,128]{1,0:T(8,128)} %copy-done.35, f32[2,192,768]{2,1,0:T(8,128)} %fusion.13.after_ref.part_ref, ...), custom_call_target="tpu_custom_call" | custom-call | flops 1024 | bytes 1024 | tf_op jit(solution)/shard_map/apply_gap/pallas_call | solution.py:556
  93.9 4.1 %far_chunk.2 = (bf16[512,512]{1,0:T(8,128)(2,1)}, bf16[512,512]{1,0:T(8,128)(2,1)}) custom-call(s32[1]{0:T(128)S(6)} %select_n.102.which_ref, bf16[96,768]{1,0:T(8,128)(2,1)} %copy-done.11, bf16[96,768]{1,0:T(8,128)(2,1)} %copy-done.11, bf16[4,4,128,512]{3,2,1,0:T(8,128)(2,1)} %bitcast.45, bf16[4,4,128,512]{3,2,1,0:T(8,128)(2,1)} %bitcast.37, ...), custom_call_target="tpu_custom_call" | custom-call | flops 1024 | bytes 1024 | tf_op jit(solution)/shard_map/far_chunk/pallas_call | solution.py:364
  103.6 4.1 %far_chunk.3 = (bf16[512,512]{1,0:T(8,128)(2,1)}, bf16[512,512]{1,0:T(8,128)(2,1)}) custom-call(s32[1]{0:T(128)S(6)} %select_n.103.which_ref, bf16[96,768]{1,0:T(8,128)(2,1)} %copy-done.8, bf16[96,768]{1,0:T(8,128)(2,1)} %copy-done.8, bf16[4,4,128,512]{3,2,1,0:T(8,128)(2,1)} %bitcast.46, bf16[4,4,128,512]{3,2,1,0:T(8,128)(2,1)} %bitcast.38, ...), custom_call_target="tpu_custom_call" | custom-call | flops 1024 | bytes 1024 | tf_op jit(solution)/shard_map/far_chunk/pallas_call | solution.py:364
  108.8 2.0 %collective-permute-start.13 = (bf16[512,512]{1,0:T(8,128)(2,1)}, bf16[512,512]{1,0:T(8,128)(2,1)S(1)}, u32[]{:S(2)}, u32[]{:S(2)}) collective-permute-start(bf16[512,512]{1,0:T(8,128)(2,1)} %get-tuple-element.48), channel_id=1, source_target_pairs={{0,24},{8,0},{16,8},{24,16},{32,56},{40,32},{48,40},{56,48},{64,88... | collective-permute-start | bytes 1572872 | tf_op jit(solution)/shard_map/ppermute | solution.py:585
  114.9 2.4 %collective-permute-done.10.refs_7_ = bf16[512,512]{1,0:T(8,128)(2,1)S(1)} collective-permute-done((bf16[512,512]{1,0:T(8,128)(2,1)}, bf16[512,512]{1,0:T(8,128)(2,1)S(1)}, u32[]{:S(2)}, u32[]{:S(2)}) %collective-permute-start.10) | collective-permute-done | bytes 524320 | tf_op jit(solution)/shard_map/ppermute | solution.py:585
  118.1 6.2 %side_chunks.2 = (bf16[2,512,512]{2,1,0:T(8,128)(2,1)}, bf16[2,512,512]{2,1,0:T(8,128)(2,1)}) custom-call(s32[2]{0:T(128)} %get-tuple-element.76.which_ref, bf16[96,768]{1,0:T(8,128)(2,1)} %copy-done.10, bf16[96,768]{1,0:T(8,128)(2,1)} %copy-done.10, bf16[4,4,128,512]{3,2,1,0:T(8,128)(2,1)} %bitcast.47, bf16[4,4,128,512]{3,2,1,0:T(8,128)(2,1)} %bitcast.39, ...), custom_call_target="tpu_custom_call" | custom-call | flops 1024 | bytes 1024 | tf_op jit(solution)/shard_map/side_chunks/pallas_call | solution.py:364
  126.9 2.8 %collective-permute-start.15 = (bf16[2,512,512]{2,1,0:T(8,128)(2,1)}, bf16[2,512,512]{2,1,0:T(8,128)(2,1)}, u32[]{:S(2)}, u32[]{:S(2)}) collective-permute-start(bf16[2,512,512]{2,1,0:T(8,128)(2,1)} %get-tuple-element.50), channel_id=1, source_target_pairs={{0,96},{8,104},{16,112},{24,120},{32,0},{40,8},{48,16},{56,24},{64... | collective-permute-start | bytes 3145736 | tf_op jit(solution)/shard_map/ppermute | solution.py:585
  130.7 6.2 %side_chunks.3 = (bf16[2,512,512]{2,1,0:T(8,128)(2,1)}, bf16[2,512,512]{2,1,0:T(8,128)(2,1)}) custom-call(s32[2]{0:T(128)} %get-tuple-element.77.which_ref, bf16[96,768]{1,0:T(8,128)(2,1)} %copy-done.9, bf16[96,768]{1,0:T(8,128)(2,1)} %copy-done.9, bf16[4,4,128,512]{3,2,1,0:T(8,128)(2,1)} %bitcast.49, bf16[4,4,128,512]{3,2,1,0:T(8,128)(2,1)} %bitcast.41, ...), custom_call_target="tpu_custom_call" | custom-call | flops 1024 | bytes 1024 | tf_op jit(solution)/shard_map/side_chunks/pallas_call | solution.py:364
  138.5 2.7 %collective-permute-start.20 = (bf16[2,512,512]{2,1,0:T(8,128)(2,1)}, bf16[2,512,512]{2,1,0:T(8,128)(2,1)}, u32[]{:S(2)}, u32[]{:S(2)}) collective-permute-start(bf16[2,512,512]{2,1,0:T(8,128)(2,1)} %get-tuple-element.53), channel_id=1, source_target_pairs={{0,24},{8,0},{16,8},{24,16},{32,56},{40,32},{48,40},{56,48},{64,88... | collective-permute-start | bytes 3145736 | tf_op jit(solution)/shard_map/ppermute | solution.py:585
  141.8 3.8 %own_chunk.2.after_ref.also_ref = bf16[2,512,512]{2,1,0:T(8,128)(2,1)} custom-call(s32[1]{0:T(128)S(6)} %select_n.93.which_ref, bf16[2,512,512]{2,1,0:T(8,128)(2,1)} %get-tuple-element.49.after_ref.also_ref, bf16[2,512,512]{2,1,0:T(8,128)(2,1)} %get-tuple-element.49.after_ref.also_ref, bf16[4,4,128,512]{3,2,1,0:T(8,128)(2,1)} %bitcast.51, ...), custom_call_target="tpu_custom_call" | custom-call | flops 1024 | bytes 1024 | tf_op jit(solution)/shard_map/own_chunk/pallas_call | solution.py:364
  145.6 3.8 %own_chunk.3.after_ref.also_ref = bf16[2,512,512]{2,1,0:T(8,128)(2,1)} custom-call(s32[1]{0:T(128)S(6)} %select_n.92.which_ref, bf16[2,512,512]{2,1,0:T(8,128)(2,1)} %own_chunk.2.after_ref.also_ref, bf16[2,512,512]{2,1,0:T(8,128)(2,1)} %own_chunk.2.after_ref.also_ref, bf16[4,4,128,512]{3,2,1,0:T(8,128)(2,1)} %bitcast.52, bf16[4,4,128,512]{3,2,1,0:T(8,128)(2,1)} %bitcast.44, ...), custom_call_target="tpu_custom_call" | custom-call | flops 1024 | bytes 1024 | tf_op jit(solution)/shard_map/own_chunk/pallas_call | solution.py:364
  151.5 3.9 %totals.2 = (bf16[2,128,512]{2,1,0:T(8,128)(2,1)}, bf16[2,128,512]{2,1,0:T(8,128)(2,1)}, bf16[2,128,512]{2,1,0:T(8,128)(2,1)}, bf16[2,128,512]{2,1,0:T(8,128)(2,1)}) custom-call(s32[1]{0:T(128)} %bitcast.1.which_ref, bf16[2,512,512]{2,1,0:T(8,128)(2,1)} %own_chunk.3.after_ref.also_ref, bf16[2,512,512]{2,1,0:T(8,128)(2,1)} %own_chunk.3.after_ref.also_ref, ...), custom_call_target="tpu_custom_call" | custom-call | flops 1024 | bytes 1024 | tf_op jit(solution)/shard_map/totals/pallas_call | solution.py:459
  158.1 2.2 %collective-permute-start.21 = (bf16[384,768]{1,0:T(8,128)(2,1)}, bf16[384,768]{1,0:T(8,128)(2,1)S(1)}, u32[]{:S(2)}, u32[]{:S(2)}) collective-permute-start(bf16[384,768]{1,0:T(8,128)(2,1)} %join.1.also_ref), channel_id=1, source_target_pairs={{0,4},{2,6},{4,0},{6,2},{1,5},{3,7},{5,1},{7,3},{8,12},{10,14},{12... | collective-permute-start | bytes 1769480 | tf_op jit(solution)/shard_map/ppermute | solution.py:621
  160.7 4.7 %collective-permute-done.19 = bf16[2,512,512]{2,1,0:T(8,128)(2,1)S(1)} collective-permute-done((bf16[2,512,512]{2,1,0:T(8,128)(2,1)}, bf16[2,512,512]{2,1,0:T(8,128)(2,1)S(1)}, u32[]{:S(2)}, u32[]{:S(2)}) %collective-permute-start.19) | collective-permute-done | bytes 1048608 | tf_op jit(solution)/shard_map/ppermute | solution.py:585
  166.4 3.9 %totals.3 = (bf16[2,128,512]{2,1,0:T(8,128)(2,1)}, bf16[2,128,512]{2,1,0:T(8,128)(2,1)}, bf16[2,128,512]{2,1,0:T(8,128)(2,1)}, bf16[2,128,512]{2,1,0:T(8,128)(2,1)}) custom-call(s32[1]{0:T(128)} %bitcast.which_ref, bf16[2,128,512]{2,1,0:T(8,128)(2,1)} %get-tuple-element.51.after_ref.refs_0_, bf16[384,768]{1,0:T(8,128)(2,1)} %join.1.also_ref, ...), custom_call_target="tpu_custom_call" | custom-call | flops 1024 | bytes 1024 | tf_op jit(solution)/shard_map/totals/pallas_call | solution.py:459
  170.2 4.0 %by_token.1 = bf16[512,16,128]{2,1,0:T(8,128)(2,1)} custom-call(bf16[2,128,512]{2,1,0:T(8,128)(2,1)} %get-tuple-element.54.after_ref.refs_0_, bf16[512,1024]{1,0:T(8,128)(2,1)} %get-tuple-element.40.refs_2_.refs_4_.a_ref, bf16[512,1024]{1,0:T(8,128)(2,1)} %back_second.1.gate_ref.refs_2_.refs_4_.b_ref), custom_call_target="tpu_custom_call" | custom-call | flops 1024 | bytes 1024 | tf_op jit(solution)/shard_map/by_token/pallas_call | solution.py:522
  181.1 2.1 %collective-permute-done.23.refs_2_ = bf16[2,128,512]{2,1,0:T(8,128)(2,1)S(1)} collective-permute-done((bf16[2,128,512]{2,1,0:T(8,128)(2,1)S(1)}, bf16[2,128,512]{2,1,0:T(8,128)(2,1)S(1)}, u32[]{:S(2)}, u32[]{:S(2)}) %collective-permute-start.23) | collective-permute-done | bytes 262176 | tf_op jit(solution)/shard_map/ppermute | solution.py:585
  183.2 4.8 %collective-permute-done.24.refs_3_ = bf16[2,128,512]{2,1,0:T(8,128)(2,1)S(1)} collective-permute-done((bf16[2,128,512]{2,1,0:T(8,128)(2,1)S(1)}, bf16[2,128,512]{2,1,0:T(8,128)(2,1)S(1)}, u32[]{:S(2)}, u32[]{:S(2)}) %collective-permute-start.24) | collective-permute-done | bytes 262176 | tf_op jit(solution)/shard_map/ppermute | solution.py:585
  188.7 2.0 %first_half.1.first_ref = bf16[2,128,512]{2,1,0:T(8,128)(2,1)} custom-call(bf16[768,768]{1,0:T(8,128)(2,1)} %pad_maximum_fusion.after_ref, bf16[2,128,512]{2,1,0:T(8,128)(2,1)} %get-tuple-element.51.after_ref.refs_0_, bf16[2,128,512]{2,1,0:T(8,128)(2,1)} %copy-done.20, bf16[2,128,512]{2,1,0:T(8,128)(2,1)} %copy-done.22, bf16[2,128,512]{2,1,0:T(8,128)(2,1)} %copy-done.24), custom_call_target="tpu_custom_call" | custom-call | flops 1024 | bytes 1024 | tf_op jit(solution)/shard_map/first_half/pallas_call | solution.py:484
  192.3 2.3 %finish.1 = bf16[128,16,128]{2,1,0:T(8,128)(2,1)} custom-call(bf16[2,128,512]{2,1,0:T(8,128)(2,1)} %first_half.1.first_ref, bf16[2,128,512]{2,1,0:T(8,128)(2,1)} %get-tuple-element.54.after_ref.refs_0_, bf16[2,128,512]{2,1,0:T(8,128)(2,1)} %copy-done.21, bf16[2,128,512]{2,1,0:T(8,128)(2,1)} %copy-done.23, bf16[2,128,512]{2,1,0:T(8,128)(2,1)} %copy-done.25), custom_call_target="tpu_custom_call" | custom-call | flops 1024 | bytes 1024 | tf_op jit(solution)/shard_map/finish/pallas_call | solution.py:505
  (155 shorter events, 51.3 us)
Async XLA Ops:
  0.6 30.2 %copy-start = (bf16[768,768]{1,0:T(8,128)(2,1)S(1)}, bf16[768,768]{1,0:T(8,128)(2,1)}, u32[]{:S(2)}) copy-start(bf16[768,768]{1,0:T(8,128)(2,1)} %param.22) | copy-start | bytes 3538948
  6.9 26.4 %all-to-all-start = ((bf16[16,256,128]{2,1,0:T(8,128)(2,1)}), bf16[16,256,128]{2,1,0:T(8,128)(2,1)S(1)}, u32[]{:S(2)}, u32[]{:S(2)}) async-start(bf16[16,256,128]{2,1,0:T(8,128)(2,1)} %bitcast.57), calls=%async_computation | async-start | bytes 2097152 | tf_op jit(solution)/shard_map/all_to_all | solution.py:650
  14.4 16.4 %copy-start.26 = (bf16[2,1,256,768]{3,2,1,0:T(8,128)(2,1)S(1)}, bf16[2,1,256,768]{3,2,1,0:T(8,128)(2,1)}, u32[]{:S(2)}) copy-start(bf16[2,1,256,768]{3,2,1,0:T(8,128)(2,1)} %param.21) | copy-start | bytes 2359300
  44.2 21.3 %collective-permute-start = (bf16[16,128,512]{2,1,0:T(8,128)(2,1)}, bf16[16,128,512]{2,1,0:T(8,128)(2,1)S(1)}, u32[]{:S(2)}, u32[]{:S(2)}) collective-permute-start(bf16[16,128,512]{2,1,0:T(8,128)(2,1)} %get-tuple-element.34), channel_id=1, source_target_pairs={{0,1},{1,0},{2,3},{3,2},{4,5},{5,4},{6,7},{7,6},{8,9},{9,8},{10,11... | collective-permute-start | bytes 6291464 | tf_op jit(solution)/shard_map/ppermute | solution.py:700
  45.3 20.1 %all-to-all-start.1 = ((f32[16,72,128]{2,1,0:T(8,128)}), f32[16,72,128]{2,1,0:T(8,128)S(1)}, u32[]{:S(2)}, u32[]{:S(2)}) async-start(f32[16,72,128]{2,1,0:T(8,128)} %get-tuple-element.33.after_ref), calls=%async_computation.1 | async-start | bytes 1179648 | tf_op jit(solution)/shard_map/all_to_all | solution.py:713
  72.2 20.7 %collective-permute-start.5 = (bf16[512,1024]{1,0:T(8,128)(2,1)}, bf16[512,1024]{1,0:T(8,128)(2,1)S(1)}, u32[]{:S(2)}, u32[]{:S(2)}) collective-permute-start(bf16[512,1024]{1,0:T(8,128)(2,1)} %get-tuple-element.40.refs_2_.refs_4_.a_ref), channel_id=1, source_target_pairs={{0,1},{1,0},{2,3},{3,2},{4,5},{5,4},{6,7},{7,6},{8,9},{9,8},{10,11... | collective-permute-start | bytes 3145736 | tf_op jit(solution)/shard_map/ppermute | solution.py:717
  77.1 25.5 %collective-permute-start.7 = (bf16[512,1024]{1,0:T(8,128)(2,1)}, bf16[512,1024]{1,0:T(8,128)(2,1)S(1)}, u32[]{:S(2)}, u32[]{:S(2)}) collective-permute-start(bf16[512,1024]{1,0:T(8,128)(2,1)} %back_second.1.gate_ref.refs_2_.refs_4_.b_ref), channel_id=1, source_target_pairs={{0,1},{1,0},{2,3},{3,2},{4,5},{5,4},{6,7},{7,6},{8,9},{9,8},{10,11... | collective-permute-start | bytes 3145736 | tf_op jit(solution)/shard_map/ppermute | solution.py:719
  77.7 6.5 %collective-permute-start.1 = (f32[8,128]{1,0:T(8,128)S(1)}, f32[8,128]{1,0:T(8,128)S(1)}, u32[]{:S(2)}, u32[]{:S(2)}) collective-permute-start(f32[8,128]{1,0:T(8,128)S(1)} %copy-done.32), channel_id=1, source_target_pairs={{0,2},{2,4},{4,6},{6,0},{1,3},{3,5},{5,7},{7,1},{8,10},{10,12},{12... | collective-permute-start | bytes 12296 | tf_op jit(solution)/shard_map/ppermute | solution.py:733
  79.6 5.2 %collective-permute-start.2 = (f32[8,128]{1,0:T(8,128)S(1)}, f32[8,128]{1,0:T(8,128)S(1)}, u32[]{:S(2)}, u32[]{:S(2)}) collective-permute-start(f32[8,128]{1,0:T(8,128)S(1)} %copy-done.32), channel_id=1, source_target_pairs={{0,4},{2,6},{4,0},{6,2},{1,5},{3,7},{5,1},{7,3},{8,12},{10,14},{12... | collective-permute-start | bytes 12296 | tf_op jit(solution)/shard_map/ppermute | solution.py:733
  83.1 3.6 %collective-permute-start.3 = (f32[8,128]{1,0:T(8,128)S(1)}, f32[8,128]{1,0:T(8,128)S(1)}, u32[]{:S(2)}, u32[]{:S(2)}) collective-permute-start(f32[8,128]{1,0:T(8,128)S(1)} %copy-done.32), channel_id=1, source_target_pairs={{0,6},{2,0},{4,2},{6,4},{1,7},{3,1},{5,3},{7,5},{8,14},{10,8},{12,... | collective-permute-start | bytes 12296 | tf_op jit(solution)/shard_map/ppermute | solution.py:733
  89.5 1.6 collective-permute-start.4
  92.1 6.2 %collective-permute-start.6 = (bf16[96,768]{1,0:T(8,128)(2,1)S(1)}, bf16[96,768]{1,0:T(8,128)(2,1)S(1)}, u32[]{:S(2)}, u32[]{:S(2)}) collective-permute-start(bf16[96,768]{1,0:T(8,128)(2,1)S(1)} %add_convert_fusion.4.after_ref.also_ref), channel_id=1, source_target_pairs={{0,8},{8,0},{16,24},{24,16},{32,40},{40,32},{48,56},{56,48},{64,72... | collective-permute-start | bytes 442376 | tf_op jit(solution)/shard_map/ppermute | solution.py:729
  99.2 11.7 %collective-permute-start.8 = (bf16[96,768]{1,0:T(8,128)(2,1)S(1)}, bf16[96,768]{1,0:T(8,128)(2,1)S(1)}, u32[]{:S(2)}, u32[]{:S(2)}) collective-permute-start(bf16[96,768]{1,0:T(8,128)(2,1)S(1)} %add_convert_fusion.3.after_ref.also_ref), channel_id=1, source_target_pairs={{0,32},{8,40},{16,48},{24,56},{32,0},{40,8},{48,16},{56,24},{64,96... | collective-permute-start | bytes 442376 | tf_op jit(solution)/shard_map/ppermute | solution.py:729
  99.3 15.6 %collective-permute-start.9 = (bf16[512,512]{1,0:T(8,128)(2,1)}, bf16[512,512]{1,0:T(8,128)(2,1)S(1)}, u32[]{:S(2)}, u32[]{:S(2)}) collective-permute-start(bf16[512,512]{1,0:T(8,128)(2,1)} %get-tuple-element.41), channel_id=1, source_target_pairs={{0,32},{8,40},{16,48},{24,56},{32,64},{40,72},{48,80},{56,88},{64,... | collective-permute-start | bytes 1572872 | tf_op jit(solution)/shard_map/ppermute | solution.py:585
  101.3 16.0 %collective-permute-start.10 = (bf16[512,512]{1,0:T(8,128)(2,1)}, bf16[512,512]{1,0:T(8,128)(2,1)S(1)}, u32[]{:S(2)}, u32[]{:S(2)}) collective-permute-start(bf16[512,512]{1,0:T(8,128)(2,1)} %get-tuple-element.45), channel_id=1, source_target_pairs={{0,96},{8,104},{16,112},{24,120},{32,0},{40,8},{48,16},{56,24},{64... | collective-permute-start | bytes 1572872 | tf_op jit(solution)/shard_map/ppermute | solution.py:585
  107.6 22.1 %collective-permute-start.12 = (bf16[512,512]{1,0:T(8,128)(2,1)}, bf16[512,512]{1,0:T(8,128)(2,1)S(1)}, u32[]{:S(2)}, u32[]{:S(2)}) collective-permute-start(bf16[512,512]{1,0:T(8,128)(2,1)} %get-tuple-element.43), channel_id=1, source_target_pairs={{0,8},{8,16},{16,24},{24,0},{32,40},{40,48},{48,56},{56,32},{64,72... | collective-permute-start | bytes 1572872 | tf_op jit(solution)/shard_map/ppermute | solution.py:585
  108.8 20.9 %collective-permute-start.13 = (bf16[512,512]{1,0:T(8,128)(2,1)}, bf16[512,512]{1,0:T(8,128)(2,1)S(1)}, u32[]{:S(2)}, u32[]{:S(2)}) collective-permute-start(bf16[512,512]{1,0:T(8,128)(2,1)} %get-tuple-element.48), channel_id=1, source_target_pairs={{0,24},{8,0},{16,8},{24,16},{32,56},{40,32},{48,40},{56,48},{64,88... | collective-permute-start | bytes 1572872 | tf_op jit(solution)/shard_map/ppermute | solution.py:585
  111.8 12.5 %collective-permute-start.11 = (bf16[96,768]{1,0:T(8,128)(2,1)S(1)}, bf16[96,768]{1,0:T(8,128)(2,1)S(1)}, u32[]{:S(2)}, u32[]{:S(2)}) collective-permute-start(bf16[96,768]{1,0:T(8,128)(2,1)S(1)} %add_convert_fusion.2.after_ref.also_ref), channel_id=1, source_target_pairs={{0,64},{8,72},{16,80},{24,88},{32,96},{40,104},{48,112},{56,120},{... | collective-permute-start | bytes 442376 | tf_op jit(solution)/shard_map/ppermute | solution.py:729
  125.2 11.6 %collective-permute-start.16 = (bf16[96,768]{1,0:T(8,128)(2,1)S(1)}, bf16[96,768]{1,0:T(8,128)(2,1)S(1)}, u32[]{:S(2)}, u32[]{:S(2)}) collective-permute-start(bf16[96,768]{1,0:T(8,128)(2,1)S(1)} %add_convert_fusion.1.after_ref.also_ref), channel_id=1, source_target_pairs={{0,16},{8,24},{16,0},{24,8},{32,48},{40,56},{48,32},{56,40},{64,80... | collective-permute-start | bytes 442376 | tf_op jit(solution)/shard_map/ppermute | solution.py:729
  126.4 24.1 %collective-permute-start.14 = (bf16[2,512,512]{2,1,0:T(8,128)(2,1)}, bf16[2,512,512]{2,1,0:T(8,128)(2,1)S(1)}, u32[]{:S(2)}, u32[]{:S(2)}) collective-permute-start(bf16[2,512,512]{2,1,0:T(8,128)(2,1)} %get-tuple-element.46), channel_id=1, source_target_pairs={{0,32},{8,40},{16,48},{24,56},{32,64},{40,72},{48,80},{56,88},{64,... | collective-permute-start | bytes 3145736 | tf_op jit(solution)/shard_map/ppermute | solution.py:585
  126.9 23.7 %collective-permute-start.15 = (bf16[2,512,512]{2,1,0:T(8,128)(2,1)}, bf16[2,512,512]{2,1,0:T(8,128)(2,1)}, u32[]{:S(2)}, u32[]{:S(2)}) collective-permute-start(bf16[2,512,512]{2,1,0:T(8,128)(2,1)} %get-tuple-element.50), channel_id=1, source_target_pairs={{0,96},{8,104},{16,112},{24,120},{32,0},{40,8},{48,16},{56,24},{64... | collective-permute-start | bytes 3145736 | tf_op jit(solution)/shard_map/ppermute | solution.py:585
  137.8 3.4 %collective-permute-start.17 = (bf16[96,768]{1,0:T(8,128)(2,1)S(1)}, bf16[96,768]{1,0:T(8,128)(2,1)S(1)}, u32[]{:S(2)}, u32[]{:S(2)}) collective-permute-start(bf16[96,768]{1,0:T(8,128)(2,1)S(1)} %add_convert_fusion), channel_id=1, source_target_pairs={{0,1},{1,0},{2,3},{3,2},{4,5},{5,4},{6,7},{7,6},{8,9},{9,8},{10,11... | collective-permute-start | bytes 442376 | tf_op jit(solution)/shard_map/ppermute | solution.py:621
  137.9 27.5 %collective-permute-start.19 = (bf16[2,512,512]{2,1,0:T(8,128)(2,1)}, bf16[2,512,512]{2,1,0:T(8,128)(2,1)S(1)}, u32[]{:S(2)}, u32[]{:S(2)}) collective-permute-start(bf16[2,512,512]{2,1,0:T(8,128)(2,1)} %get-tuple-element.49.after_ref.also_ref), channel_id=1, source_target_pairs={{0,8},{8,16},{16,24},{24,0},{32,40},{40,48},{48,56},{56,32},{64,72... | collective-permute-start | bytes 3145736 | tf_op jit(solution)/shard_map/ppermute | solution.py:585
  138.5 26.9 %collective-permute-start.20 = (bf16[2,512,512]{2,1,0:T(8,128)(2,1)}, bf16[2,512,512]{2,1,0:T(8,128)(2,1)}, u32[]{:S(2)}, u32[]{:S(2)}) collective-permute-start(bf16[2,512,512]{2,1,0:T(8,128)(2,1)} %get-tuple-element.53), channel_id=1, source_target_pairs={{0,24},{8,0},{16,8},{24,16},{32,56},{40,32},{48,40},{56,48},{64,88... | collective-permute-start | bytes 3145736 | tf_op jit(solution)/shard_map/ppermute | solution.py:585
  141.3 14.1 %collective-permute-start.18 = (bf16[192,768]{1,0:T(8,128)(2,1)S(1)}, bf16[192,768]{1,0:T(8,128)(2,1)S(1)}, u32[]{:S(2)}, u32[]{:S(2)}) collective-permute-start(bf16[192,768]{1,0:T(8,128)(2,1)S(1)} %pad_maximum_fusion.1.own_ref), channel_id=1, source_target_pairs={{0,2},{2,0},{4,6},{6,4},{1,3},{3,1},{5,7},{7,5},{8,10},{10,8},{12,... | collective-permute-start | bytes 884744 | tf_op jit(solution)/shard_map/ppermute | solution.py:755
  158.1 20.0 %collective-permute-start.21 = (bf16[384,768]{1,0:T(8,128)(2,1)}, bf16[384,768]{1,0:T(8,128)(2,1)S(1)}, u32[]{:S(2)}, u32[]{:S(2)}) collective-permute-start(bf16[384,768]{1,0:T(8,128)(2,1)} %join.1.also_ref), channel_id=1, source_target_pairs={{0,4},{2,6},{4,0},{6,2},{1,5},{3,7},{5,1},{7,3},{8,12},{10,14},{12... | collective-permute-start | bytes 1769480 | tf_op jit(solution)/shard_map/ppermute | solution.py:621
  160.3 16.3 %collective-permute-start.22 = (bf16[2,128,512]{2,1,0:T(8,128)(2,1)}, bf16[2,128,512]{2,1,0:T(8,128)(2,1)S(1)}, u32[]{:S(2)}, u32[]{:S(2)}) collective-permute-start(bf16[2,128,512]{2,1,0:T(8,128)(2,1)} %get-tuple-element.55), channel_id=1, source_target_pairs={{0,8},{8,16},{16,24},{24,0},{32,40},{40,48},{48,56},{56,32},{64,72... | collective-permute-start | bytes 786440 | tf_op jit(solution)/shard_map/ppermute | solution.py:585
  174.3 8.9 %collective-permute-start.23 = (bf16[2,128,512]{2,1,0:T(8,128)(2,1)S(1)}, bf16[2,128,512]{2,1,0:T(8,128)(2,1)S(1)}, u32[]{:S(2)}, u32[]{:S(2)}) collective-permute-start(bf16[2,128,512]{2,1,0:T(8,128)(2,1)S(1)} %copy-done.40), channel_id=1, source_target_pairs={{0,16},{8,24},{16,0},{24,8},{32,48},{40,56},{48,32},{56,40},{64,80... | collective-permute-start | bytes 786440 | tf_op jit(solution)/shard_map/ppermute | solution.py:585
  175.7 12.3 %collective-permute-start.24 = (bf16[2,128,512]{2,1,0:T(8,128)(2,1)S(1)}, bf16[2,128,512]{2,1,0:T(8,128)(2,1)S(1)}, u32[]{:S(2)}, u32[]{:S(2)}) collective-permute-start(bf16[2,128,512]{2,1,0:T(8,128)(2,1)S(1)} %copy-done.39), channel_id=1, source_target_pairs={{0,24},{8,0},{16,8},{24,16},{32,56},{40,32},{48,40},{56,48},{64,88... | collective-permute-start | bytes 786440 | tf_op jit(solution)/shard_map/ppermute | solution.py:585
  176.5 14.2 %collective-permute-start.25 = (bf16[2,128,512]{2,1,0:T(8,128)(2,1)}, bf16[2,128,512]{2,1,0:T(8,128)(2,1)S(1)}, u32[]{:S(2)}, u32[]{:S(2)}) collective-permute-start(bf16[2,128,512]{2,1,0:T(8,128)(2,1)} %get-tuple-element.58), channel_id=1, source_target_pairs={{0,32},{8,40},{16,48},{24,56},{32,64},{40,72},{48,80},{56,88},{64,... | collective-permute-start | bytes 786440 | tf_op jit(solution)/shard_map/ppermute | solution.py:585
  176.6 14.2 %collective-permute-start.26 = (bf16[2,128,512]{2,1,0:T(8,128)(2,1)}, bf16[2,128,512]{2,1,0:T(8,128)(2,1)S(1)}, u32[]{:S(2)}, u32[]{:S(2)}) collective-permute-start(bf16[2,128,512]{2,1,0:T(8,128)(2,1)} %get-tuple-element.59), channel_id=1, source_target_pairs={{0,64},{8,72},{16,80},{24,88},{32,96},{40,104},{48,112},{56,120},{... | collective-permute-start | bytes 786440 | tf_op jit(solution)/shard_map/ppermute | solution.py:585
  178.1 13.1 %collective-permute-start.27 = (bf16[2,128,512]{2,1,0:T(8,128)(2,1)}, bf16[2,128,512]{2,1,0:T(8,128)(2,1)S(1)}, u32[]{:S(2)}, u32[]{:S(2)}) collective-permute-start(bf16[2,128,512]{2,1,0:T(8,128)(2,1)} %get-tuple-element.60), channel_id=1, source_target_pairs={{0,96},{8,104},{16,112},{24,120},{32,0},{40,8},{48,16},{56,24},{64... | collective-permute-start | bytes 786440 | tf_op jit(solution)/shard_map/ppermute | solution.py:585
  (39 other events, 178.6 us)

commit v5 on v4

--- a/solution.py
+++ b/solution.py
@@ -759,9 +759,10 @@
         pieces.append([cuts[0]] + [send(cuts[k], 1 - part, k) for k in range(1, SIDE)])
         if part == 0:
             ret_half = joined(cuts[0], quarter, far, 1, dec_rank)
-        last = (cuts[0], ret_half)
+            by_tokens = by_token(cuts[0], flat_a, flat_b)
+        last = (by_tokens, ret_half)
     ret_weight_grad = doubled(ret_half, "dec", 2, dec_rank)
-    kv_grad = by_token(cuts[0], flat_a, flat_b).reshape(
+    kv_grad = by_tokens.reshape(
         pass_dev, 1, slot_len, heads, pair_width
     )
     summed = first_half(ret_weight_grad, pieces[0])

time: 196 us -> 191 us (0.974)
  waiting for transfers between devices: 30.1 us -> 23.1 us
  starting transfers between devices: 46.8 us -> 49.7 us
    ppermute x14, waiting for transfers between devices: 16.7 us -> 9.68 us  [send(): return lax.ppermute(value, 'enc', ring_pairs(axis, step))]
    ppermute x14, starting transfers between devices: 19.1 us -> 21.9 us  [send(): return lax.ppermute(value, 'enc', ring_pairs(axis, step))]
    unnamed x84 -> x80, local copies, waits for them, and re-layouts: 13.9 us -> 13.2 us
  transfers between devices with their start and end apart: 30 -> 30, of which waited for: 12 -> 11; matrix products, arithmetic and copies ran while one was open for 7% -> 8% of each run, Pallas kernels for 35% -> 35%
where the time goes in v5:
time: 191 us; the launch traced here: 190 us
  Pallas kernels  87.5 us (46%)
  starting transfers between devices  49.7 us (26%)
  waiting for transfers between devices  23.1 us (12%)
  local copies, waits for them, and re-layouts  15.1 us (8%)
  other arithmetic  7.37 us (4%)
  matrix products  6.03 us (3%)
    pallas_call x6, Pallas kernels, chunk_call(): pl.pallas_call(functools.partial(ordered, kernel), grid_spec=pltpu.Prefet...  28.2 us
    ppermute x14, starting transfers between devices, send(): return lax.ppermute(value, 'enc', ring_pairs(axis, step))  21.9 us
    pallas_call x1, Pallas kernels, project(): pl.pallas_call(project_kernel, grid=(width // depth,), out_shape=jax.Shap...  16.2 us
    unnamed x80, local copies, waits for them, and re-layouts  13.2 us
    ppermute x14, waiting for transfers between devices, send(): return lax.ppermute(value, 'enc', ring_pairs(axis, step))  9.68 us
    all_to_all x1, waiting for transfers between devices, on_device(): lax.all_to_all(stats, 'enc', split_axis=0, concat_axis=0, tiled=True)  8.99 us
    pallas_call x2, Pallas kernels, totals(): pl.pallas_call(total_kernel, grid_spec=pltpu.PrefetchScalarGridSpec(num_s...  7.86 us
    all_to_all x1, starting transfers between devices, on_device(): lax.all_to_all(stats, 'enc', split_axis=0, concat_axis=0, tiled=True)  7.22 us
  transfers between devices with their start and end apart: 30, of which 11 were waited for; matrix products, arithmetic and copies ran while one was open for 8% of the time, Pallas kernels for 35%

profile of v5, /device:TPU:0, one launch (start us, length us, event | category | flops | bytes accessed | tf_op | source)
XLA Modules:
  0.0 189.6 jit_solution(5160608071825321191)
XLA Ops:
  3.9 2.9 %pack.1 = bf16[32,128,128]{2,1,0:T(8,128)(2,1)} custom-call(s32[32]{0:T(128)} %bitcast.65, bf16[512,64]{1,0:T(8,128)(2,1)} %bitcast.61, bf16[512,64]{1,0:T(8,128)(2,1)} %bitcast.62), custom_call_target="tpu_custom_call" | custom-call | flops 1024 | bytes 1024 | tf_op jit(solution)/shard_map/pack/pallas_call | solution.py:46
  6.9 7.1 %all-to-all-start = ((bf16[16,256,128]{2,1,0:T(8,128)(2,1)}), bf16[16,256,128]{2,1,0:T(8,128)(2,1)S(1)}, u32[]{:S(2)}, u32[]{:S(2)}) async-start(bf16[16,256,128]{2,1,0:T(8,128)(2,1)} %bitcast.58), calls=%async_computation | async-start | bytes 2097152 | tf_op jit(solution)/shard_map/all_to_all | solution.py:650
  14.4 16.2 %project.1.kv_ref = f32[16,512,128]{2,1,0:T(8,128)} custom-call(bf16[512,4096]{1,0:T(8,128)(2,1)} %bitcast.54, bf16[4096,16,128]{2,1,0:T(8,128)(2,1)} %w_ref.1), custom_call_target="tpu_custom_call" | custom-call | flops 1024 | bytes 1024 | tf_op jit(solution)/shard_map/project/pallas_call | solution.py:78
  30.8 2.2 %select_reduce_fusion = (f32[2,768]{1,0:T(2,128)S(1)}, f32[2,256,768]{2,1,0:T(8,128)}) fusion(pred[2,256]{1,0:T(4,128)(4,1)S(1)} %iota_compare_fusion, bf16[768,768]{1,0:T(8,128)(2,1)S(1)} %copy-done, bf16[2,1,256,768]{3,2,1,0:T(8,128)(2,1)S(1)} %copy-done.26), kind=kOutput, calls=%fused_computation.14 | convolution fusion | flops 607910400 | bytes 3545600 | tf_op jit(solution)/shard_map/dot_general | solution.py:682
  34.2 5.8 %local_stats.1 = (f32[16,72,128]{2,1,0:T(8,128)}, f32[2,768]{1,0:T(2,128)}) custom-call(s32[2]{0:T(128)} %copy-done.30, s32[2]{0:T(128)} %copy-done.29, f32[16,512,128]{2,1,0:T(8,128)} %project.1.kv_ref, bf16[16,256,128]{2,1,0:T(8,128)(2,1)} %copy-done.3, f32[8,128]{1,0:T(8,128)} %broadcast_in_dim.86.score_ref, f32[2,768]{1,0:T(2,128)} %copy-done.27), custom_call_target="tpu_custom_call" | custom-call | flops 1024 | bytes 1024 | tf_op jit(solution)/shard_map/local_stats/pallas_call | solution.py:179
  40.0 4.2 %turn.1 = (bf16[16,128,512]{2,1,0:T(8,128)(2,1)}, bf16[16,128,512]{2,1,0:T(8,128)(2,1)}) custom-call(s32[1]{0:T(128)} %bitcast.2.rank_ref, f32[16,72,128]{2,1,0:T(8,128)} %get-tuple-element.33.after_ref, bf16[512,4096]{1,0:T(8,128)(2,1)} %bitcast.55), custom_call_target="tpu_custom_call" | custom-call | bytes 67108864 | tf_op jit(solution)/shard_map/turn/pallas_call | solution.py:105
  45.4 7.2 %all-to-all-start.1 = ((f32[16,72,128]{2,1,0:T(8,128)}), f32[16,72,128]{2,1,0:T(8,128)S(1)}, u32[]{:S(2)}, u32[]{:S(2)}) async-start(f32[16,72,128]{2,1,0:T(8,128)} %get-tuple-element.33.after_ref), calls=%async_computation.1 | async-start | bytes 1179648 | tf_op jit(solution)/shard_map/all_to_all | solution.py:713
  52.7 3.8 %fusion.13.after_ref.part_ref = f32[2,192,768]{2,1,0:T(8,128)} fusion(bf16[2,256,192]{2,1,0:T(8,128)(2,1)S(1)} %bitcast.63, f32[2,256,768]{2,1,0:T(8,128)} %get-tuple-element.79, f32[2,768]{1,0:T(2,128)S(1)} %broadcast_divide_fusion, pred[2,256]{1,0:T(4,128)(4,1)S(1)} %iota_compare_fusion), kind=kOutput, calls=%fused_computation.19 | convolution fusion | flops 159252480 | bytes 2955776 | tf_op jit(solution)/shard_map/dot_general | solution.py:707
  56.5 9.0 %all-to-all-done.1.stats_ref = f32[16,72,128]{2,1,0:T(8,128)S(1)} async-done(((f32[16,72,128]{2,1,0:T(8,128)}), f32[16,72,128]{2,1,0:T(8,128)S(1)}, u32[]{:S(2)}, u32[]{:S(2)}) %all-to-all-start.1) | async-done | bytes 589856 | tf_op jit(solution)/shard_map/all_to_all | solution.py:713
  67.0 5.2 %back_first.1 = (bf16[512,1024]{1,0:T(8,128)(2,1)}, f32[4,16,128]{2,1,0:T(8,128)}, f32[8,128]{1,0:T(8,128)}) custom-call(s32[2]{0:T(128)} %copy-done.30, s32[2]{0:T(128)} %copy-done.29, s32[1]{0:T(128)} %bitcast.5.own_ref, s32[32]{0:T(128)} %bitcast.66, f32[2,192,768]{2,1,0:T(8,128)} %fusion.13.after_ref.part_ref, bf16[16,128,512]{2,1,0:T(8,128)(2,1)} %copy-done.2, ...), custom_call_target="tpu_custom_call" | custom-call | bytes 33554432 | tf_op jit(solution)/shard_map/back_first/pallas_call | solution.py:292
  72.2 4.8 %back_second.1.gate_ref.refs_2_.refs_4_.b_ref = bf16[512,1024]{1,0:T(8,128)(2,1)} custom-call(s32[2]{0:T(128)} %copy-done.30, s32[2]{0:T(128)} %copy-done.29, f32[16,512,128]{2,1,0:T(8,128)} %project.1.kv_ref, bf16[16,256,128]{2,1,0:T(8,128)(2,1)} %copy-done.3, f32[4,16,128]{2,1,0:T(8,128)} %get-tuple-element.36.norm_ref), custom_call_target="tpu_custom_call" | custom-call | bytes 33554432 | tf_op jit(solution)/shard_map/back_second/pallas_call | solution.py:319
  79.6 3.5 %collective-permute-start.2 = (f32[8,128]{1,0:T(8,128)S(1)}, f32[8,128]{1,0:T(8,128)S(1)}, u32[]{:S(2)}, u32[]{:S(2)}) collective-permute-start(f32[8,128]{1,0:T(8,128)S(1)} %copy-done.32), channel_id=1, source_target_pairs={{0,4},{2,6},{4,0},{6,2},{1,5},{3,7},{5,1},{7,3},{8,12},{10,14},{12... | collective-permute-start | bytes 12296 | tf_op jit(solution)/shard_map/ppermute | solution.py:733
  87.3 2.1 %apply_gap.1 = (f32[96,768]{1,0:T(8,128)}, bf16[96,768]{1,0:T(8,128)(2,1)}) custom-call(s32[1]{0:T(128)} %bitcast.2.rank_ref, f32[8,128]{1,0:T(8,128)} %get-tuple-element.35.aux_ref, f32[8,128]{1,0:T(8,128)} %copy-done.33, f32[8,128]{1,0:T(8,128)} %copy-done.34, f32[8,128]{1,0:T(8,128)} %copy-done.35, f32[2,192,768]{2,1,0:T(8,128)} %fusion.13.after_ref.part_ref, ...), custom_call_target="tpu_custom_call" | custom-call | flops 1024 | bytes 1024 | tf_op jit(solution)/shard_map/apply_gap/pallas_call | solution.py:556
  93.9 4.1 %far_chunk.2 = (bf16[512,512]{1,0:T(8,128)(2,1)}, bf16[512,512]{1,0:T(8,128)(2,1)}) custom-call(s32[1]{0:T(128)S(6)} %select_n.102.which_ref, bf16[96,768]{1,0:T(8,128)(2,1)} %copy-done.11, bf16[96,768]{1,0:T(8,128)(2,1)} %copy-done.11, bf16[4,4,128,512]{3,2,1,0:T(8,128)(2,1)} %bitcast.45, bf16[4,4,128,512]{3,2,1,0:T(8,128)(2,1)} %bitcast.37, ...), custom_call_target="tpu_custom_call" | custom-call | flops 1024 | bytes 1024 | tf_op jit(solution)/shard_map/far_chunk/pallas_call | solution.py:364
  99.3 2.0 %collective-permute-start.9 = (bf16[512,512]{1,0:T(8,128)(2,1)}, bf16[512,512]{1,0:T(8,128)(2,1)S(1)}, u32[]{:S(2)}, u32[]{:S(2)}) collective-permute-start(bf16[512,512]{1,0:T(8,128)(2,1)} %get-tuple-element.41), channel_id=1, source_target_pairs={{0,32},{8,40},{16,48},{24,56},{32,64},{40,72},{48,80},{56,88},{64,... | collective-permute-start | bytes 1572872 | tf_op jit(solution)/shard_map/ppermute | solution.py:585
  103.6 4.1 %far_chunk.3 = (bf16[512,512]{1,0:T(8,128)(2,1)}, bf16[512,512]{1,0:T(8,128)(2,1)}) custom-call(s32[1]{0:T(128)S(6)} %select_n.103.which_ref, bf16[96,768]{1,0:T(8,128)(2,1)} %copy-done.8, bf16[96,768]{1,0:T(8,128)(2,1)} %copy-done.8, bf16[4,4,128,512]{3,2,1,0:T(8,128)(2,1)} %bitcast.46, bf16[4,4,128,512]{3,2,1,0:T(8,128)(2,1)} %bitcast.38, ...), custom_call_target="tpu_custom_call" | custom-call | flops 1024 | bytes 1024 | tf_op jit(solution)/shard_map/far_chunk/pallas_call | solution.py:364
  114.9 2.4 %collective-permute-done.10.refs_7_ = bf16[512,512]{1,0:T(8,128)(2,1)S(1)} collective-permute-done((bf16[512,512]{1,0:T(8,128)(2,1)}, bf16[512,512]{1,0:T(8,128)(2,1)S(1)}, u32[]{:S(2)}, u32[]{:S(2)}) %collective-permute-start.10) | collective-permute-done | bytes 524320 | tf_op jit(solution)/shard_map/ppermute | solution.py:585
  118.1 6.2 %side_chunks.2 = (bf16[2,512,512]{2,1,0:T(8,128)(2,1)}, bf16[2,512,512]{2,1,0:T(8,128)(2,1)}) custom-call(s32[2]{0:T(128)} %get-tuple-element.76.which_ref, bf16[96,768]{1,0:T(8,128)(2,1)} %copy-done.10, bf16[96,768]{1,0:T(8,128)(2,1)} %copy-done.10, bf16[4,4,128,512]{3,2,1,0:T(8,128)(2,1)} %bitcast.47, bf16[4,4,128,512]{3,2,1,0:T(8,128)(2,1)} %bitcast.39, ...), custom_call_target="tpu_custom_call" | custom-call | flops 1024 | bytes 1024 | tf_op jit(solution)/shard_map/side_chunks/pallas_call | solution.py:364
  127.0 2.8 %collective-permute-start.15 = (bf16[2,512,512]{2,1,0:T(8,128)(2,1)}, bf16[2,512,512]{2,1,0:T(8,128)(2,1)}, u32[]{:S(2)}, u32[]{:S(2)}) collective-permute-start(bf16[2,512,512]{2,1,0:T(8,128)(2,1)} %get-tuple-element.50), channel_id=1, source_target_pairs={{0,96},{8,104},{16,112},{24,120},{32,0},{40,8},{48,16},{56,24},{64... | collective-permute-start | bytes 3145736 | tf_op jit(solution)/shard_map/ppermute | solution.py:585
  130.7 6.2 %side_chunks.3 = (bf16[2,512,512]{2,1,0:T(8,128)(2,1)}, bf16[2,512,512]{2,1,0:T(8,128)(2,1)}) custom-call(s32[2]{0:T(128)} %get-tuple-element.77.which_ref, bf16[96,768]{1,0:T(8,128)(2,1)} %copy-done.9, bf16[96,768]{1,0:T(8,128)(2,1)} %copy-done.9, bf16[4,4,128,512]{3,2,1,0:T(8,128)(2,1)} %bitcast.49, bf16[4,4,128,512]{3,2,1,0:T(8,128)(2,1)} %bitcast.41, ...), custom_call_target="tpu_custom_call" | custom-call | flops 1024 | bytes 1024 | tf_op jit(solution)/shard_map/side_chunks/pallas_call | solution.py:364
  138.5 2.7 %collective-permute-start.24 = (bf16[2,512,512]{2,1,0:T(8,128)(2,1)}, bf16[2,512,512]{2,1,0:T(8,128)(2,1)S(1)}, u32[]{:S(2)}, u32[]{:S(2)}) collective-permute-start(bf16[2,512,512]{2,1,0:T(8,128)(2,1)} %get-tuple-element.56), channel_id=1, source_target_pairs={{0,24},{8,0},{16,8},{24,16},{32,56},{40,32},{48,40},{56,48},{64,88... | collective-permute-start | bytes 3145736 | tf_op jit(solution)/shard_map/ppermute | solution.py:585
  141.9 3.8 %own_chunk.2.after_ref.also_ref = bf16[2,512,512]{2,1,0:T(8,128)(2,1)} custom-call(s32[1]{0:T(128)S(6)} %select_n.93.which_ref, bf16[2,512,512]{2,1,0:T(8,128)(2,1)} %get-tuple-element.49.after_ref.also_ref, bf16[2,512,512]{2,1,0:T(8,128)(2,1)} %get-tuple-element.49.after_ref.also_ref, bf16[4,4,128,512]{3,2,1,0:T(8,128)(2,1)} %bitcast.51, ...), custom_call_target="tpu_custom_call" | custom-call | flops 1024 | bytes 1024 | tf_op jit(solution)/shard_map/own_chunk/pallas_call | solution.py:364
  145.7 3.8 %own_chunk.3.after_ref.also_ref = bf16[2,512,512]{2,1,0:T(8,128)(2,1)} custom-call(s32[1]{0:T(128)S(6)} %select_n.91.which_ref, bf16[2,512,512]{2,1,0:T(8,128)(2,1)} %own_chunk.2.after_ref.also_ref, bf16[2,512,512]{2,1,0:T(8,128)(2,1)} %own_chunk.2.after_ref.also_ref, bf16[4,4,128,512]{3,2,1,0:T(8,128)(2,1)} %bitcast.52, bf16[4,4,128,512]{3,2,1,0:T(8,128)(2,1)} %bitcast.44, ...), custom_call_target="tpu_custom_call" | custom-call | flops 1024 | bytes 1024 | tf_op jit(solution)/shard_map/own_chunk/pallas_call | solution.py:364
  150.7 3.9 %totals.2 = (bf16[2,128,512]{2,1,0:T(8,128)(2,1)}, bf16[2,128,512]{2,1,0:T(8,128)(2,1)}, bf16[2,128,512]{2,1,0:T(8,128)(2,1)}, bf16[2,128,512]{2,1,0:T(8,128)(2,1)}) custom-call(s32[1]{0:T(128)} %bitcast.which_ref, bf16[2,512,512]{2,1,0:T(8,128)(2,1)} %own_chunk.3.after_ref.also_ref, bf16[2,512,512]{2,1,0:T(8,128)(2,1)} %own_chunk.3.after_ref.also_ref, ...), custom_call_target="tpu_custom_call" | custom-call | flops 1024 | bytes 1024 | tf_op jit(solution)/shard_map/totals/pallas_call | solution.py:459
  157.2 2.1 %collective-permute-start.19 = (bf16[384,768]{1,0:T(8,128)(2,1)}, bf16[384,768]{1,0:T(8,128)(2,1)S(1)}, u32[]{:S(2)}, u32[]{:S(2)}) collective-permute-start(bf16[384,768]{1,0:T(8,128)(2,1)} %join.1.also_ref), channel_id=1, source_target_pairs={{0,4},{2,6},{4,0},{6,2},{1,5},{3,7},{5,1},{7,3},{8,12},{10,14},{12... | collective-permute-start | bytes 1769480 | tf_op jit(solution)/shard_map/ppermute | solution.py:621
  159.8 3.9 %by_token.1.after_ref = bf16[512,16,128]{2,1,0:T(8,128)(2,1)} custom-call(bf16[2,128,512]{2,1,0:T(8,128)(2,1)} %get-tuple-element.51.after_ref.refs_0_, bf16[512,1024]{1,0:T(8,128)(2,1)} %get-tuple-element.40.refs_2_.refs_4_.a_ref, bf16[512,1024]{1,0:T(8,128)(2,1)} %back_second.1.gate_ref.refs_2_.refs_4_.b_ref), custom_call_target="tpu_custom_call" | custom-call | flops 1024 | bytes 1024 | tf_op jit(solution)/shard_map/by_token/pallas_call | solution.py:522
  163.8 3.7 %collective-permute-start.21 = (bf16[2,128,512]{2,1,0:T(8,128)(2,1)}, bf16[2,128,512]{2,1,0:T(8,128)(2,1)S(1)}, u32[]{:S(2)}, u32[]{:S(2)}) collective-permute-start(bf16[2,128,512]{2,1,0:T(8,128)(2,1)} %get-tuple-element.54), channel_id=1, source_target_pairs={{0,16},{8,24},{16,0},{24,8},{32,48},{40,56},{48,32},{56,40},{64,80... | collective-permute-start | bytes 786440 | tf_op jit(solution)/shard_map/ppermute | solution.py:585
  168.8 4.0 %totals.3 = (bf16[2,128,512]{2,1,0:T(8,128)(2,1)}, bf16[2,128,512]{2,1,0:T(8,128)(2,1)}, bf16[2,128,512]{2,1,0:T(8,128)(2,1)}, bf16[2,128,512]{2,1,0:T(8,128)(2,1)}) custom-call(s32[1]{0:T(128)} %bitcast.1.which_ref, bf16[512,16,128]{2,1,0:T(8,128)(2,1)} %by_token.1.after_ref, bf16[384,768]{1,0:T(8,128)(2,1)} %join.1.also_ref, ...), custom_call_target="tpu_custom_call" | custom-call | flops 1024 | bytes 1024 | tf_op jit(solution)/shard_map/totals/pallas_call | solution.py:459
  172.7 4.4 %collective-permute-start.26 = (bf16[2,128,512]{2,1,0:T(8,128)(2,1)}, bf16[2,128,512]{2,1,0:T(8,128)(2,1)S(1)}, u32[]{:S(2)}, u32[]{:S(2)}) collective-permute-start(bf16[2,128,512]{2,1,0:T(8,128)(2,1)} %get-tuple-element.59), channel_id=1, source_target_pairs={{0,64},{8,72},{16,80},{24,88},{32,96},{40,104},{48,112},{56,120},{... | collective-permute-start | bytes 786440 | tf_op jit(solution)/shard_map/ppermute | solution.py:585
  179.8 2.0 %first_half.1.first_ref = bf16[2,128,512]{2,1,0:T(8,128)(2,1)} custom-call(bf16[768,768]{1,0:T(8,128)(2,1)} %pad_maximum_fusion.after_ref, bf16[2,128,512]{2,1,0:T(8,128)(2,1)} %get-tuple-element.51.after_ref.refs_0_, bf16[2,128,512]{2,1,0:T(8,128)(2,1)} %copy-done.20, bf16[2,128,512]{2,1,0:T(8,128)(2,1)} %copy-done.21, bf16[2,128,512]{2,1,0:T(8,128)(2,1)} %copy-done.22), custom_call_target="tpu_custom_call" | custom-call | flops 1024 | bytes 1024 | tf_op jit(solution)/shard_map/first_half/pallas_call | solution.py:484
  181.8 4.2 %collective-permute-done.25.refs_1_ = bf16[2,128,512]{2,1,0:T(8,128)(2,1)S(1)} collective-permute-done((bf16[2,128,512]{2,1,0:T(8,128)(2,1)}, bf16[2,128,512]{2,1,0:T(8,128)(2,1)S(1)}, u32[]{:S(2)}, u32[]{:S(2)}) %collective-permute-start.25) | collective-permute-done | bytes 262176 | tf_op jit(solution)/shard_map/ppermute | solution.py:585
  187.4 2.3 %finish.1 = bf16[128,16,128]{2,1,0:T(8,128)(2,1)} custom-call(bf16[2,128,512]{2,1,0:T(8,128)(2,1)} %first_half.1.first_ref, bf16[2,128,512]{2,1,0:T(8,128)(2,1)} %get-tuple-element.57.refs_0_, bf16[2,128,512]{2,1,0:T(8,128)(2,1)} %copy-done.23, bf16[2,128,512]{2,1,0:T(8,128)(2,1)} %copy-done.24, bf16[2,128,512]{2,1,0:T(8,128)(2,1)} %copy-done.25), custom_call_target="tpu_custom_call" | custom-call | flops 1024 | bytes 1024 | tf_op jit(solution)/shard_map/finish/pallas_call | solution.py:505
  (151 shorter events, 45.9 us)
Async XLA Ops:
  0.6 30.2 %copy-start = (bf16[768,768]{1,0:T(8,128)(2,1)S(1)}, bf16[768,768]{1,0:T(8,128)(2,1)}, u32[]{:S(2)}) copy-start(bf16[768,768]{1,0:T(8,128)(2,1)} %param.22) | copy-start | bytes 3538948
  6.9 26.4 %all-to-all-start = ((bf16[16,256,128]{2,1,0:T(8,128)(2,1)}), bf16[16,256,128]{2,1,0:T(8,128)(2,1)S(1)}, u32[]{:S(2)}, u32[]{:S(2)}) async-start(bf16[16,256,128]{2,1,0:T(8,128)(2,1)} %bitcast.58), calls=%async_computation | async-start | bytes 2097152 | tf_op jit(solution)/shard_map/all_to_all | solution.py:650
  14.4 16.4 %copy-start.26 = (bf16[2,1,256,768]{3,2,1,0:T(8,128)(2,1)S(1)}, bf16[2,1,256,768]{3,2,1,0:T(8,128)(2,1)}, u32[]{:S(2)}) copy-start(bf16[2,1,256,768]{3,2,1,0:T(8,128)(2,1)} %param.21) | copy-start | bytes 2359300
  44.2 21.3 %collective-permute-start = (bf16[16,128,512]{2,1,0:T(8,128)(2,1)}, bf16[16,128,512]{2,1,0:T(8,128)(2,1)S(1)}, u32[]{:S(2)}, u32[]{:S(2)}) collective-permute-start(bf16[16,128,512]{2,1,0:T(8,128)(2,1)} %get-tuple-element.34), channel_id=1, source_target_pairs={{0,1},{1,0},{2,3},{3,2},{4,5},{5,4},{6,7},{7,6},{8,9},{9,8},{10,11... | collective-permute-start | bytes 6291464 | tf_op jit(solution)/shard_map/ppermute | solution.py:700
  45.4 20.1 %all-to-all-start.1 = ((f32[16,72,128]{2,1,0:T(8,128)}), f32[16,72,128]{2,1,0:T(8,128)S(1)}, u32[]{:S(2)}, u32[]{:S(2)}) async-start(f32[16,72,128]{2,1,0:T(8,128)} %get-tuple-element.33.after_ref), calls=%async_computation.1 | async-start | bytes 1179648 | tf_op jit(solution)/shard_map/all_to_all | solution.py:713
  72.2 20.7 %collective-permute-start.5 = (bf16[512,1024]{1,0:T(8,128)(2,1)}, bf16[512,1024]{1,0:T(8,128)(2,1)S(1)}, u32[]{:S(2)}, u32[]{:S(2)}) collective-permute-start(bf16[512,1024]{1,0:T(8,128)(2,1)} %get-tuple-element.40.refs_2_.refs_4_.a_ref), channel_id=1, source_target_pairs={{0,1},{1,0},{2,3},{3,2},{4,5},{5,4},{6,7},{7,6},{8,9},{9,8},{10,11... | collective-permute-start | bytes 3145736 | tf_op jit(solution)/shard_map/ppermute | solution.py:717
  77.0 25.5 %collective-permute-start.7 = (bf16[512,1024]{1,0:T(8,128)(2,1)}, bf16[512,1024]{1,0:T(8,128)(2,1)S(1)}, u32[]{:S(2)}, u32[]{:S(2)}) collective-permute-start(bf16[512,1024]{1,0:T(8,128)(2,1)} %back_second.1.gate_ref.refs_2_.refs_4_.b_ref), channel_id=1, source_target_pairs={{0,1},{1,0},{2,3},{3,2},{4,5},{5,4},{6,7},{7,6},{8,9},{9,8},{10,11... | collective-permute-start | bytes 3145736 | tf_op jit(solution)/shard_map/ppermute | solution.py:719
  77.7 6.5 %collective-permute-start.1 = (f32[8,128]{1,0:T(8,128)S(1)}, f32[8,128]{1,0:T(8,128)S(1)}, u32[]{:S(2)}, u32[]{:S(2)}) collective-permute-start(f32[8,128]{1,0:T(8,128)S(1)} %copy-done.32), channel_id=1, source_target_pairs={{0,2},{2,4},{4,6},{6,0},{1,3},{3,5},{5,7},{7,1},{8,10},{10,12},{12... | collective-permute-start | bytes 12296 | tf_op jit(solution)/shard_map/ppermute | solution.py:733
  79.6 5.2 %collective-permute-start.2 = (f32[8,128]{1,0:T(8,128)S(1)}, f32[8,128]{1,0:T(8,128)S(1)}, u32[]{:S(2)}, u32[]{:S(2)}) collective-permute-start(f32[8,128]{1,0:T(8,128)S(1)} %copy-done.32), channel_id=1, source_target_pairs={{0,4},{2,6},{4,0},{6,2},{1,5},{3,7},{5,1},{7,3},{8,12},{10,14},{12... | collective-permute-start | bytes 12296 | tf_op jit(solution)/shard_map/ppermute | solution.py:733
  83.1 3.6 %collective-permute-start.3 = (f32[8,128]{1,0:T(8,128)S(1)}, f32[8,128]{1,0:T(8,128)S(1)}, u32[]{:S(2)}, u32[]{:S(2)}) collective-permute-start(f32[8,128]{1,0:T(8,128)S(1)} %copy-done.32), channel_id=1, source_target_pairs={{0,6},{2,0},{4,2},{6,4},{1,7},{3,1},{5,3},{7,5},{8,14},{10,8},{12,... | collective-permute-start | bytes 12296 | tf_op jit(solution)/shard_map/ppermute | solution.py:733
  89.5 1.6 collective-permute-start.4
  92.1 6.2 %collective-permute-start.6 = (bf16[96,768]{1,0:T(8,128)(2,1)S(1)}, bf16[96,768]{1,0:T(8,128)(2,1)S(1)}, u32[]{:S(2)}, u32[]{:S(2)}) collective-permute-start(bf16[96,768]{1,0:T(8,128)(2,1)S(1)} %add_convert_fusion.4.after_ref.also_ref), channel_id=1, source_target_pairs={{0,8},{8,0},{16,24},{24,16},{32,40},{40,32},{48,56},{56,48},{64,72... | collective-permute-start | bytes 442376 | tf_op jit(solution)/shard_map/ppermute | solution.py:729
  99.2 11.7 %collective-permute-start.8 = (bf16[96,768]{1,0:T(8,128)(2,1)S(1)}, bf16[96,768]{1,0:T(8,128)(2,1)S(1)}, u32[]{:S(2)}, u32[]{:S(2)}) collective-permute-start(bf16[96,768]{1,0:T(8,128)(2,1)S(1)} %add_convert_fusion.3.after_ref.also_ref), channel_id=1, source_target_pairs={{0,32},{8,40},{16,48},{24,56},{32,0},{40,8},{48,16},{56,24},{64,96... | collective-permute-start | bytes 442376 | tf_op jit(solution)/shard_map/ppermute | solution.py:729
  99.3 15.6 %collective-permute-start.9 = (bf16[512,512]{1,0:T(8,128)(2,1)}, bf16[512,512]{1,0:T(8,128)(2,1)S(1)}, u32[]{:S(2)}, u32[]{:S(2)}) collective-permute-start(bf16[512,512]{1,0:T(8,128)(2,1)} %get-tuple-element.41), channel_id=1, source_target_pairs={{0,32},{8,40},{16,48},{24,56},{32,64},{40,72},{48,80},{56,88},{64,... | collective-permute-start | bytes 1572872 | tf_op jit(solution)/shard_map/ppermute | solution.py:585
  101.3 16.0 %collective-permute-start.10 = (bf16[512,512]{1,0:T(8,128)(2,1)}, bf16[512,512]{1,0:T(8,128)(2,1)S(1)}, u32[]{:S(2)}, u32[]{:S(2)}) collective-permute-start(bf16[512,512]{1,0:T(8,128)(2,1)} %get-tuple-element.45), channel_id=1, source_target_pairs={{0,96},{8,104},{16,112},{24,120},{32,0},{40,8},{48,16},{56,24},{64... | collective-permute-start | bytes 1572872 | tf_op jit(solution)/shard_map/ppermute | solution.py:585
  107.6 22.1 %collective-permute-start.12 = (bf16[512,512]{1,0:T(8,128)(2,1)}, bf16[512,512]{1,0:T(8,128)(2,1)S(1)}, u32[]{:S(2)}, u32[]{:S(2)}) collective-permute-start(bf16[512,512]{1,0:T(8,128)(2,1)} %get-tuple-element.43), channel_id=1, source_target_pairs={{0,8},{8,16},{16,24},{24,0},{32,40},{40,48},{48,56},{56,32},{64,72... | collective-permute-start | bytes 1572872 | tf_op jit(solution)/shard_map/ppermute | solution.py:585
  108.9 20.9 %collective-permute-start.13 = (bf16[512,512]{1,0:T(8,128)(2,1)}, bf16[512,512]{1,0:T(8,128)(2,1)S(1)}, u32[]{:S(2)}, u32[]{:S(2)}) collective-permute-start(bf16[512,512]{1,0:T(8,128)(2,1)} %get-tuple-element.48), channel_id=1, source_target_pairs={{0,24},{8,0},{16,8},{24,16},{32,56},{40,32},{48,40},{56,48},{64,88... | collective-permute-start | bytes 1572872 | tf_op jit(solution)/shard_map/ppermute | solution.py:585
  111.8 12.5 %collective-permute-start.11 = (bf16[96,768]{1,0:T(8,128)(2,1)S(1)}, bf16[96,768]{1,0:T(8,128)(2,1)S(1)}, u32[]{:S(2)}, u32[]{:S(2)}) collective-permute-start(bf16[96,768]{1,0:T(8,128)(2,1)S(1)} %add_convert_fusion.2.after_ref.also_ref), channel_id=1, source_target_pairs={{0,64},{8,72},{16,80},{24,88},{32,96},{40,104},{48,112},{56,120},{... | collective-permute-start | bytes 442376 | tf_op jit(solution)/shard_map/ppermute | solution.py:729
  125.2 11.7 %collective-permute-start.16 = (bf16[96,768]{1,0:T(8,128)(2,1)S(1)}, bf16[96,768]{1,0:T(8,128)(2,1)S(1)}, u32[]{:S(2)}, u32[]{:S(2)}) collective-permute-start(bf16[96,768]{1,0:T(8,128)(2,1)S(1)} %add_convert_fusion.1.after_ref.also_ref), channel_id=1, source_target_pairs={{0,16},{8,24},{16,0},{24,8},{32,48},{40,56},{48,32},{56,40},{64,80... | collective-permute-start | bytes 442376 | tf_op jit(solution)/shard_map/ppermute | solution.py:729
  126.5 24.2 %collective-permute-start.14 = (bf16[2,512,512]{2,1,0:T(8,128)(2,1)}, bf16[2,512,512]{2,1,0:T(8,128)(2,1)}, u32[]{:S(2)}, u32[]{:S(2)}) collective-permute-start(bf16[2,512,512]{2,1,0:T(8,128)(2,1)} %get-tuple-element.46), channel_id=1, source_target_pairs={{0,32},{8,40},{16,48},{24,56},{32,64},{40,72},{48,80},{56,88},{64,... | collective-permute-start | bytes 3145736 | tf_op jit(solution)/shard_map/ppermute | solution.py:585
  127.0 23.7 %collective-permute-start.15 = (bf16[2,512,512]{2,1,0:T(8,128)(2,1)}, bf16[2,512,512]{2,1,0:T(8,128)(2,1)}, u32[]{:S(2)}, u32[]{:S(2)}) collective-permute-start(bf16[2,512,512]{2,1,0:T(8,128)(2,1)} %get-tuple-element.50), channel_id=1, source_target_pairs={{0,96},{8,104},{16,112},{24,120},{32,0},{40,8},{48,16},{56,24},{64... | collective-permute-start | bytes 3145736 | tf_op jit(solution)/shard_map/ppermute | solution.py:585
  137.9 3.4 %collective-permute-start.17 = (bf16[96,768]{1,0:T(8,128)(2,1)S(1)}, bf16[96,768]{1,0:T(8,128)(2,1)S(1)}, u32[]{:S(2)}, u32[]{:S(2)}) collective-permute-start(bf16[96,768]{1,0:T(8,128)(2,1)S(1)} %add_convert_fusion), channel_id=1, source_target_pairs={{0,1},{1,0},{2,3},{3,2},{4,5},{5,4},{6,7},{7,6},{8,9},{9,8},{10,11... | collective-permute-start | bytes 442376 | tf_op jit(solution)/shard_map/ppermute | solution.py:621
  138.0 29.5 %collective-permute-start.23 = (bf16[2,512,512]{2,1,0:T(8,128)(2,1)}, bf16[2,512,512]{2,1,0:T(8,128)(2,1)S(1)}, u32[]{:S(2)}, u32[]{:S(2)}) collective-permute-start(bf16[2,512,512]{2,1,0:T(8,128)(2,1)} %get-tuple-element.49.after_ref.also_ref), channel_id=1, source_target_pairs={{0,8},{8,16},{16,24},{24,0},{32,40},{40,48},{48,56},{56,32},{64,72... | collective-permute-start | bytes 3145736 | tf_op jit(solution)/shard_map/ppermute | solution.py:585
  138.5 29.2 %collective-permute-start.24 = (bf16[2,512,512]{2,1,0:T(8,128)(2,1)}, bf16[2,512,512]{2,1,0:T(8,128)(2,1)S(1)}, u32[]{:S(2)}, u32[]{:S(2)}) collective-permute-start(bf16[2,512,512]{2,1,0:T(8,128)(2,1)} %get-tuple-element.56), channel_id=1, source_target_pairs={{0,24},{8,0},{16,8},{24,16},{32,56},{40,32},{48,40},{56,48},{64,88... | collective-permute-start | bytes 3145736 | tf_op jit(solution)/shard_map/ppermute | solution.py:585
  141.3 13.2 %collective-permute-start.18 = (bf16[192,768]{1,0:T(8,128)(2,1)S(1)}, bf16[192,768]{1,0:T(8,128)(2,1)S(1)}, u32[]{:S(2)}, u32[]{:S(2)}) collective-permute-start(bf16[192,768]{1,0:T(8,128)(2,1)S(1)} %pad_maximum_fusion.1.own_ref), channel_id=1, source_target_pairs={{0,2},{2,0},{4,6},{6,4},{1,3},{3,1},{5,7},{7,5},{8,10},{10,8},{12,... | collective-permute-start | bytes 884744 | tf_op jit(solution)/shard_map/ppermute | solution.py:755
  157.2 19.9 %collective-permute-start.19 = (bf16[384,768]{1,0:T(8,128)(2,1)}, bf16[384,768]{1,0:T(8,128)(2,1)S(1)}, u32[]{:S(2)}, u32[]{:S(2)}) collective-permute-start(bf16[384,768]{1,0:T(8,128)(2,1)} %join.1.also_ref), channel_id=1, source_target_pairs={{0,4},{2,6},{4,0},{6,2},{1,5},{3,7},{5,1},{7,3},{8,12},{10,14},{12... | collective-permute-start | bytes 1769480 | tf_op jit(solution)/shard_map/ppermute | solution.py:621
  159.3 13.4 %collective-permute-start.20 = (bf16[2,128,512]{2,1,0:T(8,128)(2,1)}, bf16[2,128,512]{2,1,0:T(8,128)(2,1)S(1)}, u32[]{:S(2)}, u32[]{:S(2)}) collective-permute-start(bf16[2,128,512]{2,1,0:T(8,128)(2,1)} %get-tuple-element.53), channel_id=1, source_target_pairs={{0,8},{8,16},{16,24},{24,0},{32,40},{40,48},{48,56},{56,32},{64,72... | collective-permute-start | bytes 786440 | tf_op jit(solution)/shard_map/ppermute | solution.py:585
  163.8 14.6 %collective-permute-start.21 = (bf16[2,128,512]{2,1,0:T(8,128)(2,1)}, bf16[2,128,512]{2,1,0:T(8,128)(2,1)S(1)}, u32[]{:S(2)}, u32[]{:S(2)}) collective-permute-start(bf16[2,128,512]{2,1,0:T(8,128)(2,1)} %get-tuple-element.54), channel_id=1, source_target_pairs={{0,16},{8,24},{16,0},{24,8},{32,48},{40,56},{48,32},{56,40},{64,80... | collective-permute-start | bytes 786440 | tf_op jit(solution)/shard_map/ppermute | solution.py:585
  167.4 11.0 %collective-permute-start.22 = (bf16[2,128,512]{2,1,0:T(8,128)(2,1)}, bf16[2,128,512]{2,1,0:T(8,128)(2,1)S(1)}, u32[]{:S(2)}, u32[]{:S(2)}) collective-permute-start(bf16[2,128,512]{2,1,0:T(8,128)(2,1)} %get-tuple-element.55), channel_id=1, source_target_pairs={{0,24},{8,0},{16,8},{24,16},{32,56},{40,32},{48,40},{56,48},{64,88... | collective-permute-start | bytes 786440 | tf_op jit(solution)/shard_map/ppermute | solution.py:585
  172.7 13.3 %collective-permute-start.25 = (bf16[2,128,512]{2,1,0:T(8,128)(2,1)}, bf16[2,128,512]{2,1,0:T(8,128)(2,1)S(1)}, u32[]{:S(2)}, u32[]{:S(2)}) collective-permute-start(bf16[2,128,512]{2,1,0:T(8,128)(2,1)} %get-tuple-element.58), channel_id=1, source_target_pairs={{0,32},{8,40},{16,48},{24,56},{32,64},{40,72},{48,80},{56,88},{64,... | collective-permute-start | bytes 786440 | tf_op jit(solution)/shard_map/ppermute | solution.py:585
  172.7 13.3 %collective-permute-start.26 = (bf16[2,128,512]{2,1,0:T(8,128)(2,1)}, bf16[2,128,512]{2,1,0:T(8,128)(2,1)S(1)}, u32[]{:S(2)}, u32[]{:S(2)}) collective-permute-start(bf16[2,128,512]{2,1,0:T(8,128)(2,1)} %get-tuple-element.59), channel_id=1, source_target_pairs={{0,64},{8,72},{16,80},{24,88},{32,96},{40,104},{48,112},{56,120},{... | collective-permute-start | bytes 786440 | tf_op jit(solution)/shard_map/ppermute | solution.py:585
  177.1 9.5 %collective-permute-start.27 = (bf16[2,128,512]{2,1,0:T(8,128)(2,1)}, bf16[2,128,512]{2,1,0:T(8,128)(2,1)S(1)}, u32[]{:S(2)}, u32[]{:S(2)}) collective-permute-start(bf16[2,128,512]{2,1,0:T(8,128)(2,1)} %get-tuple-element.60), channel_id=1, source_target_pairs={{0,96},{8,104},{16,112},{24,120},{32,0},{40,8},{48,16},{56,24},{64... | collective-permute-start | bytes 786440 | tf_op jit(solution)/shard_map/ppermute | solution.py:585
  (37 other events, 162.8 us)

commit v6 on v5

--- a/solution.py
+++ b/solution.py
@@ -72,7 +72,7 @@
         o_ref[2 * pair + 1] += part[:, 128:]
 
 
-def project(tok_rows, kv_weight, depth=512):
+def project(tok_rows, kv_weight, depth=1024):
     tokens, width = tok_rows.shape
     heads, pair_width = kv_weight.shape[1:]
     return pl.pallas_call(

time: 191 us -> 189 us (0.990)
  transfers between devices with their start and end apart: 30 -> 30, of which waited for: 11 -> 12; matrix products, arithmetic and copies ran while one was open for 8% -> 8% of each run, Pallas kernels for 35% -> 35%
where the time goes in v6:
time: 189 us; the launch traced here: 188 us
  Pallas kernels  85.8 us (45%)
  starting transfers between devices  49.4 us (26%)
  waiting for transfers between devices  23.2 us (12%)
  local copies, waits for them, and re-layouts  15.1 us (8%)
  other arithmetic  7.37 us (4%)
  matrix products  6.03 us (3%)
    pallas_call x6, Pallas kernels, chunk_call(): pl.pallas_call(functools.partial(ordered, kernel), grid_spec=pltpu.Prefet...  28.2 us
    ppermute x14, starting transfers between devices, send(): return lax.ppermute(value, 'enc', ring_pairs(axis, step))  21.9 us
    pallas_call x1, Pallas kernels, project(): pl.pallas_call(project_kernel, grid=(width // depth,), out_shape=jax.Shap...  14.6 us
    unnamed x80, local copies, waits for them, and re-layouts  13.2 us
    ppermute x14, waiting for transfers between devices, send(): return lax.ppermute(value, 'enc', ring_pairs(axis, step))  9.67 us
    all_to_all x1, waiting for transfers between devices, on_device(): lax.all_to_all(stats, 'enc', split_axis=0, concat_axis=0, tiled=True)  8.99 us
    pallas_call x2, Pallas kernels, totals(): pl.pallas_call(total_kernel, grid_spec=pltpu.PrefetchScalarGridSpec(num_s...  7.86 us
    all_to_all x1, starting transfers between devices, on_device(): lax.all_to_all(packed.reshape(N_ENC, pass_dev * query_len, pair_width), '...  7.12 us
  transfers between devices with their start and end apart: 30, of which 12 were waited for; matrix products, arithmetic and copies ran while one was open for 8% of the time, Pallas kernels for 35%

profile of v6, /device:TPU:0, one launch (start us, length us, event | category | flops | bytes accessed | tf_op | source)
XLA Modules:
  0.0 187.8 jit_solution(4871870865460010195)
XLA Ops:
  3.9 2.9 %pack.1 = bf16[32,128,128]{2,1,0:T(8,128)(2,1)} custom-call(s32[32]{0:T(128)} %bitcast.65, bf16[512,64]{1,0:T(8,128)(2,1)} %bitcast.61, bf16[512,64]{1,0:T(8,128)(2,1)} %bitcast.62), custom_call_target="tpu_custom_call" | custom-call | flops 1024 | bytes 1024 | tf_op jit(solution)/shard_map/pack/pallas_call | solution.py:46
  6.9 7.1 %all-to-all-start = ((bf16[16,256,128]{2,1,0:T(8,128)(2,1)}), bf16[16,256,128]{2,1,0:T(8,128)(2,1)S(1)}, u32[]{:S(2)}, u32[]{:S(2)}) async-start(bf16[16,256,128]{2,1,0:T(8,128)(2,1)} %bitcast.58), calls=%async_computation | async-start | bytes 2097152 | tf_op jit(solution)/shard_map/all_to_all | solution.py:650
  14.4 14.6 %project.1.kv_ref = f32[16,512,128]{2,1,0:T(8,128)} custom-call(bf16[512,4096]{1,0:T(8,128)(2,1)} %bitcast.54, bf16[4096,16,128]{2,1,0:T(8,128)(2,1)} %w_ref.1), custom_call_target="tpu_custom_call" | custom-call | flops 1024 | bytes 1024 | tf_op jit(solution)/shard_map/project/pallas_call | solution.py:78
  29.2 2.2 %select_reduce_fusion = (f32[2,768]{1,0:T(2,128)S(1)}, f32[2,256,768]{2,1,0:T(8,128)}) fusion(pred[2,256]{1,0:T(4,128)(4,1)S(1)} %iota_compare_fusion, bf16[768,768]{1,0:T(8,128)(2,1)S(1)} %copy-done, bf16[2,1,256,768]{3,2,1,0:T(8,128)(2,1)S(1)} %copy-done.26), kind=kOutput, calls=%fused_computation.14 | convolution fusion | flops 607910400 | bytes 3545600 | tf_op jit(solution)/shard_map/dot_general | solution.py:682
  32.7 5.8 %local_stats.1 = (f32[16,72,128]{2,1,0:T(8,128)}, f32[2,768]{1,0:T(2,128)}) custom-call(s32[2]{0:T(128)} %copy-done.30, s32[2]{0:T(128)} %copy-done.29, f32[16,512,128]{2,1,0:T(8,128)} %project.1.kv_ref, bf16[16,256,128]{2,1,0:T(8,128)(2,1)} %copy-done.3, f32[8,128]{1,0:T(8,128)} %broadcast_in_dim.86.score_ref, f32[2,768]{1,0:T(2,128)} %copy-done.27), custom_call_target="tpu_custom_call" | custom-call | flops 1024 | bytes 1024 | tf_op jit(solution)/shard_map/local_stats/pallas_call | solution.py:179
  38.4 4.2 %turn.1 = (bf16[16,128,512]{2,1,0:T(8,128)(2,1)}, bf16[16,128,512]{2,1,0:T(8,128)(2,1)}) custom-call(s32[1]{0:T(128)} %bitcast.2.rank_ref, f32[16,72,128]{2,1,0:T(8,128)} %get-tuple-element.33.after_ref, bf16[512,4096]{1,0:T(8,128)(2,1)} %bitcast.55), custom_call_target="tpu_custom_call" | custom-call | bytes 67108864 | tf_op jit(solution)/shard_map/turn/pallas_call | solution.py:105
  43.8 7.1 %all-to-all-start.1 = ((f32[16,72,128]{2,1,0:T(8,128)}), f32[16,72,128]{2,1,0:T(8,128)S(1)}, u32[]{:S(2)}, u32[]{:S(2)}) async-start(f32[16,72,128]{2,1,0:T(8,128)} %get-tuple-element.33.after_ref), calls=%async_computation.1 | async-start | bytes 1179648 | tf_op jit(solution)/shard_map/all_to_all | solution.py:713
  51.0 3.8 %fusion.13.after_ref.part_ref = f32[2,192,768]{2,1,0:T(8,128)} fusion(bf16[2,256,192]{2,1,0:T(8,128)(2,1)S(1)} %bitcast.63, f32[2,256,768]{2,1,0:T(8,128)} %get-tuple-element.79, f32[2,768]{1,0:T(2,128)S(1)} %broadcast_divide_fusion, pred[2,256]{1,0:T(4,128)(4,1)S(1)} %iota_compare_fusion), kind=kOutput, calls=%fused_computation.19 | convolution fusion | flops 159252480 | bytes 2955776 | tf_op jit(solution)/shard_map/dot_general | solution.py:707
  54.8 9.0 %all-to-all-done.1.stats_ref = f32[16,72,128]{2,1,0:T(8,128)S(1)} async-done(((f32[16,72,128]{2,1,0:T(8,128)}), f32[16,72,128]{2,1,0:T(8,128)S(1)}, u32[]{:S(2)}, u32[]{:S(2)}) %all-to-all-start.1) | async-done | bytes 589856 | tf_op jit(solution)/shard_map/all_to_all | solution.py:713
  65.3 5.2 %back_first.1 = (bf16[512,1024]{1,0:T(8,128)(2,1)}, f32[4,16,128]{2,1,0:T(8,128)}, f32[8,128]{1,0:T(8,128)}) custom-call(s32[2]{0:T(128)} %copy-done.30, s32[2]{0:T(128)} %copy-done.29, s32[1]{0:T(128)} %bitcast.5.own_ref, s32[32]{0:T(128)} %bitcast.66, f32[2,192,768]{2,1,0:T(8,128)} %fusion.13.after_ref.part_ref, bf16[16,128,512]{2,1,0:T(8,128)(2,1)} %copy-done.2, ...), custom_call_target="tpu_custom_call" | custom-call | bytes 33554432 | tf_op jit(solution)/shard_map/back_first/pallas_call | solution.py:292
  70.6 4.8 %back_second.1.gate_ref.refs_2_.refs_4_.b_ref = bf16[512,1024]{1,0:T(8,128)(2,1)} custom-call(s32[2]{0:T(128)} %copy-done.30, s32[2]{0:T(128)} %copy-done.29, f32[16,512,128]{2,1,0:T(8,128)} %project.1.kv_ref, bf16[16,256,128]{2,1,0:T(8,128)(2,1)} %copy-done.3, f32[4,16,128]{2,1,0:T(8,128)} %get-tuple-element.36.norm_ref), custom_call_target="tpu_custom_call" | custom-call | bytes 33554432 | tf_op jit(solution)/shard_map/back_second/pallas_call | solution.py:319
  77.9 3.5 %collective-permute-start.2 = (f32[8,128]{1,0:T(8,128)S(1)}, f32[8,128]{1,0:T(8,128)S(1)}, u32[]{:S(2)}, u32[]{:S(2)}) collective-permute-start(f32[8,128]{1,0:T(8,128)S(1)} %copy-done.32), channel_id=1, source_target_pairs={{0,4},{2,6},{4,0},{6,2},{1,5},{3,7},{5,1},{7,3},{8,12},{10,14},{12... | collective-permute-start | bytes 12296 | tf_op jit(solution)/shard_map/ppermute | solution.py:733
  85.7 2.1 %apply_gap.1 = (f32[96,768]{1,0:T(8,128)}, bf16[96,768]{1,0:T(8,128)(2,1)}) custom-call(s32[1]{0:T(128)} %bitcast.2.rank_ref, f32[8,128]{1,0:T(8,128)} %get-tuple-element.35.aux_ref, f32[8,128]{1,0:T(8,128)} %copy-done.33, f32[8,128]{1,0:T(8,128)} %copy-done.34, f32[8,128]{1,0:T(8,128)} %copy-done.35, f32[2,192,768]{2,1,0:T(8,128)} %fusion.13.after_ref.part_ref, ...), custom_call_target="tpu_custom_call" | custom-call | flops 1024 | bytes 1024 | tf_op jit(solution)/shard_map/apply_gap/pallas_call | solution.py:556
  92.1 4.1 %far_chunk.2 = (bf16[512,512]{1,0:T(8,128)(2,1)}, bf16[512,512]{1,0:T(8,128)(2,1)}) custom-call(s32[1]{0:T(128)S(6)} %select_n.102.which_ref, bf16[96,768]{1,0:T(8,128)(2,1)} %copy-done.11, bf16[96,768]{1,0:T(8,128)(2,1)} %copy-done.11, bf16[4,4,128,512]{3,2,1,0:T(8,128)(2,1)} %bitcast.45, bf16[4,4,128,512]{3,2,1,0:T(8,128)(2,1)} %bitcast.37, ...), custom_call_target="tpu_custom_call" | custom-call | flops 1024 | bytes 1024 | tf_op jit(solution)/shard_map/far_chunk/pallas_call | solution.py:364
  97.4 2.0 %collective-permute-start.9 = (bf16[512,512]{1,0:T(8,128)(2,1)}, bf16[512,512]{1,0:T(8,128)(2,1)S(1)}, u32[]{:S(2)}, u32[]{:S(2)}) collective-permute-start(bf16[512,512]{1,0:T(8,128)(2,1)} %get-tuple-element.41), channel_id=1, source_target_pairs={{0,32},{8,40},{16,48},{24,56},{32,64},{40,72},{48,80},{56,88},{64,... | collective-permute-start | bytes 1572872 | tf_op jit(solution)/shard_map/ppermute | solution.py:585
  101.7 4.1 %far_chunk.3 = (bf16[512,512]{1,0:T(8,128)(2,1)}, bf16[512,512]{1,0:T(8,128)(2,1)}) custom-call(s32[1]{0:T(128)S(6)} %select_n.103.which_ref, bf16[96,768]{1,0:T(8,128)(2,1)} %copy-done.8, bf16[96,768]{1,0:T(8,128)(2,1)} %copy-done.8, bf16[4,4,128,512]{3,2,1,0:T(8,128)(2,1)} %bitcast.46, bf16[4,4,128,512]{3,2,1,0:T(8,128)(2,1)} %bitcast.38, ...), custom_call_target="tpu_custom_call" | custom-call | flops 1024 | bytes 1024 | tf_op jit(solution)/shard_map/far_chunk/pallas_call | solution.py:364
  113.0 2.4 %collective-permute-done.10.refs_7_ = bf16[512,512]{1,0:T(8,128)(2,1)S(1)} collective-permute-done((bf16[512,512]{1,0:T(8,128)(2,1)}, bf16[512,512]{1,0:T(8,128)(2,1)S(1)}, u32[]{:S(2)}, u32[]{:S(2)}) %collective-permute-start.10) | collective-permute-done | bytes 524320 | tf_op jit(solution)/shard_map/ppermute | solution.py:585
  116.2 6.2 %side_chunks.2 = (bf16[2,512,512]{2,1,0:T(8,128)(2,1)}, bf16[2,512,512]{2,1,0:T(8,128)(2,1)}) custom-call(s32[2]{0:T(128)} %get-tuple-element.76.which_ref, bf16[96,768]{1,0:T(8,128)(2,1)} %copy-done.10, bf16[96,768]{1,0:T(8,128)(2,1)} %copy-done.10, bf16[4,4,128,512]{3,2,1,0:T(8,128)(2,1)} %bitcast.47, bf16[4,4,128,512]{3,2,1,0:T(8,128)(2,1)} %bitcast.39, ...), custom_call_target="tpu_custom_call" | custom-call | flops 1024 | bytes 1024 | tf_op jit(solution)/shard_map/side_chunks/pallas_call | solution.py:364
  125.1 2.8 %collective-permute-start.15 = (bf16[2,512,512]{2,1,0:T(8,128)(2,1)}, bf16[2,512,512]{2,1,0:T(8,128)(2,1)}, u32[]{:S(2)}, u32[]{:S(2)}) collective-permute-start(bf16[2,512,512]{2,1,0:T(8,128)(2,1)} %get-tuple-element.50), channel_id=1, source_target_pairs={{0,96},{8,104},{16,112},{24,120},{32,0},{40,8},{48,16},{56,24},{64... | collective-permute-start | bytes 3145736 | tf_op jit(solution)/shard_map/ppermute | solution.py:585
  128.9 6.2 %side_chunks.3 = (bf16[2,512,512]{2,1,0:T(8,128)(2,1)}, bf16[2,512,512]{2,1,0:T(8,128)(2,1)}) custom-call(s32[2]{0:T(128)} %get-tuple-element.77.which_ref, bf16[96,768]{1,0:T(8,128)(2,1)} %copy-done.9, bf16[96,768]{1,0:T(8,128)(2,1)} %copy-done.9, bf16[4,4,128,512]{3,2,1,0:T(8,128)(2,1)} %bitcast.49, bf16[4,4,128,512]{3,2,1,0:T(8,128)(2,1)} %bitcast.41, ...), custom_call_target="tpu_custom_call" | custom-call | flops 1024 | bytes 1024 | tf_op jit(solution)/shard_map/side_chunks/pallas_call | solution.py:364
  136.7 2.7 %collective-permute-start.24 = (bf16[2,512,512]{2,1,0:T(8,128)(2,1)}, bf16[2,512,512]{2,1,0:T(8,128)(2,1)S(1)}, u32[]{:S(2)}, u32[]{:S(2)}) collective-permute-start(bf16[2,512,512]{2,1,0:T(8,128)(2,1)} %get-tuple-element.56), channel_id=1, source_target_pairs={{0,24},{8,0},{16,8},{24,16},{32,56},{40,32},{48,40},{56,48},{64,88... | collective-permute-start | bytes 3145736 | tf_op jit(solution)/shard_map/ppermute | solution.py:585
  140.1 3.8 %own_chunk.2.after_ref.also_ref = bf16[2,512,512]{2,1,0:T(8,128)(2,1)} custom-call(s32[1]{0:T(128)S(6)} %select_n.93.which_ref, bf16[2,512,512]{2,1,0:T(8,128)(2,1)} %get-tuple-element.49.after_ref.also_ref, bf16[2,512,512]{2,1,0:T(8,128)(2,1)} %get-tuple-element.49.after_ref.also_ref, bf16[4,4,128,512]{3,2,1,0:T(8,128)(2,1)} %bitcast.51, ...), custom_call_target="tpu_custom_call" | custom-call | flops 1024 | bytes 1024 | tf_op jit(solution)/shard_map/own_chunk/pallas_call | solution.py:364
  143.9 3.8 %own_chunk.3.after_ref.also_ref = bf16[2,512,512]{2,1,0:T(8,128)(2,1)} custom-call(s32[1]{0:T(128)S(6)} %select_n.91.which_ref, bf16[2,512,512]{2,1,0:T(8,128)(2,1)} %own_chunk.2.after_ref.also_ref, bf16[2,512,512]{2,1,0:T(8,128)(2,1)} %own_chunk.2.after_ref.also_ref, bf16[4,4,128,512]{3,2,1,0:T(8,128)(2,1)} %bitcast.52, bf16[4,4,128,512]{3,2,1,0:T(8,128)(2,1)} %bitcast.44, ...), custom_call_target="tpu_custom_call" | custom-call | flops 1024 | bytes 1024 | tf_op jit(solution)/shard_map/own_chunk/pallas_call | solution.py:364
  148.8 3.9 %totals.2 = (bf16[2,128,512]{2,1,0:T(8,128)(2,1)}, bf16[2,128,512]{2,1,0:T(8,128)(2,1)}, bf16[2,128,512]{2,1,0:T(8,128)(2,1)}, bf16[2,128,512]{2,1,0:T(8,128)(2,1)}) custom-call(s32[1]{0:T(128)} %bitcast.which_ref, bf16[2,512,512]{2,1,0:T(8,128)(2,1)} %own_chunk.3.after_ref.also_ref, bf16[2,512,512]{2,1,0:T(8,128)(2,1)} %own_chunk.3.after_ref.also_ref, ...), custom_call_target="tpu_custom_call" | custom-call | flops 1024 | bytes 1024 | tf_op jit(solution)/shard_map/totals/pallas_call | solution.py:459
  155.4 2.1 %collective-permute-start.19 = (bf16[384,768]{1,0:T(8,128)(2,1)}, bf16[384,768]{1,0:T(8,128)(2,1)S(1)}, u32[]{:S(2)}, u32[]{:S(2)}) collective-permute-start(bf16[384,768]{1,0:T(8,128)(2,1)} %join.1.also_ref), channel_id=1, source_target_pairs={{0,4},{2,6},{4,0},{6,2},{1,5},{3,7},{5,1},{7,3},{8,12},{10,14},{12... | collective-permute-start | bytes 1769480 | tf_op jit(solution)/shard_map/ppermute | solution.py:621
  158.0 3.9 %by_token.1.after_ref = bf16[512,16,128]{2,1,0:T(8,128)(2,1)} custom-call(bf16[2,128,512]{2,1,0:T(8,128)(2,1)} %get-tuple-element.51.after_ref.refs_0_, bf16[512,1024]{1,0:T(8,128)(2,1)} %get-tuple-element.40.refs_2_.refs_4_.a_ref, bf16[512,1024]{1,0:T(8,128)(2,1)} %back_second.1.gate_ref.refs_2_.refs_4_.b_ref), custom_call_target="tpu_custom_call" | custom-call | flops 1024 | bytes 1024 | tf_op jit(solution)/shard_map/by_token/pallas_call | solution.py:522
  161.9 3.7 %collective-permute-start.21 = (bf16[2,128,512]{2,1,0:T(8,128)(2,1)}, bf16[2,128,512]{2,1,0:T(8,128)(2,1)S(1)}, u32[]{:S(2)}, u32[]{:S(2)}) collective-permute-start(bf16[2,128,512]{2,1,0:T(8,128)(2,1)} %get-tuple-element.54), channel_id=1, source_target_pairs={{0,16},{8,24},{16,0},{24,8},{32,48},{40,56},{48,32},{56,40},{64,80... | collective-permute-start | bytes 786440 | tf_op jit(solution)/shard_map/ppermute | solution.py:585
  166.9 4.0 %totals.3 = (bf16[2,128,512]{2,1,0:T(8,128)(2,1)}, bf16[2,128,512]{2,1,0:T(8,128)(2,1)}, bf16[2,128,512]{2,1,0:T(8,128)(2,1)}, bf16[2,128,512]{2,1,0:T(8,128)(2,1)}) custom-call(s32[1]{0:T(128)} %bitcast.1.which_ref, bf16[512,16,128]{2,1,0:T(8,128)(2,1)} %by_token.1.after_ref, bf16[384,768]{1,0:T(8,128)(2,1)} %join.1.also_ref, ...), custom_call_target="tpu_custom_call" | custom-call | flops 1024 | bytes 1024 | tf_op jit(solution)/shard_map/totals/pallas_call | solution.py:459
  170.9 4.4 %collective-permute-start.26 = (bf16[2,128,512]{2,1,0:T(8,128)(2,1)}, bf16[2,128,512]{2,1,0:T(8,128)(2,1)S(1)}, u32[]{:S(2)}, u32[]{:S(2)}) collective-permute-start(bf16[2,128,512]{2,1,0:T(8,128)(2,1)} %get-tuple-element.59), channel_id=1, source_target_pairs={{0,64},{8,72},{16,80},{24,88},{32,96},{40,104},{48,112},{56,120},{... | collective-permute-start | bytes 786440 | tf_op jit(solution)/shard_map/ppermute | solution.py:585
  178.0 2.0 %first_half.1.first_ref = bf16[2,128,512]{2,1,0:T(8,128)(2,1)} custom-call(bf16[768,768]{1,0:T(8,128)(2,1)} %pad_maximum_fusion.after_ref, bf16[2,128,512]{2,1,0:T(8,128)(2,1)} %get-tuple-element.51.after_ref.refs_0_, bf16[2,128,512]{2,1,0:T(8,128)(2,1)} %copy-done.20, bf16[2,128,512]{2,1,0:T(8,128)(2,1)} %copy-done.21, bf16[2,128,512]{2,1,0:T(8,128)(2,1)} %copy-done.22), custom_call_target="tpu_custom_call" | custom-call | flops 1024 | bytes 1024 | tf_op jit(solution)/shard_map/first_half/pallas_call | solution.py:484
  180.0 4.2 %collective-permute-done.25.refs_1_ = bf16[2,128,512]{2,1,0:T(8,128)(2,1)S(1)} collective-permute-done((bf16[2,128,512]{2,1,0:T(8,128)(2,1)}, bf16[2,128,512]{2,1,0:T(8,128)(2,1)S(1)}, u32[]{:S(2)}, u32[]{:S(2)}) %collective-permute-start.25) | collective-permute-done | bytes 262176 | tf_op jit(solution)/shard_map/ppermute | solution.py:585
  185.6 2.3 %finish.1 = bf16[128,16,128]{2,1,0:T(8,128)(2,1)} custom-call(bf16[2,128,512]{2,1,0:T(8,128)(2,1)} %first_half.1.first_ref, bf16[2,128,512]{2,1,0:T(8,128)(2,1)} %get-tuple-element.57.refs_0_, bf16[2,128,512]{2,1,0:T(8,128)(2,1)} %copy-done.23, bf16[2,128,512]{2,1,0:T(8,128)(2,1)} %copy-done.24, bf16[2,128,512]{2,1,0:T(8,128)(2,1)} %copy-done.25), custom_call_target="tpu_custom_call" | custom-call | flops 1024 | bytes 1024 | tf_op jit(solution)/shard_map/finish/pallas_call | solution.py:505
  (151 shorter events, 45.9 us)
Async XLA Ops:
  0.6 28.5 %copy-start = (bf16[768,768]{1,0:T(8,128)(2,1)S(1)}, bf16[768,768]{1,0:T(8,128)(2,1)}, u32[]{:S(2)}) copy-start(bf16[768,768]{1,0:T(8,128)(2,1)} %param.22) | copy-start | bytes 3538948
  6.9 24.8 %all-to-all-start = ((bf16[16,256,128]{2,1,0:T(8,128)(2,1)}), bf16[16,256,128]{2,1,0:T(8,128)(2,1)S(1)}, u32[]{:S(2)}, u32[]{:S(2)}) async-start(bf16[16,256,128]{2,1,0:T(8,128)(2,1)} %bitcast.58), calls=%async_computation | async-start | bytes 2097152 | tf_op jit(solution)/shard_map/all_to_all | solution.py:650
  14.4 14.8 %copy-start.26 = (bf16[2,1,256,768]{3,2,1,0:T(8,128)(2,1)S(1)}, bf16[2,1,256,768]{3,2,1,0:T(8,128)(2,1)}, u32[]{:S(2)}) copy-start(bf16[2,1,256,768]{3,2,1,0:T(8,128)(2,1)} %param.21) | copy-start | bytes 2359300
  42.7 21.2 %collective-permute-start = (bf16[16,128,512]{2,1,0:T(8,128)(2,1)}, bf16[16,128,512]{2,1,0:T(8,128)(2,1)S(1)}, u32[]{:S(2)}, u32[]{:S(2)}) collective-permute-start(bf16[16,128,512]{2,1,0:T(8,128)(2,1)} %get-tuple-element.34), channel_id=1, source_target_pairs={{0,1},{1,0},{2,3},{3,2},{4,5},{5,4},{6,7},{7,6},{8,9},{9,8},{10,11... | collective-permute-start | bytes 6291464 | tf_op jit(solution)/shard_map/ppermute | solution.py:700
  43.8 20.0 %all-to-all-start.1 = ((f32[16,72,128]{2,1,0:T(8,128)}), f32[16,72,128]{2,1,0:T(8,128)S(1)}, u32[]{:S(2)}, u32[]{:S(2)}) async-start(f32[16,72,128]{2,1,0:T(8,128)} %get-tuple-element.33.after_ref), calls=%async_computation.1 | async-start | bytes 1179648 | tf_op jit(solution)/shard_map/all_to_all | solution.py:713
  70.5 20.5 %collective-permute-start.5 = (bf16[512,1024]{1,0:T(8,128)(2,1)}, bf16[512,1024]{1,0:T(8,128)(2,1)S(1)}, u32[]{:S(2)}, u32[]{:S(2)}) collective-permute-start(bf16[512,1024]{1,0:T(8,128)(2,1)} %get-tuple-element.40.refs_2_.refs_4_.a_ref), channel_id=1, source_target_pairs={{0,1},{1,0},{2,3},{3,2},{4,5},{5,4},{6,7},{7,6},{8,9},{9,8},{10,11... | collective-permute-start | bytes 3145736 | tf_op jit(solution)/shard_map/ppermute | solution.py:717
  75.4 25.4 %collective-permute-start.7 = (bf16[512,1024]{1,0:T(8,128)(2,1)}, bf16[512,1024]{1,0:T(8,128)(2,1)S(1)}, u32[]{:S(2)}, u32[]{:S(2)}) collective-permute-start(bf16[512,1024]{1,0:T(8,128)(2,1)} %back_second.1.gate_ref.refs_2_.refs_4_.b_ref), channel_id=1, source_target_pairs={{0,1},{1,0},{2,3},{3,2},{4,5},{5,4},{6,7},{7,6},{8,9},{9,8},{10,11... | collective-permute-start | bytes 3145736 | tf_op jit(solution)/shard_map/ppermute | solution.py:719
  76.0 6.5 %collective-permute-start.1 = (f32[8,128]{1,0:T(8,128)S(1)}, f32[8,128]{1,0:T(8,128)S(1)}, u32[]{:S(2)}, u32[]{:S(2)}) collective-permute-start(f32[8,128]{1,0:T(8,128)S(1)} %copy-done.32), channel_id=1, source_target_pairs={{0,2},{2,4},{4,6},{6,0},{1,3},{3,5},{5,7},{7,1},{8,10},{10,12},{12... | collective-permute-start | bytes 12296 | tf_op jit(solution)/shard_map/ppermute | solution.py:733
  77.9 5.2 %collective-permute-start.2 = (f32[8,128]{1,0:T(8,128)S(1)}, f32[8,128]{1,0:T(8,128)S(1)}, u32[]{:S(2)}, u32[]{:S(2)}) collective-permute-start(f32[8,128]{1,0:T(8,128)S(1)} %copy-done.32), channel_id=1, source_target_pairs={{0,4},{2,6},{4,0},{6,2},{1,5},{3,7},{5,1},{7,3},{8,12},{10,14},{12... | collective-permute-start | bytes 12296 | tf_op jit(solution)/shard_map/ppermute | solution.py:733
  81.5 3.6 %collective-permute-start.3 = (f32[8,128]{1,0:T(8,128)S(1)}, f32[8,128]{1,0:T(8,128)S(1)}, u32[]{:S(2)}, u32[]{:S(2)}) collective-permute-start(f32[8,128]{1,0:T(8,128)S(1)} %copy-done.32), channel_id=1, source_target_pairs={{0,6},{2,0},{4,2},{6,4},{1,7},{3,1},{5,3},{7,5},{8,14},{10,8},{12,... | collective-permute-start | bytes 12296 | tf_op jit(solution)/shard_map/ppermute | solution.py:733
  87.8 1.6 collective-permute-start.4
  90.4 6.0 %collective-permute-start.6 = (bf16[96,768]{1,0:T(8,128)(2,1)S(1)}, bf16[96,768]{1,0:T(8,128)(2,1)S(1)}, u32[]{:S(2)}, u32[]{:S(2)}) collective-permute-start(bf16[96,768]{1,0:T(8,128)(2,1)S(1)} %add_convert_fusion.4.after_ref.also_ref), channel_id=1, source_target_pairs={{0,8},{8,0},{16,24},{24,16},{32,40},{40,32},{48,56},{56,48},{64,72... | collective-permute-start | bytes 442376 | tf_op jit(solution)/shard_map/ppermute | solution.py:729
  97.4 11.7 %collective-permute-start.8 = (bf16[96,768]{1,0:T(8,128)(2,1)S(1)}, bf16[96,768]{1,0:T(8,128)(2,1)S(1)}, u32[]{:S(2)}, u32[]{:S(2)}) collective-permute-start(bf16[96,768]{1,0:T(8,128)(2,1)S(1)} %add_convert_fusion.3.after_ref.also_ref), channel_id=1, source_target_pairs={{0,32},{8,40},{16,48},{24,56},{32,0},{40,8},{48,16},{56,24},{64,96... | collective-permute-start | bytes 442376 | tf_op jit(solution)/shard_map/ppermute | solution.py:729
  97.4 15.6 %collective-permute-start.9 = (bf16[512,512]{1,0:T(8,128)(2,1)}, bf16[512,512]{1,0:T(8,128)(2,1)S(1)}, u32[]{:S(2)}, u32[]{:S(2)}) collective-permute-start(bf16[512,512]{1,0:T(8,128)(2,1)} %get-tuple-element.41), channel_id=1, source_target_pairs={{0,32},{8,40},{16,48},{24,56},{32,64},{40,72},{48,80},{56,88},{64,... | collective-permute-start | bytes 1572872 | tf_op jit(solution)/shard_map/ppermute | solution.py:585
  99.5 16.0 %collective-permute-start.10 = (bf16[512,512]{1,0:T(8,128)(2,1)}, bf16[512,512]{1,0:T(8,128)(2,1)S(1)}, u32[]{:S(2)}, u32[]{:S(2)}) collective-permute-start(bf16[512,512]{1,0:T(8,128)(2,1)} %get-tuple-element.45), channel_id=1, source_target_pairs={{0,96},{8,104},{16,112},{24,120},{32,0},{40,8},{48,16},{56,24},{64... | collective-permute-start | bytes 1572872 | tf_op jit(solution)/shard_map/ppermute | solution.py:585
  105.8 22.1 %collective-permute-start.12 = (bf16[512,512]{1,0:T(8,128)(2,1)}, bf16[512,512]{1,0:T(8,128)(2,1)S(1)}, u32[]{:S(2)}, u32[]{:S(2)}) collective-permute-start(bf16[512,512]{1,0:T(8,128)(2,1)} %get-tuple-element.43), channel_id=1, source_target_pairs={{0,8},{8,16},{16,24},{24,0},{32,40},{40,48},{48,56},{56,32},{64,72... | collective-permute-start | bytes 1572872 | tf_op jit(solution)/shard_map/ppermute | solution.py:585
  107.0 20.9 %collective-permute-start.13 = (bf16[512,512]{1,0:T(8,128)(2,1)}, bf16[512,512]{1,0:T(8,128)(2,1)S(1)}, u32[]{:S(2)}, u32[]{:S(2)}) collective-permute-start(bf16[512,512]{1,0:T(8,128)(2,1)} %get-tuple-element.48), channel_id=1, source_target_pairs={{0,24},{8,0},{16,8},{24,16},{32,56},{40,32},{48,40},{56,48},{64,88... | collective-permute-start | bytes 1572872 | tf_op jit(solution)/shard_map/ppermute | solution.py:585
  110.0 12.5 %collective-permute-start.11 = (bf16[96,768]{1,0:T(8,128)(2,1)S(1)}, bf16[96,768]{1,0:T(8,128)(2,1)S(1)}, u32[]{:S(2)}, u32[]{:S(2)}) collective-permute-start(bf16[96,768]{1,0:T(8,128)(2,1)S(1)} %add_convert_fusion.2.after_ref.also_ref), channel_id=1, source_target_pairs={{0,64},{8,72},{16,80},{24,88},{32,96},{40,104},{48,112},{56,120},{... | collective-permute-start | bytes 442376 | tf_op jit(solution)/shard_map/ppermute | solution.py:729
  123.4 11.7 %collective-permute-start.16 = (bf16[96,768]{1,0:T(8,128)(2,1)S(1)}, bf16[96,768]{1,0:T(8,128)(2,1)S(1)}, u32[]{:S(2)}, u32[]{:S(2)}) collective-permute-start(bf16[96,768]{1,0:T(8,128)(2,1)S(1)} %add_convert_fusion.1.after_ref.also_ref), channel_id=1, source_target_pairs={{0,16},{8,24},{16,0},{24,8},{32,48},{40,56},{48,32},{56,40},{64,80... | collective-permute-start | bytes 442376 | tf_op jit(solution)/shard_map/ppermute | solution.py:729
  124.7 24.2 %collective-permute-start.14 = (bf16[2,512,512]{2,1,0:T(8,128)(2,1)}, bf16[2,512,512]{2,1,0:T(8,128)(2,1)}, u32[]{:S(2)}, u32[]{:S(2)}) collective-permute-start(bf16[2,512,512]{2,1,0:T(8,128)(2,1)} %get-tuple-element.46), channel_id=1, source_target_pairs={{0,32},{8,40},{16,48},{24,56},{32,64},{40,72},{48,80},{56,88},{64,... | collective-permute-start | bytes 3145736 | tf_op jit(solution)/shard_map/ppermute | solution.py:585
  125.1 23.7 %collective-permute-start.15 = (bf16[2,512,512]{2,1,0:T(8,128)(2,1)}, bf16[2,512,512]{2,1,0:T(8,128)(2,1)}, u32[]{:S(2)}, u32[]{:S(2)}) collective-permute-start(bf16[2,512,512]{2,1,0:T(8,128)(2,1)} %get-tuple-element.50), channel_id=1, source_target_pairs={{0,96},{8,104},{16,112},{24,120},{32,0},{40,8},{48,16},{56,24},{64... | collective-permute-start | bytes 3145736 | tf_op jit(solution)/shard_map/ppermute | solution.py:585
  136.0 3.4 %collective-permute-start.17 = (bf16[96,768]{1,0:T(8,128)(2,1)S(1)}, bf16[96,768]{1,0:T(8,128)(2,1)S(1)}, u32[]{:S(2)}, u32[]{:S(2)}) collective-permute-start(bf16[96,768]{1,0:T(8,128)(2,1)S(1)} %add_convert_fusion), channel_id=1, source_target_pairs={{0,1},{1,0},{2,3},{3,2},{4,5},{5,4},{6,7},{7,6},{8,9},{9,8},{10,11... | collective-permute-start | bytes 442376 | tf_op jit(solution)/shard_map/ppermute | solution.py:621
  136.1 29.5 %collective-permute-start.23 = (bf16[2,512,512]{2,1,0:T(8,128)(2,1)}, bf16[2,512,512]{2,1,0:T(8,128)(2,1)S(1)}, u32[]{:S(2)}, u32[]{:S(2)}) collective-permute-start(bf16[2,512,512]{2,1,0:T(8,128)(2,1)} %get-tuple-element.49.after_ref.also_ref), channel_id=1, source_target_pairs={{0,8},{8,16},{16,24},{24,0},{32,40},{40,48},{48,56},{56,32},{64,72... | collective-permute-start | bytes 3145736 | tf_op jit(solution)/shard_map/ppermute | solution.py:585
  136.7 29.2 %collective-permute-start.24 = (bf16[2,512,512]{2,1,0:T(8,128)(2,1)}, bf16[2,512,512]{2,1,0:T(8,128)(2,1)S(1)}, u32[]{:S(2)}, u32[]{:S(2)}) collective-permute-start(bf16[2,512,512]{2,1,0:T(8,128)(2,1)} %get-tuple-element.56), channel_id=1, source_target_pairs={{0,24},{8,0},{16,8},{24,16},{32,56},{40,32},{48,40},{56,48},{64,88... | collective-permute-start | bytes 3145736 | tf_op jit(solution)/shard_map/ppermute | solution.py:585
  139.5 13.2 %collective-permute-start.18 = (bf16[192,768]{1,0:T(8,128)(2,1)S(1)}, bf16[192,768]{1,0:T(8,128)(2,1)S(1)}, u32[]{:S(2)}, u32[]{:S(2)}) collective-permute-start(bf16[192,768]{1,0:T(8,128)(2,1)S(1)} %pad_maximum_fusion.1.own_ref), channel_id=1, source_target_pairs={{0,2},{2,0},{4,6},{6,4},{1,3},{3,1},{5,7},{7,5},{8,10},{10,8},{12,... | collective-permute-start | bytes 884744 | tf_op jit(solution)/shard_map/ppermute | solution.py:755
  155.4 19.9 %collective-permute-start.19 = (bf16[384,768]{1,0:T(8,128)(2,1)}, bf16[384,768]{1,0:T(8,128)(2,1)S(1)}, u32[]{:S(2)}, u32[]{:S(2)}) collective-permute-start(bf16[384,768]{1,0:T(8,128)(2,1)} %join.1.also_ref), channel_id=1, source_target_pairs={{0,4},{2,6},{4,0},{6,2},{1,5},{3,7},{5,1},{7,3},{8,12},{10,14},{12... | collective-permute-start | bytes 1769480 | tf_op jit(solution)/shard_map/ppermute | solution.py:621
  157.5 13.4 %collective-permute-start.20 = (bf16[2,128,512]{2,1,0:T(8,128)(2,1)}, bf16[2,128,512]{2,1,0:T(8,128)(2,1)S(1)}, u32[]{:S(2)}, u32[]{:S(2)}) collective-permute-start(bf16[2,128,512]{2,1,0:T(8,128)(2,1)} %get-tuple-element.53), channel_id=1, source_target_pairs={{0,8},{8,16},{16,24},{24,0},{32,40},{40,48},{48,56},{56,32},{64,72... | collective-permute-start | bytes 786440 | tf_op jit(solution)/shard_map/ppermute | solution.py:585
  161.9 14.6 %collective-permute-start.21 = (bf16[2,128,512]{2,1,0:T(8,128)(2,1)}, bf16[2,128,512]{2,1,0:T(8,128)(2,1)S(1)}, u32[]{:S(2)}, u32[]{:S(2)}) collective-permute-start(bf16[2,128,512]{2,1,0:T(8,128)(2,1)} %get-tuple-element.54), channel_id=1, source_target_pairs={{0,16},{8,24},{16,0},{24,8},{32,48},{40,56},{48,32},{56,40},{64,80... | collective-permute-start | bytes 786440 | tf_op jit(solution)/shard_map/ppermute | solution.py:585
  165.6 11.0 %collective-permute-start.22 = (bf16[2,128,512]{2,1,0:T(8,128)(2,1)}, bf16[2,128,512]{2,1,0:T(8,128)(2,1)S(1)}, u32[]{:S(2)}, u32[]{:S(2)}) collective-permute-start(bf16[2,128,512]{2,1,0:T(8,128)(2,1)} %get-tuple-element.55), channel_id=1, source_target_pairs={{0,24},{8,0},{16,8},{24,16},{32,56},{40,32},{48,40},{56,48},{64,88... | collective-permute-start | bytes 786440 | tf_op jit(solution)/shard_map/ppermute | solution.py:585
  170.9 13.3 %collective-permute-start.25 = (bf16[2,128,512]{2,1,0:T(8,128)(2,1)}, bf16[2,128,512]{2,1,0:T(8,128)(2,1)S(1)}, u32[]{:S(2)}, u32[]{:S(2)}) collective-permute-start(bf16[2,128,512]{2,1,0:T(8,128)(2,1)} %get-tuple-element.58), channel_id=1, source_target_pairs={{0,32},{8,40},{16,48},{24,56},{32,64},{40,72},{48,80},{56,88},{64,... | collective-permute-start | bytes 786440 | tf_op jit(solution)/shard_map/ppermute | solution.py:585
  170.9 13.3 %collective-permute-start.26 = (bf16[2,128,512]{2,1,0:T(8,128)(2,1)}, bf16[2,128,512]{2,1,0:T(8,128)(2,1)S(1)}, u32[]{:S(2)}, u32[]{:S(2)}) collective-permute-start(bf16[2,128,512]{2,1,0:T(8,128)(2,1)} %get-tuple-element.59), channel_id=1, source_target_pairs={{0,64},{8,72},{16,80},{24,88},{32,96},{40,104},{48,112},{56,120},{... | collective-permute-start | bytes 786440 | tf_op jit(solution)/shard_map/ppermute | solution.py:585
  175.3 9.5 %collective-permute-start.27 = (bf16[2,128,512]{2,1,0:T(8,128)(2,1)}, bf16[2,128,512]{2,1,0:T(8,128)(2,1)S(1)}, u32[]{:S(2)}, u32[]{:S(2)}) collective-permute-start(bf16[2,128,512]{2,1,0:T(8,128)(2,1)} %get-tuple-element.60), channel_id=1, source_target_pairs={{0,96},{8,104},{16,112},{24,120},{32,0},{40,8},{48,16},{56,24},{64... | collective-permute-start | bytes 786440 | tf_op jit(solution)/shard_map/ppermute | solution.py:585
  (37 other events, 157.6 us)
